TPU v7x, 32 devices: a whole 2x2x4 slice. The times are simulated.
32 devices in a mesh: dp: 4 (over y, x), grp: 4 (over z), loc: 2 (over core).
Axes of the slice: x: 2, y: 2, z: 4, core: 2. Of those that a mesh axis runs over, the one named last changes fastest.
Arguments:
- tokens: bfloat16 [1024, 2048], P(('grp', 'loc'), 'dp'), may hold values from -6 to 6
- grad_out: bfloat16 [1024, 2048], P(('grp', 'loc'), 'dp'), may hold values from -6 to 6
- expert_ids: int32 [1024, 4], P(('grp', 'loc')), may hold values from 0 to 7, all different within a row; in each aligned block of 128 rows (0 to 127, 128 to 255, ...) at most 128 rows name the same one
- gate_scale: float32 [1024, 4], P(('grp', 'loc')), may hold values from 0.1 to 1
- gate_weight: bfloat16 [8, 768, 2048], P(('grp', 'loc'), 'dp'), may hold values from -0.125 to 0.125
- up_weight: bfloat16 [8, 768, 2048], P(('grp', 'loc'), 'dp'), may hold values from -0.125 to 0.125
- down_weight: bfloat16 [8, 768, 2048], P(('grp', 'loc'), None, 'dp'), may hold values from -0.21875 to 0.21875
Outputs:
- layer_out: bfloat16 [1024, 2048], P(('grp', 'loc'), 'dp')
- gate_gradient: bfloat16 [8, 768, 2048], P(('grp', 'loc'), 'dp')
- up_gradient: bfloat16 [8, 768, 2048], P(('grp', 'loc'), 'dp')
- down_gradient: bfloat16 [8, 768, 2048], P(('grp', 'loc'), None, 'dp')
Inputs may be any that keep to these rules, and one draw needn't show every extreme that they name: `expert_ids`: each token names 4 different experts. Within one index of grp and loc (aligned blocks of 128 token rows) no expert is named by more than 128 rows, a bound that some block reaches.
All inputs are finite; a program needn't handle non-finite values.
Results may differ from a plain program's by a relative error of at most 0.0058.
Values may be sent and summed in bfloat16 or wider, within the bound.
No kernel may reach another device: no remote copies, remote signals or barrier semaphores. Data moves between devices by JAX's collectives and lax.ppermute only.
A program may use at most 64 MiB of HBM per device.

v0:
```python
import jax
import jax.numpy as jnp
from jax import lax
from jax.sharding import PartitionSpec as P


def slot_layout(route_ids, experts, capacity):
    flat_ids = route_ids.reshape(-1)
    onehot = (
        flat_ids[:, None] == lax.broadcasted_iota(jnp.int32, (flat_ids.shape[0], experts), 1)
    ).astype(jnp.int32)
    ranks = jnp.sum((jnp.cumsum(onehot, axis=0) - 1) * onehot, axis=1)
    return flat_ids * capacity + ranks


def place_matrix(positions, tok_rows, per_token, slots_total):
    slot_index = lax.broadcasted_iota(jnp.int32, (slots_total, tok_rows, per_token), 0)
    hits = slot_index == positions.reshape(1, tok_rows, per_token)
    return jnp.sum(hits.astype(jnp.float32), axis=2).astype(jnp.bfloat16)


def send_rows(outgoing):
    return lax.all_to_all(outgoing, ("grp", "loc"), split_axis=0, concat_axis=0, tiled=True)


def return_rows(results):
    return lax.all_to_all(results, ("grp", "loc"), split_axis=0, concat_axis=0, tiled=True)


def body(tokens, grad_out, expert_ids, gate_scale, gate_weight, up_weight, down_weight):
    tok_rows, quarter = tokens.shape
    per_token = expert_ids.shape[1]
    experts = lax.axis_size(("grp", "loc"))
    capacity = min(tok_rows, max(2, 2 * tok_rows * per_token // experts))
    slots_total = experts * capacity
    positions = slot_layout(expert_ids, experts, capacity)
    unit_place = place_matrix(positions, tok_rows, per_token, slots_total)
    slot_scale = jnp.zeros((slots_total,), jnp.float32).at[positions].set(gate_scale.reshape(-1))
    picked_grads = jnp.dot(unit_place, grad_out, preferred_element_type=jnp.float32)
    grad_rows = (picked_grads * slot_scale[:, None]).astype(jnp.bfloat16)
    full_tokens = lax.all_gather(tokens, "dp", axis=1, tiled=True)
    features = full_tokens.shape[1]
    token_rows = jnp.dot(unit_place, full_tokens, preferred_element_type=jnp.float32).astype(
        jnp.bfloat16
    )
    outgoing = jnp.concatenate([token_rows, grad_rows], axis=1).reshape(
        experts, capacity, features + quarter
    )
    arrived = send_rows(outgoing)
    slot_tokens = arrived[:, :, :features]
    slot_grads = arrived[:, :, features:]
    flat_tokens = slot_tokens.reshape(slots_total, -1)
    flat_grads = slot_grads.reshape(slots_total, quarter)
    gate_mat = gate_weight[0]
    up_mat = up_weight[0]
    down_mat = down_weight[0]
    feature_contract = (((1,), (1,)), ((), ()))
    gate_pre = lax.dot_general(
        gate_mat, flat_tokens, feature_contract, preferred_element_type=jnp.float32
    )
    up_pre = lax.dot_general(
        up_mat, flat_tokens, feature_contract, preferred_element_type=jnp.float32
    )
    sigmoid_gate = jax.nn.sigmoid(gate_pre)
    activated = gate_pre * sigmoid_gate
    hidden = (activated * up_pre).astype(jnp.bfloat16)
    piece = lax.all_gather(hidden, "dp", axis=0, tiled=True)
    down_rows = down_mat
    out_total = lax.dot_general(
        piece, down_rows, (((0,), (0,)), ((), ())), preferred_element_type=jnp.float32
    )
    block_grad = jnp.dot(piece, flat_grads, preferred_element_type=jnp.float32)
    down_total = block_grad
    out_total, down_total = (out_total, down_total)
    expert_out = out_total.astype(jnp.bfloat16)
    down_gradient = down_total.astype(jnp.bfloat16)
    returned = return_rows(expert_out.reshape(experts, capacity, quarter)).reshape(
        slots_total, quarter
    )
    picked = returned[positions].astype(jnp.float32) * gate_scale.reshape(-1)[:, None]
    layer_out = jnp.sum(picked.reshape(tok_rows, per_token, quarter), axis=1).astype(jnp.bfloat16)
    down_rows = down_mat
    hidden_grad = lax.psum_scatter(
        lax.dot_general(
            down_rows, flat_grads, feature_contract, preferred_element_type=jnp.float32
        ),
        "dp",
        scatter_dimension=0,
        tiled=True,
    )
    gate_grad = (
        hidden_grad * up_pre * sigmoid_gate * (1.0 + gate_pre * (1.0 - sigmoid_gate))
    ).astype(jnp.bfloat16)
    up_grad = (hidden_grad * activated).astype(jnp.bfloat16)
    gate_gradient = jnp.dot(gate_grad, flat_tokens, preferred_element_type=jnp.float32).astype(
        jnp.bfloat16
    )
    up_gradient = jnp.dot(up_grad, flat_tokens, preferred_element_type=jnp.float32).astype(
        jnp.bfloat16
    )
    return (layer_out, gate_gradient[None], up_gradient[None], down_gradient[None])


def solution(mesh):
    return jax.shard_map(
        body,
        mesh=mesh,
        in_specs=(
            P(("grp", "loc"), "dp"),
            P(("grp", "loc"), "dp"),
            P(("grp", "loc"), None),
            P(("grp", "loc"), None),
            P(("grp", "loc"), "dp", None),
            P(("grp", "loc"), "dp", None),
            P(("grp", "loc"), None, "dp"),
        ),
        out_specs=(
            P(("grp", "loc"), "dp"),
            P(("grp", "loc"), "dp", None),
            P(("grp", "loc"), "dp", None),
            P(("grp", "loc"), None, "dp"),
        ),
        check_vma=False,
    )
```

profile of v0, /device:TPU:0, one launch (start us, length us, event | category | flops | bytes accessed | tf_op | source)
XLA Modules:
  0.0 249.2 jit_solution(11712515003381444284)
XLA Ops:
  7.2 0.0 copy-start
  7.2 0.0 all-gather.2.cloned.1.call-start
  7.2 0.9 copy.22
  8.1 0.1 eq.29
  8.2 0.1 eq.26
  8.3 1.1 reduce-window.6
  9.5 0.2 slice_reduce_fusion
  9.7 0.8 copy.26
  10.5 0.1 reshape.110
  10.6 0.1 fusion.12
  10.7 0.1 reduce_sum.32
  10.8 0.1 copy.25
  10.9 0.1 mul.62
  11.0 0.2 convert_reduce_fusion
  11.3 11.8 %all_gather.6 = bf16[128,2048]{1,0:T(8,128)(2,1)S(1)} all-gather(bf16[128,512]{1,0:T(8,128)(2,1)} %param.7), channel_id=1, replica_groups=mesh['dp'=4,'grp'=4,'loc'=2] {'dp'}, dimensions={1}, use_global_device_ids=true | all-gather | bytes 655360 | tf_op jit(solution)/shard_map/all_gather | solution.py:41
  23.1 3.2 %convolution_convert_fusion = bf16[1024,2048]{1,0:T(8,128)(2,1)} fusion(bf16[128,2048]{1,0:T(8,128)(2,1)S(1)} %all_gather.6, bf16[1024,128]{1,0:T(8,128)(2,1)S(1)} %convert_reduce_fusion), kind=kOutput, calls=%fused_computation.3 | convolution fusion | flops 538968064 | bytes 4980736 | tf_op jit(solution)/shard_map/dot_general | solution.py:43
  26.3 2.4 scatter_custom_fusion
  28.7 0.0 copy-done.4
  28.8 0.4 multiply_convert_fusion
  29.2 2.6 %pad_maximum_fusion = bf16[1024,2560]{1,0:T(8,128)(2,1)S(1)} fusion(bf16[1024,512]{1,0:T(8,128)(2,1)S(1)} %multiply_convert_fusion, bf16[1024,2048]{1,0:T(8,128)(2,1)} %convolution_convert_fusion), kind=kLoop, calls=%fused_computation.2 | loop fusion | flops 10485760 | bytes 10485760 | tf_op jit(solution)/shard_map/concatenate | solution.py:46
  31.8 121.3 %all_to_all.10 = bf16[8,128,2560]{2,1,0:T(8,128)(2,1)S(1)} all-to-all(bf16[8,128,2560]{2,1,0:T(8,128)(2,1)S(1)} %bitcast.52), channel_id=1, replica_groups=mesh['dp'=4,'grp'=4,'loc'=2] {'grp','loc'}, dimensions={0} | all-to-all | bytes 10485760 | tf_op jit(solution)/shard_map/all_to_all | solution.py:23
  153.1 0.6 slice.19
  153.7 0.0 copy-start.2
  153.7 0.0 copy-start.6
  153.7 1.7 copy-done.1
  155.4 0.0 copy-done.5
  155.4 1.5 convolution_bitcast_fusion.2
  156.9 2.6 %multiply_convert_fusion.3 = (bf16[192,1024]{1,0:T(8,128)(2,1)}, f32[192,1024]{1,0:T(8,128)}) fusion(f32[192,1024]{1,0:T(8,128)S(1)} %convolution_bitcast_fusion.2, bf16[1024,2048]{1,0:T(8,128)(2,1)S(1)} %bitcast.56, bf16[1,192,2048]{2,1,0:T(8,128)(2,1)S(1)} %copy-done.6), kind=kOutput, calls=%fused_computation.24 | convolution fusion | flops 806486016 | bytes 6946816 | tf_op jit(solution)/shard_map/dot_general | solution.py:61
  159.6 0.0 copy-done.8
  159.6 0.0 all-gather.2.cloned.1.call-update
  159.6 0.0 reduce-scatter.2.cloned.1.call-start
  159.7 1.3 slice.20
  161.0 0.0 copy-done
  161.0 2.7 %convolution_bitcast_fusion = f32[768,1024]{1,0:T(8,128)} fusion(bf16[1024,512]{1,0:T(8,128)(2,1)S(1)} %bitcast.53, bf16[1,768,512]{2,1,0:T(8,128)(2,1)S(1)} %copy-done), kind=kOutput, calls=%fused_computation.11 | convolution fusion | flops 805306368 | bytes 4980736 | tf_op jit(solution)/shard_map/dot_general | solution.py:84
  163.7 0.0 reduce-scatter.2.cloned.1.call-update
  163.7 24.9 %all-gather.2.cloned.1.call-done = bf16[768,1024]{1,0:T(8,128)(2,1)} async-done(((bf16[192,1024]{1,0:T(8,128)(2,1)}), bf16[768,1024]{1,0:T(8,128)(2,1)}) %all-gather.2.cloned.1.call-update) | async-done | bytes 1572880 | tf_op jit(solution)/shard_map/all_gather | solution.py:67
  188.6 3.4 %convolution_convert_fusion.3 = bf16[1024,512]{1,0:T(8,128)(2,1)} fusion(bf16[768,1024]{1,0:T(8,128)(2,1)} %all-gather.2.cloned.1.call-done, bf16[1,768,512]{2,1,0:T(8,128)(2,1)S(1)} %copy-done), kind=kOutput, calls=%fused_computation.12 | convolution fusion | flops 805830656 | bytes 3407872 | tf_op jit(solution)/shard_map/dot_general | solution.py:69
  192.0 4.6 %all-to-all-start.1 = ((bf16[8,128,512]{2,1,0:T(8,128)(2,1)}), bf16[8,128,512]{2,1,0:T(8,128)(2,1)S(1)}, u32[]{:S(2)}, u32[]{:S(2)}) async-start(bf16[8,128,512]{2,1,0:T(8,128)(2,1)} %bitcast.59), calls=%async_computation.1 | async-start | bytes 2097152 | tf_op jit(solution)/shard_map/all_to_all | solution.py:27
  196.6 3.3 %fusion.2 = bf16[1,768,512]{2,1,0:T(8,128)(2,1)} fusion(bf16[768,1024]{1,0:T(8,128)(2,1)} %all-gather.2.cloned.1.call-done, bf16[1024,512]{1,0:T(8,128)(2,1)S(1)} %bitcast.54), kind=kOutput, calls=%fused_computation.14 | convolution fusion | flops 805699584 | bytes 3407872 | tf_op jit(solution)/shard_map/dot_general | solution.py:72
  199.9 23.3 %all-to-all-done.1 = bf16[8,128,512]{2,1,0:T(8,128)(2,1)S(1)} async-done(((bf16[8,128,512]{2,1,0:T(8,128)(2,1)}), bf16[8,128,512]{2,1,0:T(8,128)(2,1)S(1)}, u32[]{:S(2)}, u32[]{:S(2)}) %all-to-all-start.1) | async-done | bytes 1048608 | tf_op jit(solution)/shard_map/all_to_all | solution.py:27
  223.2 2.0 gather_fusion
  225.2 0.3 reshape.97
  225.5 1.4 multiply_reduce_fusion
  226.9 8.7 %reduce-scatter.2.cloned.1.call-done = f32[192,1024]{1,0:T(8,128)} async-done(((f32[768,1024]{1,0:T(8,128)}), f32[192,1024]{1,0:T(8,128)}) %reduce-scatter.2.cloned.1.call-update) | async-done | bytes 786448 | tf_op jit(solution)/shard_map/reduce_scatter | solution.py:83
  235.6 4.7 %fusion.1 = bf16[1,192,2048]{2,1,0:T(8,128)(2,1)} fusion(bf16[1024,2048]{1,0:T(8,128)(2,1)} %bitcast.57, f32[192,1024]{1,0:T(8,128)} %reduce-scatter.2.cloned.1.call-done, f32[192,1024]{1,0:T(8,128)} %copy-done.8), kind=kOutput, calls=%fused_computation.7 | convolution fusion | flops 806879232 | bytes 6553600 | tf_op jit(solution)/shard_map/dot_general | solution.py:98
  240.3 0.0 copy-done.9
  240.3 0.0 copy-done.3
  240.3 2.0 fusion
  (18 shorter events, 0.1 us)
Async XLA Ops:
  7.2 153.8 %copy-start = (bf16[1,768,512]{2,1,0:T(8,128)(2,1)S(1)}, bf16[1,768,512]{2,1,0:T(8,128)(2,1)}, u32[]{:S(2)}) copy-start(bf16[1,768,512]{2,1,0:T(8,128)(2,1)} %param.13) | copy-start | bytes 2359300
  7.2 181.4 %all-gather.2.cloned.1.call-start = ((), (), s32[]{:S(2)}) async-start(), calls=%async_computation.3 | async-start | bytes 1966080 | tf_op jit(solution)/shard_map/all_gather | solution.py:67
  23.1 5.6 %copy-start.4 = (bf16[128,512]{1,0:T(8,128)(2,1)S(1)}, bf16[128,512]{1,0:T(8,128)(2,1)}, u32[]{:S(2)}) copy-start(bf16[128,512]{1,0:T(8,128)(2,1)} %param.8) | copy-start | bytes 393220
  153.1 2.3 copy-start.1
  153.1 2.3 copy-start.5
  153.7 5.9 %copy-start.2 = (bf16[8,128,2048]{2,1,0:T(8,128)(2,1)}, bf16[8,128,2048]{2,1,0:T(8,128)(2,1)S(1)}, u32[]{:S(2)}) copy-start(bf16[8,128,2048]{2,1,0:T(8,128)(2,1)S(1)} %slice.19) | copy-start | bytes 12582916
  153.7 3.2 %copy-start.6 = (bf16[1,192,2048]{2,1,0:T(8,128)(2,1)S(1)}, bf16[1,192,2048]{2,1,0:T(8,128)(2,1)}, u32[]{:S(2)}) copy-start(bf16[1,192,2048]{2,1,0:T(8,128)(2,1)} %param.12) | copy-start | bytes 2359300
  156.9 2.7 %copy-start.8 = (f32[192,1024]{1,0:T(8,128)}, f32[192,1024]{1,0:T(8,128)S(1)}, u32[]{:S(2)}) copy-start(f32[192,1024]{1,0:T(8,128)S(1)} %convolution_bitcast_fusion.2) | copy-start | bytes 2359300
  159.6 75.9 %reduce-scatter.2.cloned.1.call-start = ((), (), s32[]{:S(2)}) async-start(), calls=%async_computation.4 | async-start | bytes 3932160 | tf_op jit(solution)/shard_map/reduce_scatter | solution.py:83
  192.0 31.2 %all-to-all-start.1 = ((bf16[8,128,512]{2,1,0:T(8,128)(2,1)}), bf16[8,128,512]{2,1,0:T(8,128)(2,1)S(1)}, u32[]{:S(2)}, u32[]{:S(2)}) async-start(bf16[8,128,512]{2,1,0:T(8,128)(2,1)} %bitcast.59), calls=%async_computation.1 | async-start | bytes 2097152 | tf_op jit(solution)/shard_map/all_to_all | solution.py:27
  226.9 13.4 %copy-start.9 = (f32[192,1024]{1,0:T(8,128)S(1)}, f32[192,1024]{1,0:T(8,128)}, u32[]{:S(2)}) copy-start(f32[192,1024]{1,0:T(8,128)} %copy-done.8) | copy-start | bytes 2359300
  226.9 13.4 %copy-start.10 = (f32[192,1024]{1,0:T(8,128)S(1)}, f32[192,1024]{1,0:T(8,128)}, u32[]{:S(2)}) copy-start(f32[192,1024]{1,0:T(8,128)} %get-tuple-element.7) | copy-start | bytes 2359300
  235.6 4.7 %copy-start.3 = (bf16[8,128,2048]{2,1,0:T(8,128)(2,1)S(1)}, bf16[8,128,2048]{2,1,0:T(8,128)(2,1)}, u32[]{:S(2)}) copy-start(bf16[8,128,2048]{2,1,0:T(8,128)(2,1)} %copy-done.2) | copy-start | bytes 12582916
  235.6 4.7 %copy-start.7 = (f32[192,1024]{1,0:T(8,128)S(1)}, f32[192,1024]{1,0:T(8,128)}, u32[]{:S(2)}) copy-start(f32[192,1024]{1,0:T(8,128)} %reduce-scatter.2.cloned.1.call-done) | copy-start | bytes 2359300
Sparse Core Ops, SparseCore 0:
  159.7 28.7 all-gather.1
  191.6 43.9 reduce-scatter.1
where the time goes:
time: 250 us; the launch traced here: 249 us
  blocking collectives  133 us (53%)
  waiting for transfers between devices  56.9 us (23%)
  matrix products  23.9 us (10%)
  between operations  14.2 us (6%)
  local copies, waits for them, and re-layouts  10.9 us (4%)
  other arithmetic  5.51 us (2%)
  starting transfers between devices  4.69 us (2%)
    all_to_all x1, blocking collectives, send_rows(): lax.all_to_all(outgoing, ('grp', 'loc'), split_axis=0, concat_axis=0, til...  121 us
    all_gather x1, waiting for transfers between devices, body(): piece = lax.all_gather(hidden, 'dp', axis=0, tiled=True)  24.9 us
    all_to_all x1, waiting for transfers between devices, return_rows(): lax.all_to_all(results, ('grp', 'loc'), split_axis=0, concat_axis=0, tile...  23.3 us
    all_gather x1, blocking collectives, body(): full_tokens = lax.all_gather(tokens, 'dp', axis=1, tiled=True)  11.8 us
    reduce_scatter x1, waiting for transfers between devices, body(): lax.psum_scatter(lax.dot_general(down_rows, flat_grads, feature_contract,...  8.69 us
  transfers between devices with their start and end apart: 3, of which 3 were waited for; matrix products, arithmetic and copies ran while one was open for 6% of the time, Pallas kernels for 0%

commit v1 on v0

--- a/solution.py
+++ b/solution.py
@@ -27,7 +27,7 @@
     return lax.all_to_all(results, ("grp", "loc"), split_axis=0, concat_axis=0, tiled=True)
 
 
-def body(tokens, grad_out, expert_ids, gate_scale, gate_weight, up_weight, down_weight):
+def slot_body(tokens, grad_out, expert_ids, gate_scale, gate_weight, up_weight, down_weight):
     tok_rows, quarter = tokens.shape
     per_token = expert_ids.shape[1]
     experts = lax.axis_size(("grp", "loc"))
@@ -101,6 +101,113 @@
     return (layer_out, gate_gradient[None], up_gradient[None], down_gradient[None])
 
 
+GROUPS = ((0, 1), (2, 3))
+
+
+def swap(value, axis, bit):
+    pairs = [(i, i ^ bit) for i in range(lax.axis_size(axis))]
+    return lax.ppermute(value, axis, pairs)
+
+
+def square_gather(own):
+    near_x, near_y = swap(own, "dp", 1), swap(own, "dp", 2)
+    half = own.shape[0] // 2
+    far = jnp.concatenate([swap(near_x[:half], "dp", 2), swap(near_y[half:], "dp", 1)], axis=0)
+    return [own, near_x, near_y, far]
+
+
+def square_scatter(parts):
+    far = parts[3].astype(jnp.bfloat16)
+    half = far.shape[0] // 2
+    top, bottom = swap(far[:half], "dp", 2), swap(far[half:], "dp", 1)
+    for_x = jnp.concatenate([parts[1][:half] + top.astype(jnp.float32), parts[1][half:]], axis=0)
+    for_y = jnp.concatenate([parts[2][:half], parts[2][half:] + bottom.astype(jnp.float32)], axis=0)
+    from_x = swap(for_x.astype(jnp.bfloat16), "dp", 1)
+    from_y = swap(for_y.astype(jnp.bfloat16), "dp", 2)
+    return parts[0] + from_x.astype(jnp.float32) + from_y.astype(jnp.float32)
+
+
+def regroup(value, axis, place):
+    size = value.shape[axis] // 4
+    return jnp.concatenate(
+        [lax.dynamic_slice_in_dim(value, (place ^ j) * size, size, axis) for j in range(4)], axis=axis
+    )
+
+
+def dense_body(tokens, grad_out, expert_ids, gate_scale, gate_weight, up_weight, down_weight):
+    rows, quarter = tokens.shape
+    experts = lax.axis_size(("grp", "loc"))
+    place = lax.axis_index("dp")
+    expert = lax.axis_index(("grp", "loc"))
+    units = gate_weight.shape[1]
+    contract_last = (((1,), (1,)), ((), ()))
+    contract_first = (((0,), (0,)), ((), ()))
+
+    named = lax.broadcasted_iota(jnp.int32, (experts, rows, 1), 0) == expert_ids[None]
+    scales = jnp.sum(jnp.where(named, gate_scale[None], 0.0), axis=2)
+    span = range(lax.axis_size("grp"))
+    token_blocks = [tokens if j == 0 else swap(tokens, "grp", j) for j in span]
+    grad_blocks = [grad_out if j == 0 else swap(grad_out, "grp", j) for j in span]
+    scale_blocks = jnp.stack([scales if j == 0 else swap(scales, "grp", j) for j in span])
+    scale_other = swap(scale_blocks, "loc", 1)
+    scale_own = lax.dynamic_index_in_dim(scale_blocks, expert, 1, keepdims=False)
+    scale_other = lax.dynamic_index_in_dim(scale_other, expert, 1, keepdims=False)
+
+    in_weights = regroup(jnp.concatenate([gate_weight[0], up_weight[0]], axis=0), 1, place)
+    down_rows = regroup(down_weight[0], 0, place)
+
+    all_tokens, all_hidden, gate_factors, up_factors, grads, pieces = [], [], [], [], [], []
+    for group in GROUPS:
+        own = square_gather(jnp.concatenate([token_blocks[j] for j in group], axis=0))
+        own = jnp.concatenate(own, axis=1)
+        both = jnp.concatenate([own, swap(own, "loc", 1)], axis=0)
+        all_tokens.append(both)
+        pre = lax.dot_general(in_weights, both, contract_last, preferred_element_type=jnp.float32)
+        scale = jnp.concatenate([s[j] for s in (scale_own, scale_other) for j in group])[None]
+        gate_pre, up_pre = pre[:units], pre[units:]
+        sig = jax.nn.sigmoid(gate_pre)
+        activated = gate_pre * sig
+        hidden = (activated * up_pre * scale).astype(jnp.bfloat16)
+        gate_factors.append(up_pre * sig * (1.0 + gate_pre * (1.0 - sig)) * scale)
+        up_factors.append(activated * scale)
+        hidden = jnp.concatenate(square_gather(hidden), axis=0)
+        all_hidden.append(hidden)
+        out = lax.dot_general(hidden, down_rows, contract_first, preferred_element_type=jnp.float32)
+        half = out.shape[0] // 2
+        mine = out[:half] + swap(out[half:].astype(jnp.bfloat16), "loc", 1).astype(jnp.float32)
+        for i, j in enumerate(group):
+            block = mine[i * rows : (i + 1) * rows]
+            pieces.append(block if j == 0 else swap(block.astype(jnp.bfloat16), "grp", j).astype(jnp.float32))
+        grads_own = jnp.concatenate([grad_blocks[j] for j in group], axis=0)
+        grads.append(jnp.concatenate([grads_own, swap(grads_own, "loc", 1)], axis=0))
+    layer_out = sum(pieces).astype(jnp.bfloat16)
+    grads = jnp.concatenate(grads, axis=0)
+    all_tokens = jnp.concatenate(all_tokens, axis=0)
+    all_hidden = jnp.concatenate(all_hidden, axis=1)
+    shares = lax.dot_general(down_rows, grads, contract_last, preferred_element_type=jnp.float32)
+    hidden_grad = square_scatter([shares[j * units : (j + 1) * units] for j in range(4)])
+    down_gradient = jnp.dot(all_hidden, grads, preferred_element_type=jnp.float32).astype(jnp.bfloat16)
+    both_grads = jnp.concatenate(
+        [
+            (hidden_grad * jnp.concatenate(gate_factors, axis=1)).astype(jnp.bfloat16),
+            (hidden_grad * jnp.concatenate(up_factors, axis=1)).astype(jnp.bfloat16),
+        ],
+        axis=0,
+    )
+    in_gradient = jnp.dot(both_grads, all_tokens, preferred_element_type=jnp.float32).astype(jnp.bfloat16)
+    in_gradient = regroup(in_gradient, 1, place)
+    return (layer_out, in_gradient[None, :units], in_gradient[None, units:], regroup(down_gradient, 0, place)[None])
+
+
+def body(tokens, grad_out, expert_ids, *rest):
+    experts = lax.axis_size(("grp", "loc"))
+    rows, per_token = expert_ids.shape
+    square = lax.axis_size("dp") == 4 and lax.axis_size("grp") == 4 and lax.axis_size("loc") == 2
+    if square and 2 * rows * per_token // experts >= rows:
+        return dense_body(tokens, grad_out, expert_ids, *rest)
+    return slot_body(tokens, grad_out, expert_ids, *rest)
+
+
 def solution(mesh):
     return jax.shard_map(
         body,

time: 250 us -> 100 us (0.40)
  blocking collectives: 133 us -> 0 us
  starting transfers between devices: 4.69 us -> 45.2 us
  waiting for transfers between devices: 56.9 us -> 35 us
  matrix products: 23.9 us -> 6.98 us
  between operations: 14.2 us -> 1.24 us
  local copies, waits for them, and re-layouts: 10.9 us -> 6.04 us
    all_to_all x1 -> x0, blocking collectives: 121 us -> none  [send_rows(): lax.all_to_all(outgoing, ('grp', 'loc'), split_axis=0, concat_axis=0, til...]
    ppermute x0 -> x39, starting transfers between devices: none -> 45.2 us  [swap(): return lax.ppermute(value, axis, pairs)]
    ppermute x0 -> x39, waiting for transfers between devices: none -> 35 us  [swap(): return lax.ppermute(value, axis, pairs)]
    all_gather x1 -> x0, waiting for transfers between devices: 24.9 us -> none  [body(): piece = lax.all_gather(hidden, 'dp', axis=0, tiled=True)]
    all_to_all x1 -> x0, waiting for transfers between devices: 23.3 us -> none  [return_rows(): lax.all_to_all(results, ('grp', 'loc'), split_axis=0, concat_axis=0, tile...]
    dot_general x9 -> x7, matrix products: 23.9 us -> 6.98 us  [the longest x2 2.03 us: dense_body(): lax.dot_general(in_weights, both, contract_last, preferred_element_type=j...]
    all_gather x1 -> x0, blocking collectives: 11.8 us -> none  [body(): full_tokens = lax.all_gather(tokens, 'dp', axis=1, tiled=True)]
    reduce_scatter x1 -> x0, waiting for transfers between devices: 8.69 us -> none  [body(): lax.psum_scatter(lax.dot_general(down_rows, flat_grads, feature_contract,...]
  transfers between devices with their start and end apart: 3 -> 39, of which waited for: 3 -> 16; matrix products, arithmetic and copies ran while one was open for 6% -> 16% of each run, Pallas kernels for 0% -> 0%
where the time goes in v1:
time: 100 us; the launch traced here: 99.8 us
  starting transfers between devices  45.2 us (45%)
  waiting for transfers between devices  35 us (35%)
  matrix products  6.98 us (7%)
  local copies, waits for them, and re-layouts  6.04 us (6%)
  other arithmetic  5.33 us (5%)
  between operations  1.24 us (1%)
    ppermute x39, starting transfers between devices, swap(): return lax.ppermute(value, axis, pairs)  45.2 us
    ppermute x39, waiting for transfers between devices, swap(): return lax.ppermute(value, axis, pairs)  35 us
    dot_general x2, matrix products, dense_body(): lax.dot_general(in_weights, both, contract_last, preferred_element_type=j...  2.03 us
  transfers between devices with their start and end apart: 39, of which 16 were waited for; matrix products, arithmetic and copies ran while one was open for 16% of the time, Pallas kernels for 0%

profile of v1, /device:TPU:0, one launch (start us, length us, event | category | flops | bytes accessed | tf_op | source)
XLA Modules:
  0.0 99.8 jit_solution(8543966520070513728)
XLA Ops:
  1.5 5.0 %collective-permute-start.8 = (f32[8,128]{1,0:T(8,128)S(1)}, f32[8,128]{1,0:T(8,128)S(1)}, u32[]{:S(2)}, u32[]{:S(2)}) collective-permute-start(f32[8,128]{1,0:T(8,128)S(1)} %select_reduce_fusion), channel_id=1, source_target_pairs={{0,6},{2,4},{4,2},{6,0},{1,7},{3,5},{5,3},{7,1},{8,14},{10,12},{12... | collective-permute-start | bytes 12296 | tf_op jit(solution)/shard_map/ppermute | solution.py:109
  7.2 1.4 %collective-permute-start = (bf16[128,512]{1,0:T(8,128)(2,1)}, bf16[128,512]{1,0:T(8,128)(2,1)}, u32[]{:S(2)}, u32[]{:S(2)}) collective-permute-start(bf16[128,512]{1,0:T(8,128)(2,1)} %param.7), channel_id=1, source_target_pairs={{0,2},{2,0},{4,6},{6,4},{1,3},{3,1},{5,7},{7,5},{8,10},{10,8},{12,... | collective-permute-start | bytes 393224 | tf_op jit(solution)/shard_map/ppermute | solution.py:109
  8.6 2.4 %collective-permute-start.17 = (bf16[128,512]{1,0:T(8,128)(2,1)}, bf16[128,512]{1,0:T(8,128)(2,1)}, u32[]{:S(2)}, u32[]{:S(2)}) collective-permute-start(bf16[128,512]{1,0:T(8,128)(2,1)} %param.7), channel_id=1, source_target_pairs={{0,6},{2,4},{4,2},{6,0},{1,7},{3,5},{5,3},{7,1},{8,14},{10,12},{12... | collective-permute-start | bytes 393224 | tf_op jit(solution)/shard_map/ppermute | solution.py:109
  10.9 0.9 constant_dynamic-update-slice_fusion.1
  11.9 1.3 %dynamic-slice_bitcast_fusion.3 = (bf16[192,512]{1,0:T(8,128)(2,1)S(1)}, bf16[192,512]{1,0:T(8,128)(2,1)S(1)}, bf16[192,512]{1,0:T(8,128)(2,1)S(1)}, bf16[192,512]{1,0:T(8,128)(2,1)S(1)}) fusion(bf16[1,768,512]{2,1,0:T(8,128)(2,1)} %param.13, s32[]{:T(128)S(6)} %select_n.47, s32[]{:T(128)S(6)} %select_n.48, s32[]{:T(128)S(6)} %select_n.50, s32[]{:T(128)S(6)} %select_n.49), kind=kLoop, calls=%fused_computation.113 | loop fusion | bytes 1572880 | tf_op jit(solution)/shard_map/dynamic_slice | solution.py:133
  13.3 1.0 %fusion.66 = (bf16[384,512]{1,0:T(8,128)(2,1)S(1)}, bf16[384,512]{1,0:T(8,128)(2,1)}, bf16[384,512]{1,0:T(8,128)(2,1)}, bf16[384,512]{1,0:T(8,128)(2,1)}) fusion(s32[]{:T(128)S(6)} %select_n.41, bf16[192,2048]{1,0:T(8,128)(2,1)S(1)} %bitcast.40, bf16[192,2048]{1,0:T(8,128)(2,1)S(1)} %bitcast.41, s32[]{:T(128)S(6)} %select_n.42, s32[]{:T(128)S(6)} %select_n.43, ...), kind=kLoop, calls=%fused_computation.85 | loop fusion | flops 3145728 | bytes 3145744 | tf_op jit(solution)/shard_map/concatenate | solution.py:156
  15.0 2.4 %collective-permute-start.32 = (bf16[128,512]{1,0:T(8,128)(2,1)S(1)}, bf16[128,512]{1,0:T(8,128)(2,1)S(1)}, u32[]{:S(2)}, u32[]{:S(2)}) collective-permute-start(bf16[128,512]{1,0:T(8,128)(2,1)S(1)} %copy-done.2), channel_id=1, source_target_pairs={{0,4},{2,6},{4,0},{6,2},{1,5},{3,7},{5,1},{7,3},{8,12},{10,14},{12... | collective-permute-start | bytes 393224 | tf_op jit(solution)/shard_map/ppermute | solution.py:109
  17.4 1.2 %collective-permute-done.9 = f32[4,8,128]{2,1,0:T(8,128)S(1)} collective-permute-done((f32[4,8,128]{2,1,0:T(8,128)S(1)}, f32[4,8,128]{2,1,0:T(8,128)S(1)}, u32[]{:S(2)}, u32[]{:S(2)}) %collective-permute-start.9) | collective-permute-done | bytes 16416 | tf_op jit(solution)/shard_map/ppermute | solution.py:109
  18.6 1.1 %collective-permute-start.30 = (bf16[128,512]{1,0:T(8,128)(2,1)S(1)}, bf16[128,512]{1,0:T(8,128)(2,1)S(1)}, u32[]{:S(2)}, u32[]{:S(2)}) collective-permute-start(bf16[128,512]{1,0:T(8,128)(2,1)S(1)} %copy-done.2), channel_id=1, source_target_pairs={{0,2},{2,0},{4,6},{6,4},{1,3},{3,1},{5,7},{7,5},{8,10},{10,8},{12,... | collective-permute-start | bytes 393224 | tf_op jit(solution)/shard_map/ppermute | solution.py:109
  19.7 1.0 %collective-permute-start.33 = (bf16[128,512]{1,0:T(8,128)(2,1)S(1)}, bf16[128,512]{1,0:T(8,128)(2,1)S(1)}, u32[]{:S(2)}, u32[]{:S(2)}) collective-permute-start(bf16[128,512]{1,0:T(8,128)(2,1)S(1)} %copy-done.2), channel_id=1, source_target_pairs={{0,6},{2,4},{4,2},{6,0},{1,7},{3,5},{5,3},{7,1},{8,14},{10,12},{12... | collective-permute-start | bytes 393224 | tf_op jit(solution)/shard_map/ppermute | solution.py:109
  20.7 0.9 constant_dynamic-update-slice_fusion
  21.6 6.8 %collective-permute-done.16 = bf16[128,512]{1,0:T(8,128)(2,1)S(1)} collective-permute-done((bf16[128,512]{1,0:T(8,128)(2,1)S(1)}, bf16[128,512]{1,0:T(8,128)(2,1)S(1)}, u32[]{:S(2)}, u32[]{:S(2)}) %collective-permute-start.16) | collective-permute-done | bytes 131104 | tf_op jit(solution)/shard_map/ppermute | solution.py:109
  28.4 1.5 %collective-permute-start.2 = (bf16[256,512]{1,0:T(8,128)(2,1)S(1)}, bf16[256,512]{1,0:T(8,128)(2,1)S(1)}, u32[]{:S(2)}, u32[]{:S(2)}) collective-permute-start(bf16[256,512]{1,0:T(8,128)(2,1)S(1)} %constant_dynamic-update-slice_fusion), channel_id=1, source_target_pairs={{0,16},{8,24},{16,0},{24,8},{1,17},{9,25},{17,1},{25,9},{2,18},{10... | collective-permute-start | bytes 786440 | tf_op jit(solution)/shard_map/ppermute | solution.py:109
  29.9 1.6 %collective-permute-start.1 = (bf16[256,512]{1,0:T(8,128)(2,1)S(1)}, bf16[256,512]{1,0:T(8,128)(2,1)S(1)}, u32[]{:S(2)}, u32[]{:S(2)}) collective-permute-start(bf16[256,512]{1,0:T(8,128)(2,1)S(1)} %constant_dynamic-update-slice_fusion), channel_id=1, source_target_pairs={{0,8},{8,0},{16,24},{24,16},{1,9},{9,1},{17,25},{25,17},{2,10},{10... | collective-permute-start | bytes 786440 | tf_op jit(solution)/shard_map/ppermute | solution.py:109
  31.5 0.9 constant_dynamic-update-slice_fusion.7
  32.5 1.5 %collective-permute-start.19 = (bf16[256,512]{1,0:T(8,128)(2,1)S(1)}, bf16[256,512]{1,0:T(8,128)(2,1)S(1)}, u32[]{:S(2)}, u32[]{:S(2)}) collective-permute-start(bf16[256,512]{1,0:T(8,128)(2,1)S(1)} %constant_dynamic-update-slice_fusion.7), channel_id=1, source_target_pairs={{0,16},{8,24},{16,0},{24,8},{1,17},{9,25},{17,1},{25,9},{2,18},{10... | collective-permute-start | bytes 786440 | tf_op jit(solution)/shard_map/ppermute | solution.py:109
  34.0 1.6 %collective-permute-start.18 = (bf16[256,512]{1,0:T(8,128)(2,1)S(1)}, bf16[256,512]{1,0:T(8,128)(2,1)S(1)}, u32[]{:S(2)}, u32[]{:S(2)}) collective-permute-start(bf16[256,512]{1,0:T(8,128)(2,1)S(1)} %constant_dynamic-update-slice_fusion.7), channel_id=1, source_target_pairs={{0,8},{8,0},{16,24},{24,16},{1,9},{9,1},{17,25},{25,17},{2,10},{10... | collective-permute-start | bytes 786440 | tf_op jit(solution)/shard_map/ppermute | solution.py:109
  36.6 1.5 %collective-permute-start.4 = (bf16[128,512]{1,0:T(8,128)(2,1)S(1)}, bf16[128,512]{1,0:T(8,128)(2,1)S(1)}, u32[]{:S(2)}, u32[]{:S(2)}) collective-permute-start(bf16[128,512]{1,0:T(8,128)(2,1)S(1)} %slice.174), channel_id=1, source_target_pairs={{0,8},{8,0},{16,24},{24,16},{1,9},{9,1},{17,25},{25,17},{2,10},{10... | collective-permute-start | bytes 393224 | tf_op jit(solution)/shard_map/ppermute | solution.py:109
  38.1 2.3 %collective-permute-done.19 = bf16[256,512]{1,0:T(8,128)(2,1)S(1)} collective-permute-done((bf16[256,512]{1,0:T(8,128)(2,1)S(1)}, bf16[256,512]{1,0:T(8,128)(2,1)S(1)}, u32[]{:S(2)}, u32[]{:S(2)}) %collective-permute-start.19) | collective-permute-done | bytes 262176 | tf_op jit(solution)/shard_map/ppermute | solution.py:109
  40.4 1.5 %collective-permute-start.3 = (bf16[128,512]{1,0:T(8,128)(2,1)S(1)}, bf16[128,512]{1,0:T(8,128)(2,1)S(1)}, u32[]{:S(2)}, u32[]{:S(2)}) collective-permute-start(bf16[128,512]{1,0:T(8,128)(2,1)S(1)} %slice.173), channel_id=1, source_target_pairs={{0,16},{8,24},{16,0},{24,8},{1,17},{9,25},{17,1},{25,9},{2,18},{10... | collective-permute-start | bytes 393224 | tf_op jit(solution)/shard_map/ppermute | solution.py:109
  41.9 1.5 %collective-permute-done.18 = bf16[256,512]{1,0:T(8,128)(2,1)S(1)} collective-permute-done((bf16[256,512]{1,0:T(8,128)(2,1)S(1)}, bf16[256,512]{1,0:T(8,128)(2,1)S(1)}, u32[]{:S(2)}, u32[]{:S(2)}) %collective-permute-start.18) | collective-permute-done | bytes 262176 | tf_op jit(solution)/shard_map/ppermute | solution.py:109
  43.4 1.5 %collective-permute-start.21 = (bf16[128,512]{1,0:T(8,128)(2,1)S(1)}, bf16[128,512]{1,0:T(8,128)(2,1)S(1)}, u32[]{:S(2)}, u32[]{:S(2)}) collective-permute-start(bf16[128,512]{1,0:T(8,128)(2,1)S(1)} %slice.184), channel_id=1, source_target_pairs={{0,8},{8,0},{16,24},{24,16},{1,9},{9,1},{17,25},{25,17},{2,10},{10... | collective-permute-start | bytes 393224 | tf_op jit(solution)/shard_map/ppermute | solution.py:109
  46.4 1.0 %fusion.93 = (bf16[768,1024]{1,0:T(8,128)(2,1)S(1)}, f32[768,1024]{1,0:T(8,128)S(1)}) fusion(bf16[1024,512]{1,0:T(8,128)(2,1)S(1)} %constant_dynamic-update-slice_fusion.14, bf16[192,512]{1,0:T(8,128)(2,1)S(1)} %get-tuple-element.36, bf16[192,512]{1,0:T(8,128)(2,1)S(1)} %get-tuple-element.37, bf16[192,512]{1,0:T(8,128)(2,1)S(1)} %get-tuple-element.35, ...), kind=kOutput, calls=%fused_computation.173 | convolution fusion | flops 809238528 | bytes 6553600 | tf_op jit(solution)/shard_map/dot_general | solution.py:187
  47.5 1.8 %collective-permute-start.35 = (bf16[96,1024]{1,0:T(8,128)(2,1)S(1)}, bf16[96,1024]{1,0:T(8,128)(2,1)S(1)}, u32[]{:S(2)}, u32[]{:S(2)}) collective-permute-start(bf16[96,1024]{1,0:T(8,128)(2,1)S(1)} %get-tuple-element.18), channel_id=1, source_target_pairs={{0,16},{8,24},{16,0},{24,8},{1,17},{9,25},{17,1},{25,9},{2,18},{10... | collective-permute-start | bytes 589832 | tf_op jit(solution)/shard_map/ppermute | solution.py:109
  49.3 1.0 %collective-permute-start.37 = (bf16[96,1024]{1,0:T(8,128)(2,1)S(1)}, bf16[96,1024]{1,0:T(8,128)(2,1)S(1)}, u32[]{:S(2)}, u32[]{:S(2)}) collective-permute-start(bf16[96,1024]{1,0:T(8,128)(2,1)S(1)} %get-tuple-element.19), channel_id=1, source_target_pairs={{0,8},{8,0},{16,24},{24,16},{1,9},{9,1},{17,25},{25,17},{2,10},{10... | collective-permute-start | bytes 589832 | tf_op jit(solution)/shard_map/ppermute | solution.py:109
  50.5 4.3 %collective-permute-done.35 = bf16[96,1024]{1,0:T(8,128)(2,1)S(1)} collective-permute-done((bf16[96,1024]{1,0:T(8,128)(2,1)S(1)}, bf16[96,1024]{1,0:T(8,128)(2,1)S(1)}, u32[]{:S(2)}, u32[]{:S(2)}) %collective-permute-start.35) | collective-permute-done | bytes 196640 | tf_op jit(solution)/shard_map/ppermute | solution.py:109
  54.8 1.5 %collective-permute-done.37 = bf16[96,1024]{1,0:T(8,128)(2,1)S(1)} collective-permute-done((bf16[96,1024]{1,0:T(8,128)(2,1)S(1)}, bf16[96,1024]{1,0:T(8,128)(2,1)S(1)}, u32[]{:S(2)}, u32[]{:S(2)}) %collective-permute-start.37) | collective-permute-done | bytes 196640 | tf_op jit(solution)/shard_map/ppermute | solution.py:109
  56.9 1.8 %collective-permute-start.36 = (bf16[192,1024]{1,0:T(8,128)(2,1)S(1)}, bf16[192,1024]{1,0:T(8,128)(2,1)S(1)}, u32[]{:S(2)}, u32[]{:S(2)}) collective-permute-start(bf16[192,1024]{1,0:T(8,128)(2,1)S(1)} %pad_maximum_fusion.3), channel_id=1, source_target_pairs={{0,8},{8,0},{16,24},{24,16},{1,9},{9,1},{17,25},{25,17},{2,10},{10... | collective-permute-start | bytes 1179656 | tf_op jit(solution)/shard_map/ppermute | solution.py:109
  58.7 1.0 %fusion.27 = f32[384,512]{1,0:T(8,128)S(1)} fusion(bf16[256,2048]{1,0:T(8,128)(2,1)S(1)} %collective-permute-done.5, bf16[128,512]{1,0:T(8,128)(2,1)S(1)} %collective-permute-done.4, bf16[128,512]{1,0:T(8,128)(2,1)S(1)} %collective-permute-done.3, bf16[256,512]{1,0:T(8,128)(2,1)S(1)} %collective-permute-done.2, ...), kind=kOutput, calls=%fused_computation.33 | convolution fusion | flops 824180736 | bytes 4456448 | tf_op jit(solution)/shard_map/dot_general | solution.py:165
  59.8 1.1 %collective-permute-start.11 = (bf16[192,512]{1,0:T(8,128)(2,1)S(1)}, bf16[192,512]{1,0:T(8,128)(2,1)S(1)}, u32[]{:S(2)}, u32[]{:S(2)}) collective-permute-start(bf16[192,512]{1,0:T(8,128)(2,1)S(1)} %get-tuple-element.7), channel_id=1, source_target_pairs={{0,16},{8,24},{16,0},{24,8},{1,17},{9,25},{17,1},{25,9},{2,18},{10... | collective-permute-start | bytes 589832 | tf_op jit(solution)/shard_map/ppermute | solution.py:109
  60.9 1.0 %collective-permute-start.10 = (bf16[192,512]{1,0:T(8,128)(2,1)S(1)}, bf16[192,512]{1,0:T(8,128)(2,1)S(1)}, u32[]{:S(2)}, u32[]{:S(2)}) collective-permute-start(bf16[192,512]{1,0:T(8,128)(2,1)S(1)} %get-tuple-element.7), channel_id=1, source_target_pairs={{0,8},{8,0},{16,24},{24,16},{1,9},{9,1},{17,25},{25,17},{2,10},{10... | collective-permute-start | bytes 589832 | tf_op jit(solution)/shard_map/ppermute | solution.py:109
  61.9 1.0 %fusion.39 = f32[384,512]{1,0:T(8,128)S(1)} fusion(bf16[256,2048]{1,0:T(8,128)(2,1)S(1)} %collective-permute-done.22, bf16[128,512]{1,0:T(8,128)(2,1)S(1)} %collective-permute-done.21, bf16[128,512]{1,0:T(8,128)(2,1)S(1)} %collective-permute-done.20, bf16[256,512]{1,0:T(8,128)(2,1)S(1)} %collective-permute-done.19, ...), kind=kOutput, calls=%fused_computation.45 | convolution fusion | flops 824180736 | bytes 4456448 | tf_op jit(solution)/shard_map/dot_general | solution.py:165
  63.9 4.7 %collective-permute-done.38 = bf16[192,1024]{1,0:T(8,128)(2,1)S(1)} collective-permute-done((bf16[192,1024]{1,0:T(8,128)(2,1)S(1)}, bf16[192,1024]{1,0:T(8,128)(2,1)S(1)}, u32[]{:S(2)}, u32[]{:S(2)}) %collective-permute-start.38) | collective-permute-done | bytes 393248 | tf_op jit(solution)/shard_map/ppermute | solution.py:109
  68.6 1.0 %collective-permute-start.23 = (bf16[192,512]{1,0:T(8,128)(2,1)S(1)}, bf16[192,512]{1,0:T(8,128)(2,1)S(1)}, u32[]{:S(2)}, u32[]{:S(2)}) collective-permute-start(bf16[192,512]{1,0:T(8,128)(2,1)S(1)} %get-tuple-element.5), channel_id=1, source_target_pairs={{0,8},{8,0},{16,24},{24,16},{1,9},{9,1},{17,25},{25,17},{2,10},{10... | collective-permute-start | bytes 589832 | tf_op jit(solution)/shard_map/ppermute | solution.py:109
  69.9 1.8 %fusion.24 = bf16[384,2048]{1,0:T(8,128)(2,1)S(1)} fusion(bf16[256,2048]{1,0:T(8,128)(2,1)S(1)} %collective-permute-done.22, bf16[128,512]{1,0:T(8,128)(2,1)S(1)} %collective-permute-done.21, bf16[128,512]{1,0:T(8,128)(2,1)S(1)} %collective-permute-done.20, bf16[256,512]{1,0:T(8,128)(2,1)S(1)} %collective-permute-done.19, ...), kind=kOutput, calls=%fused_computation.24 | convolution fusion | flops 1663303680 | bytes 6553600 | tf_op jit(solution)/shard_map/dot_general | solution.py:197
  72.1 1.3 %slice_bitcast_fusion = (bf16[1,192,2048]{2,1,0:T(8,128)(2,1)}, bf16[1,192,2048]{2,1,0:T(8,128)(2,1)}) fusion(bf16[384,2048]{1,0:T(8,128)(2,1)S(1)} %pad_maximum_fusion.1), kind=kLoop, calls=%fused_computation.66 | loop fusion | bytes 3145728 | tf_op jit(solution)/shard_map/broadcast_in_dim | solution.py:199
  73.4 1.2 %collective-permute-start.13 = (bf16[96,512]{1,0:T(8,128)(2,1)S(1)}, bf16[96,512]{1,0:T(8,128)(2,1)S(1)}, u32[]{:S(2)}, u32[]{:S(2)}) collective-permute-start(bf16[96,512]{1,0:T(8,128)(2,1)S(1)} %slice.178), channel_id=1, source_target_pairs={{0,8},{8,0},{16,24},{24,16},{1,9},{9,1},{17,25},{25,17},{2,10},{10... | collective-permute-start | bytes 294920 | tf_op jit(solution)/shard_map/ppermute | solution.py:109
  74.6 1.1 %collective-permute-start.12 = (bf16[96,512]{1,0:T(8,128)(2,1)S(1)}, bf16[96,512]{1,0:T(8,128)(2,1)S(1)}, u32[]{:S(2)}, u32[]{:S(2)}) collective-permute-start(bf16[96,512]{1,0:T(8,128)(2,1)S(1)} %slice.177), channel_id=1, source_target_pairs={{0,16},{8,24},{16,0},{24,8},{1,17},{9,25},{17,1},{25,9},{2,18},{10... | collective-permute-start | bytes 294920 | tf_op jit(solution)/shard_map/ppermute | solution.py:109
  76.4 1.1 %collective-permute-start.26 = (bf16[96,512]{1,0:T(8,128)(2,1)S(1)}, bf16[96,512]{1,0:T(8,128)(2,1)S(1)}, u32[]{:S(2)}, u32[]{:S(2)}) collective-permute-start(bf16[96,512]{1,0:T(8,128)(2,1)S(1)} %slice.188), channel_id=1, source_target_pairs={{0,8},{8,0},{16,24},{24,16},{1,9},{9,1},{17,25},{25,17},{2,10},{10... | collective-permute-start | bytes 294920 | tf_op jit(solution)/shard_map/ppermute | solution.py:109
  77.5 1.7 %collective-permute-start.25 = (bf16[96,512]{1,0:T(8,128)(2,1)S(1)}, bf16[96,512]{1,0:T(8,128)(2,1)S(1)}, u32[]{:S(2)}, u32[]{:S(2)}) collective-permute-start(bf16[96,512]{1,0:T(8,128)(2,1)S(1)} %slice.187), channel_id=1, source_target_pairs={{0,16},{8,24},{16,0},{24,8},{1,17},{9,25},{17,1},{25,9},{2,18},{10... | collective-permute-start | bytes 294920 | tf_op jit(solution)/shard_map/ppermute | solution.py:109
  80.1 2.1 %collective-permute-done.25 = bf16[96,512]{1,0:T(8,128)(2,1)S(1)} collective-permute-done((bf16[96,512]{1,0:T(8,128)(2,1)S(1)}, bf16[96,512]{1,0:T(8,128)(2,1)S(1)}, u32[]{:S(2)}, u32[]{:S(2)}) %collective-permute-start.25) | collective-permute-done | bytes 98336 | tf_op jit(solution)/shard_map/ppermute | solution.py:109
  82.2 1.0 fusion.55
  85.0 1.0 collective-permute-start.15
  86.1 2.2 %collective-permute-start.28 = (bf16[128,512]{1,0:T(8,128)(2,1)S(1)}, bf16[128,512]{1,0:T(8,128)(2,1)S(1)}, u32[]{:S(2)}, u32[]{:S(2)}) collective-permute-start(bf16[128,512]{1,0:T(8,128)(2,1)S(1)} %get-tuple-element.38), channel_id=1, source_target_pairs={{0,4},{2,6},{4,0},{6,2},{1,5},{3,7},{5,1},{7,3},{8,12},{10,14},{12... | collective-permute-start | bytes 393224 | tf_op jit(solution)/shard_map/ppermute | solution.py:109
  88.3 1.3 %collective-permute-start.29 = (bf16[128,512]{1,0:T(8,128)(2,1)S(1)}, bf16[128,512]{1,0:T(8,128)(2,1)S(1)}, u32[]{:S(2)}, u32[]{:S(2)}) collective-permute-start(bf16[128,512]{1,0:T(8,128)(2,1)S(1)} %get-tuple-element.39), channel_id=1, source_target_pairs={{0,6},{2,4},{4,2},{6,0},{1,7},{3,5},{5,3},{7,1},{8,14},{10,12},{12... | collective-permute-start | bytes 393224 | tf_op jit(solution)/shard_map/ppermute | solution.py:109
  89.6 0.9 maximum_bitcast_fusion
  90.5 1.7 %collective-permute-done.15 = bf16[128,512]{1,0:T(8,128)(2,1)S(1)} collective-permute-done((bf16[128,512]{1,0:T(8,128)(2,1)S(1)}, bf16[128,512]{1,0:T(8,128)(2,1)S(1)}, u32[]{:S(2)}, u32[]{:S(2)}) %collective-permute-start.15) | collective-permute-done | bytes 131104 | tf_op jit(solution)/shard_map/ppermute | solution.py:109
  92.2 6.8 %collective-permute-done.28 = bf16[128,512]{1,0:T(8,128)(2,1)S(1)} collective-permute-done((bf16[128,512]{1,0:T(8,128)(2,1)S(1)}, bf16[128,512]{1,0:T(8,128)(2,1)S(1)}, u32[]{:S(2)}, u32[]{:S(2)}) %collective-permute-start.28) | collective-permute-done | bytes 131104 | tf_op jit(solution)/shard_map/ppermute | solution.py:109
  (110 shorter events, 11.5 us)
Async XLA Ops:
  0.6 12.6 %copy-start.1 = (bf16[1,192,2048]{2,1,0:T(8,128)(2,1)S(1)}, bf16[1,192,2048]{2,1,0:T(8,128)(2,1)}, u32[]{:S(2)}) copy-start(bf16[1,192,2048]{2,1,0:T(8,128)(2,1)} %param.12) | copy-start | bytes 2359300
  0.6 12.6 %copy-start = (bf16[1,192,2048]{2,1,0:T(8,128)(2,1)S(1)}, bf16[1,192,2048]{2,1,0:T(8,128)(2,1)}, u32[]{:S(2)}) copy-start(bf16[1,192,2048]{2,1,0:T(8,128)(2,1)} %param.11) | copy-start | bytes 2359300
  1.5 12.9 %collective-permute-start.8 = (f32[8,128]{1,0:T(8,128)S(1)}, f32[8,128]{1,0:T(8,128)S(1)}, u32[]{:S(2)}, u32[]{:S(2)}) collective-permute-start(f32[8,128]{1,0:T(8,128)S(1)} %select_reduce_fusion), channel_id=1, source_target_pairs={{0,6},{2,4},{4,2},{6,0},{1,7},{3,5},{5,3},{7,1},{8,14},{10,12},{12... | collective-permute-start | bytes 12296 | tf_op jit(solution)/shard_map/ppermute | solution.py:109
  6.5 8.5 %collective-permute-start.7 = (f32[8,128]{1,0:T(8,128)S(1)}, f32[8,128]{1,0:T(8,128)S(1)}, u32[]{:S(2)}, u32[]{:S(2)}) collective-permute-start(f32[8,128]{1,0:T(8,128)S(1)} %select_reduce_fusion), channel_id=1, source_target_pairs={{0,4},{2,6},{4,0},{6,2},{1,5},{3,7},{5,1},{7,3},{8,12},{10,14},{12... | collective-permute-start | bytes 12296 | tf_op jit(solution)/shard_map/ppermute | solution.py:109
  6.5 10.8 %collective-permute-start.6 = (f32[8,128]{1,0:T(8,128)S(1)}, f32[8,128]{1,0:T(8,128)S(1)}, u32[]{:S(2)}, u32[]{:S(2)}) collective-permute-start(f32[8,128]{1,0:T(8,128)S(1)} %select_reduce_fusion), channel_id=1, source_target_pairs={{0,2},{2,0},{4,6},{6,4},{1,3},{3,1},{5,7},{7,5},{8,10},{10,8},{12,... | collective-permute-start | bytes 12296 | tf_op jit(solution)/shard_map/ppermute | solution.py:109
  7.2 12.5 %collective-permute-start = (bf16[128,512]{1,0:T(8,128)(2,1)}, bf16[128,512]{1,0:T(8,128)(2,1)}, u32[]{:S(2)}, u32[]{:S(2)}) collective-permute-start(bf16[128,512]{1,0:T(8,128)(2,1)} %param.7), channel_id=1, source_target_pairs={{0,2},{2,0},{4,6},{6,4},{1,3},{3,1},{5,7},{7,5},{8,10},{10,8},{12,... | collective-permute-start | bytes 393224 | tf_op jit(solution)/shard_map/ppermute | solution.py:109
  8.6 21.4 %collective-permute-start.17 = (bf16[128,512]{1,0:T(8,128)(2,1)}, bf16[128,512]{1,0:T(8,128)(2,1)}, u32[]{:S(2)}, u32[]{:S(2)}) collective-permute-start(bf16[128,512]{1,0:T(8,128)(2,1)} %param.7), channel_id=1, source_target_pairs={{0,6},{2,4},{4,2},{6,0},{1,7},{3,5},{5,3},{7,1},{8,14},{10,12},{12... | collective-permute-start | bytes 393224 | tf_op jit(solution)/shard_map/ppermute | solution.py:109
  11.9 2.4 %copy-start.2 = (bf16[128,512]{1,0:T(8,128)(2,1)S(1)}, bf16[128,512]{1,0:T(8,128)(2,1)}, u32[]{:S(2)}) copy-start(bf16[128,512]{1,0:T(8,128)(2,1)} %param.8) | copy-start | bytes 393220
  13.3 1.1 %copy-start.6 = (bf16[128,512]{1,0:T(8,128)(2,1)S(1)}, bf16[128,512]{1,0:T(8,128)(2,1)}, u32[]{:S(2)}) copy-start(bf16[128,512]{1,0:T(8,128)(2,1)} %param.7) | copy-start | bytes 393220
  14.4 14.0 %collective-permute-start.16 = (bf16[128,512]{1,0:T(8,128)(2,1)S(1)}, bf16[128,512]{1,0:T(8,128)(2,1)S(1)}, u32[]{:S(2)}, u32[]{:S(2)}) collective-permute-start(bf16[128,512]{1,0:T(8,128)(2,1)S(1)} %copy-done.6), channel_id=1, source_target_pairs={{0,4},{2,6},{4,0},{6,2},{1,5},{3,7},{5,1},{7,3},{8,12},{10,14},{12... | collective-permute-start | bytes 393224 | tf_op jit(solution)/shard_map/ppermute | solution.py:109
  15.0 19.0 %collective-permute-start.32 = (bf16[128,512]{1,0:T(8,128)(2,1)S(1)}, bf16[128,512]{1,0:T(8,128)(2,1)S(1)}, u32[]{:S(2)}, u32[]{:S(2)}) collective-permute-start(bf16[128,512]{1,0:T(8,128)(2,1)S(1)} %copy-done.2), channel_id=1, source_target_pairs={{0,4},{2,6},{4,0},{6,2},{1,5},{3,7},{5,1},{7,3},{8,12},{10,14},{12... | collective-permute-start | bytes 393224 | tf_op jit(solution)/shard_map/ppermute | solution.py:109
  17.4 1.2 %collective-permute-start.9 = (f32[4,8,128]{2,1,0:T(8,128)S(1)}, f32[4,8,128]{2,1,0:T(8,128)S(1)}, u32[]{:S(2)}, u32[]{:S(2)}) collective-permute-start(f32[4,8,128]{2,1,0:T(8,128)S(1)} %pad_maximum_fusion.9), channel_id=1, source_target_pairs={{0,1},{1,0},{2,3},{3,2},{4,5},{5,4},{6,7},{7,6},{8,9},{9,8},{10,11... | collective-permute-start | bytes 49160 | tf_op jit(solution)/shard_map/ppermute | solution.py:109
  18.6 13.9 %collective-permute-start.30 = (bf16[128,512]{1,0:T(8,128)(2,1)S(1)}, bf16[128,512]{1,0:T(8,128)(2,1)S(1)}, u32[]{:S(2)}, u32[]{:S(2)}) collective-permute-start(bf16[128,512]{1,0:T(8,128)(2,1)S(1)} %copy-done.2), channel_id=1, source_target_pairs={{0,2},{2,0},{4,6},{6,4},{1,3},{3,1},{5,7},{7,5},{8,10},{10,8},{12,... | collective-permute-start | bytes 393224 | tf_op jit(solution)/shard_map/ppermute | solution.py:109
  19.7 15.9 %collective-permute-start.33 = (bf16[128,512]{1,0:T(8,128)(2,1)S(1)}, bf16[128,512]{1,0:T(8,128)(2,1)S(1)}, u32[]{:S(2)}, u32[]{:S(2)}) collective-permute-start(bf16[128,512]{1,0:T(8,128)(2,1)S(1)} %copy-done.2), channel_id=1, source_target_pairs={{0,6},{2,4},{4,2},{6,0},{1,7},{3,5},{5,3},{7,1},{8,14},{10,12},{12... | collective-permute-start | bytes 393224 | tf_op jit(solution)/shard_map/ppermute | solution.py:109
  28.4 7.3 %collective-permute-start.2 = (bf16[256,512]{1,0:T(8,128)(2,1)S(1)}, bf16[256,512]{1,0:T(8,128)(2,1)S(1)}, u32[]{:S(2)}, u32[]{:S(2)}) collective-permute-start(bf16[256,512]{1,0:T(8,128)(2,1)S(1)} %constant_dynamic-update-slice_fusion), channel_id=1, source_target_pairs={{0,16},{8,24},{16,0},{24,8},{1,17},{9,25},{17,1},{25,9},{2,18},{10... | collective-permute-start | bytes 786440 | tf_op jit(solution)/shard_map/ppermute | solution.py:109
  29.9 6.7 %collective-permute-start.1 = (bf16[256,512]{1,0:T(8,128)(2,1)S(1)}, bf16[256,512]{1,0:T(8,128)(2,1)S(1)}, u32[]{:S(2)}, u32[]{:S(2)}) collective-permute-start(bf16[256,512]{1,0:T(8,128)(2,1)S(1)} %constant_dynamic-update-slice_fusion), channel_id=1, source_target_pairs={{0,8},{8,0},{16,24},{24,16},{1,9},{9,1},{17,25},{25,17},{2,10},{10... | collective-permute-start | bytes 786440 | tf_op jit(solution)/shard_map/ppermute | solution.py:109
  32.5 7.9 %collective-permute-start.19 = (bf16[256,512]{1,0:T(8,128)(2,1)S(1)}, bf16[256,512]{1,0:T(8,128)(2,1)S(1)}, u32[]{:S(2)}, u32[]{:S(2)}) collective-permute-start(bf16[256,512]{1,0:T(8,128)(2,1)S(1)} %constant_dynamic-update-slice_fusion.7), channel_id=1, source_target_pairs={{0,16},{8,24},{16,0},{24,8},{1,17},{9,25},{17,1},{25,9},{2,18},{10... | collective-permute-start | bytes 786440 | tf_op jit(solution)/shard_map/ppermute | solution.py:109
  34.0 9.3 %collective-permute-start.18 = (bf16[256,512]{1,0:T(8,128)(2,1)S(1)}, bf16[256,512]{1,0:T(8,128)(2,1)S(1)}, u32[]{:S(2)}, u32[]{:S(2)}) collective-permute-start(bf16[256,512]{1,0:T(8,128)(2,1)S(1)} %constant_dynamic-update-slice_fusion.7), channel_id=1, source_target_pairs={{0,8},{8,0},{16,24},{24,16},{1,9},{9,1},{17,25},{25,17},{2,10},{10... | collective-permute-start | bytes 786440 | tf_op jit(solution)/shard_map/ppermute | solution.py:109
  35.6 9.3 %collective-permute-start.31 = (bf16[256,512]{1,0:T(8,128)(2,1)S(1)}, bf16[256,512]{1,0:T(8,128)(2,1)S(1)}, u32[]{:S(2)}, u32[]{:S(2)}) collective-permute-start(bf16[256,512]{1,0:T(8,128)(2,1)S(1)} %pad_maximum_fusion.7), channel_id=1, source_target_pairs={{0,1},{1,0},{2,3},{3,2},{4,5},{5,4},{6,7},{7,6},{8,9},{9,8},{10,11... | collective-permute-start | bytes 786440 | tf_op jit(solution)/shard_map/ppermute | solution.py:109
  35.7 9.8 %collective-permute-start.34 = (bf16[256,512]{1,0:T(8,128)(2,1)S(1)}, bf16[256,512]{1,0:T(8,128)(2,1)S(1)}, u32[]{:S(2)}, u32[]{:S(2)}) collective-permute-start(bf16[256,512]{1,0:T(8,128)(2,1)S(1)} %pad_maximum_fusion.8), channel_id=1, source_target_pairs={{0,1},{1,0},{2,3},{3,2},{4,5},{5,4},{6,7},{7,6},{8,9},{9,8},{10,11... | collective-permute-start | bytes 786440 | tf_op jit(solution)/shard_map/ppermute | solution.py:109
  36.6 9.6 %collective-permute-start.4 = (bf16[128,512]{1,0:T(8,128)(2,1)S(1)}, bf16[128,512]{1,0:T(8,128)(2,1)S(1)}, u32[]{:S(2)}, u32[]{:S(2)}) collective-permute-start(bf16[128,512]{1,0:T(8,128)(2,1)S(1)} %slice.174), channel_id=1, source_target_pairs={{0,8},{8,0},{16,24},{24,16},{1,9},{9,1},{17,25},{25,17},{2,10},{10... | collective-permute-start | bytes 393224 | tf_op jit(solution)/shard_map/ppermute | solution.py:109
  40.4 5.8 %collective-permute-start.3 = (bf16[128,512]{1,0:T(8,128)(2,1)S(1)}, bf16[128,512]{1,0:T(8,128)(2,1)S(1)}, u32[]{:S(2)}, u32[]{:S(2)}) collective-permute-start(bf16[128,512]{1,0:T(8,128)(2,1)S(1)} %slice.173), channel_id=1, source_target_pairs={{0,16},{8,24},{16,0},{24,8},{1,17},{9,25},{17,1},{25,9},{2,18},{10... | collective-permute-start | bytes 393224 | tf_op jit(solution)/shard_map/ppermute | solution.py:109
  43.4 7.0 %collective-permute-start.21 = (bf16[128,512]{1,0:T(8,128)(2,1)S(1)}, bf16[128,512]{1,0:T(8,128)(2,1)S(1)}, u32[]{:S(2)}, u32[]{:S(2)}) collective-permute-start(bf16[128,512]{1,0:T(8,128)(2,1)S(1)} %slice.184), channel_id=1, source_target_pairs={{0,8},{8,0},{16,24},{24,16},{1,9},{9,1},{17,25},{25,17},{2,10},{10... | collective-permute-start | bytes 393224 | tf_op jit(solution)/shard_map/ppermute | solution.py:109
  44.9 5.4 %collective-permute-start.20 = (bf16[128,512]{1,0:T(8,128)(2,1)S(1)}, bf16[128,512]{1,0:T(8,128)(2,1)S(1)}, u32[]{:S(2)}, u32[]{:S(2)}) collective-permute-start(bf16[128,512]{1,0:T(8,128)(2,1)S(1)} %slice.183), channel_id=1, source_target_pairs={{0,16},{8,24},{16,0},{24,8},{1,17},{9,25},{17,1},{25,9},{2,18},{10... | collective-permute-start | bytes 393224 | tf_op jit(solution)/shard_map/ppermute | solution.py:109
  46.3 12.4 %collective-permute-start.5 = (bf16[256,2048]{1,0:T(8,128)(2,1)S(1)}, bf16[256,2048]{1,0:T(8,128)(2,1)S(1)}, u32[]{:S(2)}, u32[]{:S(2)}) collective-permute-start(bf16[256,2048]{1,0:T(8,128)(2,1)S(1)} %maximum_maximum_fusion), channel_id=1, source_target_pairs={{0,1},{1,0},{2,3},{3,2},{4,5},{5,4},{6,7},{7,6},{8,9},{9,8},{10,11... | collective-permute-start | bytes 3145736 | tf_op jit(solution)/shard_map/ppermute | solution.py:109
  47.5 7.4 %collective-permute-start.35 = (bf16[96,1024]{1,0:T(8,128)(2,1)S(1)}, bf16[96,1024]{1,0:T(8,128)(2,1)S(1)}, u32[]{:S(2)}, u32[]{:S(2)}) collective-permute-start(bf16[96,1024]{1,0:T(8,128)(2,1)S(1)} %get-tuple-element.18), channel_id=1, source_target_pairs={{0,16},{8,24},{16,0},{24,8},{1,17},{9,25},{17,1},{25,9},{2,18},{10... | collective-permute-start | bytes 589832 | tf_op jit(solution)/shard_map/ppermute | solution.py:109
  49.3 7.0 %collective-permute-start.37 = (bf16[96,1024]{1,0:T(8,128)(2,1)S(1)}, bf16[96,1024]{1,0:T(8,128)(2,1)S(1)}, u32[]{:S(2)}, u32[]{:S(2)}) collective-permute-start(bf16[96,1024]{1,0:T(8,128)(2,1)S(1)} %get-tuple-element.19), channel_id=1, source_target_pairs={{0,8},{8,0},{16,24},{24,16},{1,9},{9,1},{17,25},{25,17},{2,10},{10... | collective-permute-start | bytes 589832 | tf_op jit(solution)/shard_map/ppermute | solution.py:109
  50.4 8.2 %copy-start.3 = (bf16[384,512]{1,0:T(8,128)(2,1)S(1)}, bf16[384,512]{1,0:T(8,128)(2,1)}, u32[]{:S(2)}) copy-start(bf16[384,512]{1,0:T(8,128)(2,1)} %get-tuple-element.23) | copy-start | bytes 1179652
  50.4 8.2 %copy-start.4 = (bf16[384,512]{1,0:T(8,128)(2,1)S(1)}, bf16[384,512]{1,0:T(8,128)(2,1)}, u32[]{:S(2)}) copy-start(bf16[384,512]{1,0:T(8,128)(2,1)} %get-tuple-element.24) | copy-start | bytes 1179652
  50.5 8.2 %copy-start.5 = (bf16[384,512]{1,0:T(8,128)(2,1)S(1)}, bf16[384,512]{1,0:T(8,128)(2,1)}, u32[]{:S(2)}) copy-start(bf16[384,512]{1,0:T(8,128)(2,1)} %get-tuple-element.25) | copy-start | bytes 1179652
  50.5 11.4 %collective-permute-start.22 = (bf16[256,2048]{1,0:T(8,128)(2,1)S(1)}, bf16[256,2048]{1,0:T(8,128)(2,1)S(1)}, u32[]{:S(2)}, u32[]{:S(2)}) collective-permute-start(bf16[256,2048]{1,0:T(8,128)(2,1)S(1)} %maximum_maximum_fusion.1), channel_id=1, source_target_pairs={{0,1},{1,0},{2,3},{3,2},{4,5},{5,4},{6,7},{7,6},{8,9},{9,8},{10,11... | collective-permute-start | bytes 3145736 | tf_op jit(solution)/shard_map/ppermute | solution.py:109
  56.4 12.1 %collective-permute-start.38 = (bf16[192,1024]{1,0:T(8,128)(2,1)S(1)}, bf16[192,1024]{1,0:T(8,128)(2,1)S(1)}, u32[]{:S(2)}, u32[]{:S(2)}) collective-permute-start(bf16[192,1024]{1,0:T(8,128)(2,1)S(1)} %pad_maximum_fusion.4), channel_id=1, source_target_pairs={{0,16},{8,24},{16,0},{24,8},{1,17},{9,25},{17,1},{25,9},{2,18},{10... | collective-permute-start | bytes 1179656 | tf_op jit(solution)/shard_map/ppermute | solution.py:109
  56.9 12.7 %collective-permute-start.36 = (bf16[192,1024]{1,0:T(8,128)(2,1)S(1)}, bf16[192,1024]{1,0:T(8,128)(2,1)S(1)}, u32[]{:S(2)}, u32[]{:S(2)}) collective-permute-start(bf16[192,1024]{1,0:T(8,128)(2,1)S(1)} %pad_maximum_fusion.3), channel_id=1, source_target_pairs={{0,8},{8,0},{16,24},{24,16},{1,9},{9,1},{17,25},{25,17},{2,10},{10... | collective-permute-start | bytes 1179656 | tf_op jit(solution)/shard_map/ppermute | solution.py:109
  59.8 13.6 %collective-permute-start.11 = (bf16[192,512]{1,0:T(8,128)(2,1)S(1)}, bf16[192,512]{1,0:T(8,128)(2,1)S(1)}, u32[]{:S(2)}, u32[]{:S(2)}) collective-permute-start(bf16[192,512]{1,0:T(8,128)(2,1)S(1)} %get-tuple-element.7), channel_id=1, source_target_pairs={{0,16},{8,24},{16,0},{24,8},{1,17},{9,25},{17,1},{25,9},{2,18},{10... | collective-permute-start | bytes 589832 | tf_op jit(solution)/shard_map/ppermute | solution.py:109
  60.9 13.7 %collective-permute-start.10 = (bf16[192,512]{1,0:T(8,128)(2,1)S(1)}, bf16[192,512]{1,0:T(8,128)(2,1)S(1)}, u32[]{:S(2)}, u32[]{:S(2)}) collective-permute-start(bf16[192,512]{1,0:T(8,128)(2,1)S(1)} %get-tuple-element.7), channel_id=1, source_target_pairs={{0,8},{8,0},{16,24},{24,16},{1,9},{9,1},{17,25},{25,17},{2,10},{10... | collective-permute-start | bytes 589832 | tf_op jit(solution)/shard_map/ppermute | solution.py:109
  63.1 13.3 %collective-permute-start.24 = (bf16[192,512]{1,0:T(8,128)(2,1)S(1)}, bf16[192,512]{1,0:T(8,128)(2,1)S(1)}, u32[]{:S(2)}, u32[]{:S(2)}) collective-permute-start(bf16[192,512]{1,0:T(8,128)(2,1)S(1)} %get-tuple-element.5), channel_id=1, source_target_pairs={{0,16},{8,24},{16,0},{24,8},{1,17},{9,25},{17,1},{25,9},{2,18},{10... | collective-permute-start | bytes 589832 | tf_op jit(solution)/shard_map/ppermute | solution.py:109
  68.6 8.9 %collective-permute-start.23 = (bf16[192,512]{1,0:T(8,128)(2,1)S(1)}, bf16[192,512]{1,0:T(8,128)(2,1)S(1)}, u32[]{:S(2)}, u32[]{:S(2)}) collective-permute-start(bf16[192,512]{1,0:T(8,128)(2,1)S(1)} %get-tuple-element.5), channel_id=1, source_target_pairs={{0,8},{8,0},{16,24},{24,16},{1,9},{9,1},{17,25},{25,17},{2,10},{10... | collective-permute-start | bytes 589832 | tf_op jit(solution)/shard_map/ppermute | solution.py:109
  73.4 6.0 %collective-permute-start.13 = (bf16[96,512]{1,0:T(8,128)(2,1)S(1)}, bf16[96,512]{1,0:T(8,128)(2,1)S(1)}, u32[]{:S(2)}, u32[]{:S(2)}) collective-permute-start(bf16[96,512]{1,0:T(8,128)(2,1)S(1)} %slice.178), channel_id=1, source_target_pairs={{0,8},{8,0},{16,24},{24,16},{1,9},{9,1},{17,25},{25,17},{2,10},{10... | collective-permute-start | bytes 294920 | tf_op jit(solution)/shard_map/ppermute | solution.py:109
  74.6 4.8 %collective-permute-start.12 = (bf16[96,512]{1,0:T(8,128)(2,1)S(1)}, bf16[96,512]{1,0:T(8,128)(2,1)S(1)}, u32[]{:S(2)}, u32[]{:S(2)}) collective-permute-start(bf16[96,512]{1,0:T(8,128)(2,1)S(1)} %slice.177), channel_id=1, source_target_pairs={{0,16},{8,24},{16,0},{24,8},{1,17},{9,25},{17,1},{25,9},{2,18},{10... | collective-permute-start | bytes 294920 | tf_op jit(solution)/shard_map/ppermute | solution.py:109
  76.4 5.8 %collective-permute-start.26 = (bf16[96,512]{1,0:T(8,128)(2,1)S(1)}, bf16[96,512]{1,0:T(8,128)(2,1)S(1)}, u32[]{:S(2)}, u32[]{:S(2)}) collective-permute-start(bf16[96,512]{1,0:T(8,128)(2,1)S(1)} %slice.188), channel_id=1, source_target_pairs={{0,8},{8,0},{16,24},{24,16},{1,9},{9,1},{17,25},{25,17},{2,10},{10... | collective-permute-start | bytes 294920 | tf_op jit(solution)/shard_map/ppermute | solution.py:109
  77.5 4.7 %collective-permute-start.25 = (bf16[96,512]{1,0:T(8,128)(2,1)S(1)}, bf16[96,512]{1,0:T(8,128)(2,1)S(1)}, u32[]{:S(2)}, u32[]{:S(2)}) collective-permute-start(bf16[96,512]{1,0:T(8,128)(2,1)S(1)} %slice.187), channel_id=1, source_target_pairs={{0,16},{8,24},{16,0},{24,8},{1,17},{9,25},{17,1},{25,9},{2,18},{10... | collective-permute-start | bytes 294920 | tf_op jit(solution)/shard_map/ppermute | solution.py:109
  83.3 1.6 %collective-permute-start.14 = (bf16[256,512]{1,0:T(8,128)(2,1)S(1)}, bf16[256,512]{1,0:T(8,128)(2,1)S(1)}, u32[]{:S(2)}, u32[]{:S(2)}) collective-permute-start(bf16[256,512]{1,0:T(8,128)(2,1)S(1)} %slice.248), channel_id=1, source_target_pairs={{0,1},{1,0},{2,3},{3,2},{4,5},{5,4},{6,7},{7,6},{8,9},{9,8},{10,11... | collective-permute-start | bytes 786440 | tf_op jit(solution)/shard_map/ppermute | solution.py:109
  84.0 2.0 %collective-permute-start.27 = (bf16[256,512]{1,0:T(8,128)(2,1)S(1)}, bf16[256,512]{1,0:T(8,128)(2,1)S(1)}, u32[]{:S(2)}, u32[]{:S(2)}) collective-permute-start(bf16[256,512]{1,0:T(8,128)(2,1)S(1)} %slice.247), channel_id=1, source_target_pairs={{0,1},{1,0},{2,3},{3,2},{4,5},{5,4},{6,7},{7,6},{8,9},{9,8},{10,11... | collective-permute-start | bytes 786440 | tf_op jit(solution)/shard_map/ppermute | solution.py:109
  85.0 7.3 %collective-permute-start.15 = (bf16[128,512]{1,0:T(8,128)(2,1)S(1)}, bf16[128,512]{1,0:T(8,128)(2,1)S(1)}, u32[]{:S(2)}, u32[]{:S(2)}) collective-permute-start(bf16[128,512]{1,0:T(8,128)(2,1)S(1)} %slice.249), channel_id=1, source_target_pairs={{0,2},{2,0},{4,6},{6,4},{1,3},{3,1},{5,7},{7,5},{8,10},{10,8},{12,... | collective-permute-start | bytes 393224 | tf_op jit(solution)/shard_map/ppermute | solution.py:109
  86.1 13.0 %collective-permute-start.28 = (bf16[128,512]{1,0:T(8,128)(2,1)S(1)}, bf16[128,512]{1,0:T(8,128)(2,1)S(1)}, u32[]{:S(2)}, u32[]{:S(2)}) collective-permute-start(bf16[128,512]{1,0:T(8,128)(2,1)S(1)} %get-tuple-element.38), channel_id=1, source_target_pairs={{0,4},{2,6},{4,0},{6,2},{1,5},{3,7},{5,1},{7,3},{8,12},{10,14},{12... | collective-permute-start | bytes 393224 | tf_op jit(solution)/shard_map/ppermute | solution.py:109
  88.3 10.8 %collective-permute-start.29 = (bf16[128,512]{1,0:T(8,128)(2,1)S(1)}, bf16[128,512]{1,0:T(8,128)(2,1)S(1)}, u32[]{:S(2)}, u32[]{:S(2)}) collective-permute-start(bf16[128,512]{1,0:T(8,128)(2,1)S(1)} %get-tuple-element.39), channel_id=1, source_target_pairs={{0,6},{2,4},{4,2},{6,0},{1,7},{3,5},{5,3},{7,1},{8,14},{10,12},{12... | collective-permute-start | bytes 393224 | tf_op jit(solution)/shard_map/ppermute | solution.py:109

commit v2 on v0

--- a/solution.py
+++ b/solution.py
@@ -27,7 +27,7 @@
     return lax.all_to_all(results, ("grp", "loc"), split_axis=0, concat_axis=0, tiled=True)
 
 
-def body(tokens, grad_out, expert_ids, gate_scale, gate_weight, up_weight, down_weight):
+def slot_body(tokens, grad_out, expert_ids, gate_scale, gate_weight, up_weight, down_weight):
     tok_rows, quarter = tokens.shape
     per_token = expert_ids.shape[1]
     experts = lax.axis_size(("grp", "loc"))
@@ -101,6 +101,138 @@
     return (layer_out, gate_gradient[None], up_gradient[None], down_gradient[None])
 
 
+def swap(value, axis, bit):
+    pairs = [(i, i ^ bit) for i in range(lax.axis_size(axis))]
+    return lax.ppermute(value, axis, pairs)
+
+
+def spread(value):
+    return [swap(value, "dp", j) for j in (1, 2, 3)]
+
+
+def to_core(value):
+    return swap(value, "loc", 1)
+
+
+def stack(*values):
+    return jnp.concatenate(values, axis=0)
+
+
+def beside(*values):
+    return jnp.concatenate(values, axis=1)
+
+
+def phase(*values):
+    return lax.optimization_barrier(values)
+
+
+def regroup(value, axis, place):
+    size = value.shape[axis] // 4
+    return jnp.concatenate(
+        [lax.dynamic_slice_in_dim(value, (place ^ j) * size, size, axis) for j in range(4)], axis=axis
+    )
+
+
+def activate(pre):
+    units = pre.shape[0] // 2
+    gate_pre, up_pre = pre[:units], pre[units:]
+    sig = jax.nn.sigmoid(gate_pre)
+    activated = gate_pre * sig
+    return (activated * up_pre).astype(jnp.bfloat16), up_pre * sig * (1.0 + gate_pre * (1.0 - sig)), activated
+
+
+def dense_body(tokens, grad_out, expert_ids, gate_scale, gate_weight, up_weight, down_weight):
+    rows, quarter = tokens.shape
+    experts = lax.axis_size(("grp", "loc"))
+    place = lax.axis_index("dp")
+    expert = lax.axis_index(("grp", "loc"))
+    units = gate_weight.shape[1]
+    half = units // 2
+    contract_last = (((1,), (1,)), ((), ()))
+    contract_first = (((0,), (0,)), ((), ()))
+    wide = dict(preferred_element_type=jnp.float32)
+    half_type, wide_type = jnp.bfloat16, jnp.float32
+
+    t2, t3 = swap(tokens, "grp", 2), swap(tokens, "grp", 3)
+    p0 = [tokens] + spread(tokens)
+    in_weights = stack(gate_weight[0], up_weight[0])
+    named = lax.broadcasted_iota(jnp.int32, (experts, rows, 1), 0) == expert_ids[None]
+    scales = jnp.sum(jnp.where(named, gate_scale[None], 0.0), axis=2)
+    high = lax.reduce_precision(scales, 8, 7)
+    table = stack(high, scales - high).astype(half_type)
+    table = jnp.pad(table, ((0, 0), (0, quarter - rows)))
+    payload = stack(grad_out, table)
+    far, payload, in_weights, *p0 = phase(stack(t2, t3), payload, in_weights, *p0)
+
+    p2 = [far] + spread(far)
+    p1 = swap(stack(*p0), "grp", 1)
+    p1, payload, *p2 = phase(p1, payload, *p2)
+
+    g2 = swap(payload, "grp", 2)
+    parts = [stack(p0[j], p1[j * rows : (j + 1) * rows], p2[j]) for j in range(4)]
+    parts_there = [to_core(p) for p in parts]
+    acts = []
+    for side in (parts, parts_there):
+        pre = 0.0
+        for j, part in enumerate(side):
+            w_part = lax.dynamic_slice_in_dim(in_weights, (place ^ j) * quarter, quarter, 1)
+            pre = pre + lax.dot_general(w_part, part, contract_last, **wide)
+        acts.append(activate(pre))
+    values = phase(beside(*(a[0] for a in acts)), payload, down_weight, *parts, *parts_there)
+    hidden, payload, down_weight, parts, parts_there = values[0], values[1], values[2], values[3:7], values[7:]
+
+    hx, hy = swap(hidden, "dp", 1), swap(hidden, "dp", 2)
+    last_x, last_y = swap(hy[half:], "dp", 1), swap(hx[:half], "dp", 2)
+    down_rows, payload = phase(regroup(down_weight[0], 0, place), payload)
+    g1, g3 = swap(payload, "grp", 1), swap(payload, "grp", 3)
+    blocks = jnp.stack([payload, g1, g2, g3])
+    blocks = stack(blocks, to_core(blocks))
+    table = blocks[:, rows:, :rows].astype(wide_type).reshape(8, 2, experts, rows)
+    scale = lax.dynamic_index_in_dim(table, expert, 2, keepdims=False)
+    scale = jnp.sum(scale, axis=1).reshape(8 * rows, 1)
+    grads = blocks[:, :rows].reshape(8 * rows, quarter).astype(wide_type)
+    grads = (grads * scale).astype(half_type)
+    shares = lax.dot_general(down_rows, grads, contract_last, **wide).reshape(4, units, -1)
+    sent = shares[3].astype(half_type)
+    top, bottom = swap(sent[:half], "dp", 2), swap(sent[half:], "dp", 1)
+    sums = [
+        stack(shares[1][:half] + top.astype(wide_type), shares[1][half:]).astype(half_type),
+        stack(shares[2][:half], shares[2][half:] + bottom.astype(wide_type)).astype(half_type),
+    ]
+    sums = [swap(value, "dp", j + 1) for j, value in enumerate(sums)]
+    own_share, *hidden = phase(shares[0], hidden, hx, hy, last_y, last_x)
+    hidden = stack(*hidden)
+
+    out = lax.dot_general(hidden, down_rows, contract_first, **wide).astype(half_type).astype(wide_type) * scale
+    out = out[: 4 * rows] + to_core(out[4 * rows :].astype(half_type)).astype(wide_type)
+    back = out[rows:].astype(half_type)
+    back = [swap(back[k * rows : (k + 1) * rows], "grp", k + 1) for k in (1, 0, 2)]
+    total, *sums = phase(out[:rows], *sums)
+    layer_out = total + back[0].astype(wide_type) + back[1].astype(wide_type) + back[2].astype(wide_type)
+    down_gradient = jnp.dot(hidden, grads, **wide)
+    down_gradient = regroup(down_gradient.astype(half_type), 0, place)
+
+    hidden_grad = own_share + sums[0].astype(wide_type) + sums[1].astype(wide_type)
+    both = []
+    for k in range(2):
+        side_grad = hidden_grad[:, 4 * k * rows : 4 * (k + 1) * rows]
+        both.append(stack(*((side_grad * factor).astype(half_type) for factor in acts[k][1:])))
+    in_gradient = [
+        jnp.dot(both[0], mine, **wide) + jnp.dot(both[1], other, **wide) for mine, other in zip(parts, parts_there)
+    ]
+    in_gradient = regroup(beside(*in_gradient).astype(half_type), 1, place)
+    return (layer_out.astype(half_type), in_gradient[None, :units], in_gradient[None, units:], down_gradient[None])
+
+
+def body(tokens, grad_out, expert_ids, *rest):
+    experts = lax.axis_size(("grp", "loc"))
+    rows, per_token = expert_ids.shape
+    square = lax.axis_size("dp") == 4 and lax.axis_size("grp") == 4 and lax.axis_size("loc") == 2
+    if square and 2 * rows * per_token // experts >= rows:
+        return dense_body(tokens, grad_out, expert_ids, *rest)
+    return slot_body(tokens, grad_out, expert_ids, *rest)
+
+
 def solution(mesh):
     return jax.shard_map(
         body,

time: 250 us -> 90.1 us (0.36)
  blocking collectives: 133 us -> 0 us
  starting transfers between devices: 4.69 us -> 29.7 us
  waiting for transfers between devices: 56.9 us -> 38.9 us
  matrix products: 23.9 us -> 10.1 us
  between operations: 14.2 us -> 1.2 us
  local copies, waits for them, and re-layouts: 10.9 us -> 2.11 us
    all_to_all x1 -> x0, blocking collectives: 121 us -> none  [send_rows(): lax.all_to_all(outgoing, ('grp', 'loc'), split_axis=0, concat_axis=0, til...]
    ppermute x0 -> x29, waiting for transfers between devices: none -> 38.9 us  [swap(): return lax.ppermute(value, axis, pairs)]
    ppermute x0 -> x29, starting transfers between devices: none -> 29.7 us  [swap(): return lax.ppermute(value, axis, pairs)]
    all_gather x1 -> x0, waiting for transfers between devices: 24.9 us -> none  [body(): piece = lax.all_gather(hidden, 'dp', axis=0, tiled=True)]
    all_to_all x1 -> x0, waiting for transfers between devices: 23.3 us -> none  [return_rows(): lax.all_to_all(results, ('grp', 'loc'), split_axis=0, concat_axis=0, tile...]
    dot_general x9 -> x19, matrix products: 23.9 us -> 10.1 us  [the longest x8 4.18 us: dense_body(): pre = pre + lax.dot_general(w_part, part, contract_last, **wide)]
    all_gather x1 -> x0, blocking collectives: 11.8 us -> none  [body(): full_tokens = lax.all_gather(tokens, 'dp', axis=1, tiled=True)]
    reduce_scatter x1 -> x0, waiting for transfers between devices: 8.69 us -> none  [body(): lax.psum_scatter(lax.dot_general(down_rows, flat_grads, feature_contract,...]
  transfers between devices with their start and end apart: 3 -> 29, of which waited for: 3 -> 13; matrix products, arithmetic and copies ran while one was open for 6% -> 18% of each run, Pallas kernels for 0% -> 0%
where the time goes in v2:
time: 90.1 us; the launch traced here: 89.9 us
  waiting for transfers between devices  38.9 us (43%)
  starting transfers between devices  29.7 us (33%)
  matrix products  10.1 us (11%)
  other arithmetic  7.91 us (9%)
  local copies, waits for them, and re-layouts  2.11 us (2%)
  between operations  1.2 us (1%)
    ppermute x29, waiting for transfers between devices, swap(): return lax.ppermute(value, axis, pairs)  38.9 us
    ppermute x29, starting transfers between devices, swap(): return lax.ppermute(value, axis, pairs)  29.7 us
    dot_general x8, matrix products, dense_body(): pre = pre + lax.dot_general(w_part, part, contract_last, **wide)  4.18 us
    concatenate x11, other arithmetic, stack(): return jnp.concatenate(values, axis=0)  3.53 us
  transfers between devices with their start and end apart: 29, of which 13 were waited for; matrix products, arithmetic and copies ran while one was open for 18% of the time, Pallas kernels for 0%

profile of v2, /device:TPU:0, one launch (start us, length us, event | category | flops | bytes accessed | tf_op | source)
XLA Modules:
  0.0 89.9 jit_solution(9999561998407421786)
XLA Ops:
  0.6 3.0 %collective-permute-start.3 = (bf16[128,512]{1,0:T(8,128)(2,1)}, bf16[128,512]{1,0:T(8,128)(2,1)S(1)}, u32[]{:S(2)}, u32[]{:S(2)}) collective-permute-start(bf16[128,512]{1,0:T(8,128)(2,1)} %param.7), channel_id=1, source_target_pairs={{0,16},{8,24},{16,0},{24,8},{1,17},{9,25},{17,1},{25,9},{2,18},{10... | collective-permute-start | bytes 393224 | tf_op jit(solution)/shard_map/ppermute | solution.py:106
  3.7 1.5 %collective-permute-start.2 = (bf16[128,512]{1,0:T(8,128)(2,1)}, bf16[128,512]{1,0:T(8,128)(2,1)S(1)}, u32[]{:S(2)}, u32[]{:S(2)}) collective-permute-start(bf16[128,512]{1,0:T(8,128)(2,1)} %param.7), channel_id=1, source_target_pairs={{0,8},{8,0},{16,24},{24,16},{1,9},{9,1},{17,25},{25,17},{2,10},{10... | collective-permute-start | bytes 393224 | tf_op jit(solution)/shard_map/ppermute | solution.py:106
  5.2 3.6 %collective-permute-start.1 = (bf16[128,512]{1,0:T(8,128)(2,1)}, bf16[128,512]{1,0:T(8,128)(2,1)S(1)}, u32[]{:S(2)}, u32[]{:S(2)}) collective-permute-start(bf16[128,512]{1,0:T(8,128)(2,1)} %param.7), channel_id=1, source_target_pairs={{0,6},{2,4},{4,2},{6,0},{1,7},{3,5},{5,3},{7,1},{8,14},{10,12},{12... | collective-permute-start | bytes 393224 | tf_op jit(solution)/shard_map/ppermute | solution.py:106
  8.8 0.5 collective-permute-start.4
  9.2 0.7 select_reduce_fusion
  10.0 1.5 %pad_maximum_fusion = bf16[384,2048]{1,0:T(8,128)(2,1)S(1)} fusion(bf16[192,2048]{1,0:T(8,128)(2,1)} %bitcast.50, bf16[192,2048]{1,0:T(8,128)(2,1)} %bitcast.51), kind=kLoop, calls=%fused_computation.3 | loop fusion | flops 3145728 | bytes 3145728 | tf_op jit(solution)/shard_map/concatenate | solution.py:118
  11.5 1.9 %collective-permute-done.1 = bf16[128,512]{1,0:T(8,128)(2,1)S(1)} collective-permute-done((bf16[128,512]{1,0:T(8,128)(2,1)}, bf16[128,512]{1,0:T(8,128)(2,1)S(1)}, u32[]{:S(2)}, u32[]{:S(2)}) %collective-permute-start.1) | collective-permute-done | bytes 131104 | tf_op jit(solution)/shard_map/ppermute | solution.py:106
  13.4 6.0 %collective-permute-done = bf16[128,512]{1,0:T(8,128)(2,1)S(1)} collective-permute-done((bf16[128,512]{1,0:T(8,128)(2,1)}, bf16[128,512]{1,0:T(8,128)(2,1)S(1)}, u32[]{:S(2)}, u32[]{:S(2)}) %collective-permute-start) | collective-permute-done | bytes 131104 | tf_op jit(solution)/shard_map/ppermute | solution.py:106
  19.5 0.8 fusion.9
  20.4 0.5 collective-permute-start.8
  20.9 1.5 %collective-permute-start.7 = (bf16[256,512]{1,0:T(8,128)(2,1)S(1)}, bf16[256,512]{1,0:T(8,128)(2,1)S(1)}, u32[]{:S(2)}, u32[]{:S(2)}) collective-permute-start(bf16[256,512]{1,0:T(8,128)(2,1)S(1)} %pad_maximum_fusion.15), channel_id=1, source_target_pairs={{0,16},{8,24},{16,0},{24,8},{1,17},{9,25},{17,1},{25,9},{2,18},{10... | collective-permute-start | bytes 786440 | tf_op jit(solution)/shard_map/ppermute | solution.py:106
  22.4 1.5 %collective-permute-start.6 = (bf16[256,512]{1,0:T(8,128)(2,1)S(1)}, bf16[256,512]{1,0:T(8,128)(2,1)}, u32[]{:S(2)}, u32[]{:S(2)}) collective-permute-start(bf16[256,512]{1,0:T(8,128)(2,1)S(1)} %pad_maximum_fusion.15), channel_id=1, source_target_pairs={{0,8},{8,0},{16,24},{24,16},{1,9},{9,1},{17,25},{25,17},{2,10},{10... | collective-permute-start | bytes 786440 | tf_op jit(solution)/shard_map/ppermute | solution.py:106
  23.9 6.7 %collective-permute-done.8 = bf16[256,512]{1,0:T(8,128)(2,1)S(1)} collective-permute-done((bf16[256,512]{1,0:T(8,128)(2,1)S(1)}, bf16[256,512]{1,0:T(8,128)(2,1)S(1)}, u32[]{:S(2)}, u32[]{:S(2)}) %collective-permute-start.8) | collective-permute-done | bytes 262176 | tf_op jit(solution)/shard_map/ppermute | solution.py:106
  30.5 3.0 %collective-permute-done.7 = bf16[256,512]{1,0:T(8,128)(2,1)S(1)} collective-permute-done((bf16[256,512]{1,0:T(8,128)(2,1)S(1)}, bf16[256,512]{1,0:T(8,128)(2,1)S(1)}, u32[]{:S(2)}, u32[]{:S(2)}) %collective-permute-start.7) | collective-permute-done | bytes 262176 | tf_op jit(solution)/shard_map/ppermute | solution.py:106
  33.5 1.8 %collective-permute-start.14 = (bf16[144,512]{1,0:T(8,128)(2,1)S(1)}, bf16[144,512]{1,0:T(8,128)(2,1)S(1)}, u32[]{:S(2)}, u32[]{:S(2)}) collective-permute-start(bf16[144,512]{1,0:T(8,128)(2,1)S(1)} %pad_maximum_fusion.16), channel_id=1, source_target_pairs={{0,4},{2,6},{4,0},{6,2},{1,5},{3,7},{5,1},{7,3},{8,12},{10,14},{12... | collective-permute-start | bytes 442376 | tf_op jit(solution)/shard_map/ppermute | solution.py:106
  35.3 1.0 %pad_maximum_fusion.7 = bf16[512,512]{1,0:T(8,128)(2,1)S(1)} fusion(bf16[256,512]{1,0:T(8,128)(2,1)} %collective-permute-done.6, bf16[128,512]{1,0:T(8,128)(2,1)S(1)} %get-tuple-element.108, bf16[128,512]{1,0:T(8,128)(2,1)S(1)} %collective-permute-done.2), kind=kLoop, calls=%fused_computation.35 | loop fusion | flops 1572864 | bytes 1048576 | tf_op jit(solution)/shard_map/concatenate | solution.py:118
  36.4 0.6 collective-permute-start.11
  37.1 1.4 %fusion.22 = f32[384,512]{1,0:T(8,128)S(1)} fusion(bf16[384,2048]{1,0:T(8,128)(2,1)S(1)} %pad_maximum_fusion, s32[]{:T(128)S(6)} %select_n.46, bf16[256,512]{1,0:T(8,128)(2,1)} %collective-permute-done.6, bf16[128,512]{1,0:T(8,128)(2,1)S(1)} %get-tuple-element.108, bf16[128,512]{1,0:T(8,128)(2,1)S(1)} %collective-permute-done.2), kind=kOutput, calls=%fused_computation.65 | convolution fusion | flops 202899456 | bytes 1703940 | tf_op jit(solution)/shard_map/dot_general | solution.py:179
  38.5 0.4 convolution_add_fusion.7
  38.9 0.4 convolution_add_fusion.6
  39.9 0.6 collective-permute-start.9
  42.0 0.4 fusion.2
  42.6 1.5 %collective-permute-start.18 = (bf16[192,1024]{1,0:T(8,128)(2,1)S(1)}, bf16[192,1024]{1,0:T(8,128)(2,1)S(1)}, u32[]{:S(2)}, u32[]{:S(2)}) collective-permute-start(bf16[192,1024]{1,0:T(8,128)(2,1)S(1)} %pad_maximum_fusion.10), channel_id=1, source_target_pairs={{0,16},{8,24},{16,0},{24,8},{1,17},{9,25},{17,1},{25,9},{2,18},{10... | collective-permute-start | bytes 1179656 | tf_op jit(solution)/shard_map/ppermute | solution.py:106
  44.1 0.5 collective-permute-start.17
  44.7 2.4 %collective-permute-start.15 = (bf16[144,512]{1,0:T(8,128)(2,1)S(1)}, bf16[144,512]{1,0:T(8,128)(2,1)S(1)}, u32[]{:S(2)}, u32[]{:S(2)}) collective-permute-start(bf16[144,512]{1,0:T(8,128)(2,1)S(1)} %pad_maximum_fusion.16), channel_id=1, source_target_pairs={{0,6},{2,4},{4,2},{6,0},{1,7},{3,5},{5,3},{7,1},{8,14},{10,12},{12... | collective-permute-start | bytes 442376 | tf_op jit(solution)/shard_map/ppermute | solution.py:106
  47.2 6.2 %collective-permute-done.15 = bf16[144,512]{1,0:T(8,128)(2,1)S(1)} collective-permute-done((bf16[144,512]{1,0:T(8,128)(2,1)S(1)}, bf16[144,512]{1,0:T(8,128)(2,1)S(1)}, u32[]{:S(2)}, u32[]{:S(2)}) %collective-permute-start.15) | collective-permute-done | bytes 147488 | tf_op jit(solution)/shard_map/ppermute | solution.py:106
  53.3 2.1 %collective-permute-done.13 = bf16[144,512]{1,0:T(8,128)(2,1)S(1)} collective-permute-done((bf16[144,512]{1,0:T(8,128)(2,1)S(1)}, bf16[144,512]{1,0:T(8,128)(2,1)S(1)}, u32[]{:S(2)}, u32[]{:S(2)}) %collective-permute-start.13) | collective-permute-done | bytes 147488 | tf_op jit(solution)/shard_map/ppermute | solution.py:106
  55.6 1.6 %collective-permute-start.20 = (bf16[96,1024]{1,0:T(8,128)(2,1)S(1)}, bf16[96,1024]{1,0:T(8,128)(2,1)S(1)}, u32[]{:S(2)}, u32[]{:S(2)}) collective-permute-start(bf16[96,1024]{1,0:T(8,128)(2,1)S(1)} %slice.150), channel_id=1, source_target_pairs={{0,8},{8,0},{16,24},{24,16},{1,9},{9,1},{17,25},{25,17},{2,10},{10... | collective-permute-start | bytes 589832 | tf_op jit(solution)/shard_map/ppermute | solution.py:106
  57.2 0.7 collective-permute-start.19
  58.4 1.0 %fusion.48 = (bf16[768,1024]{1,0:T(8,128)(2,1)S(1)}, f32[768,1024]{1,0:T(8,128)S(1)}) fusion(bf16[768,512]{1,0:T(8,128)(2,1)S(1)} %pad_maximum_fusion.3, bf16[1024,512]{1,0:T(8,128)(2,1)S(1)} %fusion), kind=kOutput, calls=%fused_computation.122 | convolution fusion | flops 806092800 | bytes 6553600 | tf_op jit(solution)/shard_map/dot_general | solution.py:195
  59.5 3.5 %collective-permute-done.20 = bf16[96,1024]{1,0:T(8,128)(2,1)S(1)} collective-permute-done((bf16[96,1024]{1,0:T(8,128)(2,1)S(1)}, bf16[96,1024]{1,0:T(8,128)(2,1)S(1)}, u32[]{:S(2)}, u32[]{:S(2)}) %collective-permute-start.20) | collective-permute-done | bytes 196640 | tf_op jit(solution)/shard_map/ppermute | solution.py:106
  63.0 1.3 %collective-permute-done.19 = bf16[96,1024]{1,0:T(8,128)(2,1)S(1)} collective-permute-done((bf16[96,1024]{1,0:T(8,128)(2,1)S(1)}, bf16[96,1024]{1,0:T(8,128)(2,1)S(1)}, u32[]{:S(2)}, u32[]{:S(2)}) %collective-permute-start.19) | collective-permute-done | bytes 196640 | tf_op jit(solution)/shard_map/ppermute | solution.py:106
  64.5 1.0 %convolution_convert_fusion.1 = bf16[768,512]{1,0:T(8,128)(2,1)S(1)} fusion(bf16[768,1024]{1,0:T(8,128)(2,1)S(1)} %constant_dynamic-update-slice_fusion.5, bf16[1024,512]{1,0:T(8,128)(2,1)S(1)} %fusion), kind=kOutput, calls=%fused_computation.7 | convolution fusion | flops 805699584 | bytes 3407872 | tf_op jit(solution)/shard_map/dot_general | solution.py:212
  65.4 1.0 %convert_multiply_fusion.1 = f32[1024,512]{1,0:T(8,128)S(1)} fusion(bf16[768,1024]{1,0:T(8,128)(2,1)S(1)} %constant_dynamic-update-slice_fusion.5, bf16[768,512]{1,0:T(8,128)(2,1)S(1)} %pad_maximum_fusion.3, f32[1024]{0:T(1024)S(1)} %bitcast.56), kind=kOutput, calls=%fused_computation.2 | convolution fusion | flops 806879232 | bytes 4460544 | tf_op jit(solution)/shard_map/dot_general | solution.py:206
  66.5 0.6 collective-permute-start.24
  67.1 1.3 %collective-permute-start.22 = (bf16[96,1024]{1,0:T(8,128)(2,1)S(1)}, bf16[96,1024]{1,0:T(8,128)(2,1)S(1)}, u32[]{:S(2)}, u32[]{:S(2)}) collective-permute-start(bf16[96,1024]{1,0:T(8,128)(2,1)S(1)} %get-tuple-element.91), channel_id=1, source_target_pairs={{0,16},{8,24},{16,0},{24,8},{1,17},{9,25},{17,1},{25,9},{2,18},{10... | collective-permute-start | bytes 589832 | tf_op jit(solution)/shard_map/ppermute | solution.py:106
  68.7 0.9 %maximum_bitcast_fusion = bf16[1,768,512]{2,1,0:T(8,128)(2,1)} fusion(bf16[192,512]{1,0:T(8,128)(2,1)S(1)} %get-tuple-element.93, bf16[192,512]{1,0:T(8,128)(2,1)S(1)} %get-tuple-element.94, bf16[192,512]{1,0:T(8,128)(2,1)S(1)} %get-tuple-element.95, bf16[192,512]{1,0:T(8,128)(2,1)S(1)} %get-tuple-element.92), kind=kLoop, calls=%fused_computation.27 | loop fusion | flops 3145728 | bytes 1572864 | tf_op jit(solution)/shard_map/broadcast_in_dim | solution.py:224
  69.6 3.2 %collective-permute-done.24 = bf16[96,1024]{1,0:T(8,128)(2,1)S(1)} collective-permute-done((bf16[96,1024]{1,0:T(8,128)(2,1)S(1)}, bf16[96,1024]{1,0:T(8,128)(2,1)S(1)}, u32[]{:S(2)}, u32[]{:S(2)}) %collective-permute-start.24) | collective-permute-done | bytes 196640 | tf_op jit(solution)/shard_map/ppermute | solution.py:106
  73.2 1.6 %collective-permute-start.23 = (bf16[192,1024]{1,0:T(8,128)(2,1)S(1)}, bf16[192,1024]{1,0:T(8,128)(2,1)S(1)}, u32[]{:S(2)}, u32[]{:S(2)}) collective-permute-start(bf16[192,1024]{1,0:T(8,128)(2,1)S(1)} %pad_maximum_fusion.11), channel_id=1, source_target_pairs={{0,8},{8,0},{16,24},{24,16},{1,9},{9,1},{17,25},{25,17},{2,10},{10... | collective-permute-start | bytes 1179656 | tf_op jit(solution)/shard_map/ppermute | solution.py:106
  74.8 0.7 collective-permute-start.25
  75.7 0.6 collective-permute-start.26
  76.2 2.4 %collective-permute-start.28 = (bf16[128,512]{1,0:T(8,128)(2,1)S(1)}, bf16[128,512]{1,0:T(8,128)(2,1)S(1)}, u32[]{:S(2)}, u32[]{:S(2)}) collective-permute-start(bf16[128,512]{1,0:T(8,128)(2,1)S(1)} %get-tuple-element.103), channel_id=1, source_target_pairs={{0,6},{2,4},{4,2},{6,0},{1,7},{3,5},{5,3},{7,1},{8,14},{10,12},{12... | collective-permute-start | bytes 393224 | tf_op jit(solution)/shard_map/ppermute | solution.py:106
  78.6 0.6 collective-permute-start.27
  79.2 3.2 %collective-permute-done.23 = bf16[192,1024]{1,0:T(8,128)(2,1)S(1)} collective-permute-done((bf16[192,1024]{1,0:T(8,128)(2,1)S(1)}, bf16[192,1024]{1,0:T(8,128)(2,1)S(1)}, u32[]{:S(2)}, u32[]{:S(2)}) %collective-permute-start.23) | collective-permute-done | bytes 393248 | tf_op jit(solution)/shard_map/ppermute | solution.py:106
  82.5 1.3 %collective-permute-done.25 = bf16[192,1024]{1,0:T(8,128)(2,1)S(1)} collective-permute-done((bf16[192,1024]{1,0:T(8,128)(2,1)S(1)}, bf16[192,1024]{1,0:T(8,128)(2,1)S(1)}, u32[]{:S(2)}, u32[]{:S(2)}) %collective-permute-start.25) | collective-permute-done | bytes 393248 | tf_op jit(solution)/shard_map/ppermute | solution.py:106
  83.9 0.4 multiply_convert_fusion.3
  87.9 1.3 %slice_bitcast_fusion = (bf16[1,192,2048]{2,1,0:T(8,128)(2,1)}, bf16[1,192,2048]{2,1,0:T(8,128)(2,1)}) fusion(bf16[384,2048]{1,0:T(8,128)(2,1)S(1)} %pad_maximum_fusion.2), kind=kLoop, calls=%fused_computation.24 | loop fusion | bytes 3145728 | tf_op jit(solution)/shard_map/broadcast_in_dim | solution.py:224
  89.2 0.7 add_convert_fusion
  (87 shorter events, 8.1 us)
Async XLA Ops:
  0.6 18.9 %collective-permute-start.3 = (bf16[128,512]{1,0:T(8,128)(2,1)}, bf16[128,512]{1,0:T(8,128)(2,1)S(1)}, u32[]{:S(2)}, u32[]{:S(2)}) collective-permute-start(bf16[128,512]{1,0:T(8,128)(2,1)} %param.7), channel_id=1, source_target_pairs={{0,16},{8,24},{16,0},{24,8},{1,17},{9,25},{17,1},{25,9},{2,18},{10... | collective-permute-start | bytes 393224 | tf_op jit(solution)/shard_map/ppermute | solution.py:106
  3.7 15.9 %collective-permute-start.2 = (bf16[128,512]{1,0:T(8,128)(2,1)}, bf16[128,512]{1,0:T(8,128)(2,1)S(1)}, u32[]{:S(2)}, u32[]{:S(2)}) collective-permute-start(bf16[128,512]{1,0:T(8,128)(2,1)} %param.7), channel_id=1, source_target_pairs={{0,8},{8,0},{16,24},{24,16},{1,9},{9,1},{17,25},{25,17},{2,10},{10... | collective-permute-start | bytes 393224 | tf_op jit(solution)/shard_map/ppermute | solution.py:106
  5.2 8.3 %collective-permute-start.1 = (bf16[128,512]{1,0:T(8,128)(2,1)}, bf16[128,512]{1,0:T(8,128)(2,1)S(1)}, u32[]{:S(2)}, u32[]{:S(2)}) collective-permute-start(bf16[128,512]{1,0:T(8,128)(2,1)} %param.7), channel_id=1, source_target_pairs={{0,6},{2,4},{4,2},{6,0},{1,7},{3,5},{5,3},{7,1},{8,14},{10,12},{12... | collective-permute-start | bytes 393224 | tf_op jit(solution)/shard_map/ppermute | solution.py:106
  8.8 10.7 %collective-permute-start = (bf16[128,512]{1,0:T(8,128)(2,1)}, bf16[128,512]{1,0:T(8,128)(2,1)S(1)}, u32[]{:S(2)}, u32[]{:S(2)}) collective-permute-start(bf16[128,512]{1,0:T(8,128)(2,1)} %param.7), channel_id=1, source_target_pairs={{0,4},{2,6},{4,0},{6,2},{1,5},{3,7},{5,1},{7,3},{8,12},{10,14},{12... | collective-permute-start | bytes 393224 | tf_op jit(solution)/shard_map/ppermute | solution.py:106
  8.8 10.8 %collective-permute-start.4 = (bf16[128,512]{1,0:T(8,128)(2,1)}, bf16[128,512]{1,0:T(8,128)(2,1)S(1)}, u32[]{:S(2)}, u32[]{:S(2)}) collective-permute-start(bf16[128,512]{1,0:T(8,128)(2,1)} %param.7), channel_id=1, source_target_pairs={{0,24},{8,16},{16,8},{24,0},{1,25},{9,17},{17,9},{25,1},{2,26},{10... | collective-permute-start | bytes 393224 | tf_op jit(solution)/shard_map/ppermute | solution.py:106
  10.0 1.6 %copy-start.2 = (bf16[128,512]{1,0:T(8,128)(2,1)S(1)}, bf16[128,512]{1,0:T(8,128)(2,1)}, u32[]{:S(2)}) copy-start(bf16[128,512]{1,0:T(8,128)(2,1)} %param.8) | copy-start | bytes 393220
  10.0 9.6 %copy-start = (bf16[128,512]{1,0:T(8,128)(2,1)S(1)}, bf16[128,512]{1,0:T(8,128)(2,1)}, u32[]{:S(2)}) copy-start(bf16[128,512]{1,0:T(8,128)(2,1)} %param.7) | copy-start | bytes 393220
  20.4 13.1 %collective-permute-start.5 = (bf16[512,512]{1,0:T(8,128)(2,1)}, bf16[512,512]{1,0:T(8,128)(2,1)S(1)}, u32[]{:S(2)}, u32[]{:S(2)}) collective-permute-start(bf16[512,512]{1,0:T(8,128)(2,1)} %fusion.9), channel_id=1, source_target_pairs={{0,2},{2,0},{4,6},{6,4},{1,3},{3,1},{5,7},{7,5},{8,10},{10,8},{12,... | collective-permute-start | bytes 1572872 | tf_op jit(solution)/shard_map/ppermute | solution.py:106
  20.4 10.1 %collective-permute-start.8 = (bf16[256,512]{1,0:T(8,128)(2,1)S(1)}, bf16[256,512]{1,0:T(8,128)(2,1)S(1)}, u32[]{:S(2)}, u32[]{:S(2)}) collective-permute-start(bf16[256,512]{1,0:T(8,128)(2,1)S(1)} %pad_maximum_fusion.15), channel_id=1, source_target_pairs={{0,24},{8,16},{16,8},{24,0},{1,25},{9,17},{17,9},{25,1},{2,26},{10... | collective-permute-start | bytes 786440 | tf_op jit(solution)/shard_map/ppermute | solution.py:106
  20.9 12.6 %collective-permute-start.7 = (bf16[256,512]{1,0:T(8,128)(2,1)S(1)}, bf16[256,512]{1,0:T(8,128)(2,1)S(1)}, u32[]{:S(2)}, u32[]{:S(2)}) collective-permute-start(bf16[256,512]{1,0:T(8,128)(2,1)S(1)} %pad_maximum_fusion.15), channel_id=1, source_target_pairs={{0,16},{8,24},{16,0},{24,8},{1,17},{9,25},{17,1},{25,9},{2,18},{10... | collective-permute-start | bytes 786440 | tf_op jit(solution)/shard_map/ppermute | solution.py:106
  22.4 11.1 %collective-permute-start.6 = (bf16[256,512]{1,0:T(8,128)(2,1)S(1)}, bf16[256,512]{1,0:T(8,128)(2,1)}, u32[]{:S(2)}, u32[]{:S(2)}) collective-permute-start(bf16[256,512]{1,0:T(8,128)(2,1)S(1)} %pad_maximum_fusion.15), channel_id=1, source_target_pairs={{0,8},{8,0},{16,24},{24,16},{1,9},{9,1},{17,25},{25,17},{2,10},{10... | collective-permute-start | bytes 786440 | tf_op jit(solution)/shard_map/ppermute | solution.py:106
  33.5 13.6 %collective-permute-start.14 = (bf16[144,512]{1,0:T(8,128)(2,1)S(1)}, bf16[144,512]{1,0:T(8,128)(2,1)S(1)}, u32[]{:S(2)}, u32[]{:S(2)}) collective-permute-start(bf16[144,512]{1,0:T(8,128)(2,1)S(1)} %pad_maximum_fusion.16), channel_id=1, source_target_pairs={{0,4},{2,6},{4,0},{6,2},{1,5},{3,7},{5,1},{7,3},{8,12},{10,14},{12... | collective-permute-start | bytes 442376 | tf_op jit(solution)/shard_map/ppermute | solution.py:106
  36.3 5.0 %collective-permute-start.10 = (bf16[512,512]{1,0:T(8,128)(2,1)S(1)}, bf16[512,512]{1,0:T(8,128)(2,1)S(1)}, u32[]{:S(2)}, u32[]{:S(2)}) collective-permute-start(bf16[512,512]{1,0:T(8,128)(2,1)S(1)} %pad_maximum_fusion.7), channel_id=1, source_target_pairs={{0,1},{1,0},{2,3},{3,2},{4,5},{5,4},{6,7},{7,6},{8,9},{9,8},{10,11... | collective-permute-start | bytes 1572872 | tf_op jit(solution)/shard_map/ppermute | solution.py:106
  36.4 4.4 %collective-permute-start.11 = (bf16[512,512]{1,0:T(8,128)(2,1)S(1)}, bf16[512,512]{1,0:T(8,128)(2,1)S(1)}, u32[]{:S(2)}, u32[]{:S(2)}) collective-permute-start(bf16[512,512]{1,0:T(8,128)(2,1)S(1)} %pad_maximum_fusion.8), channel_id=1, source_target_pairs={{0,1},{1,0},{2,3},{3,2},{4,5},{5,4},{6,7},{7,6},{8,9},{9,8},{10,11... | collective-permute-start | bytes 1572872 | tf_op jit(solution)/shard_map/ppermute | solution.py:106
  37.0 3.4 %collective-permute-start.12 = (bf16[512,512]{1,0:T(8,128)(2,1)S(1)}, bf16[512,512]{1,0:T(8,128)(2,1)S(1)}, u32[]{:S(2)}, u32[]{:S(2)}) collective-permute-start(bf16[512,512]{1,0:T(8,128)(2,1)S(1)} %pad_maximum_fusion.9), channel_id=1, source_target_pairs={{0,1},{1,0},{2,3},{3,2},{4,5},{5,4},{6,7},{7,6},{8,9},{9,8},{10,11... | collective-permute-start | bytes 1572872 | tf_op jit(solution)/shard_map/ppermute | solution.py:106
  39.9 2.1 %collective-permute-start.9 = (bf16[512,512]{1,0:T(8,128)(2,1)S(1)}, bf16[512,512]{1,0:T(8,128)(2,1)S(1)}, u32[]{:S(2)}, u32[]{:S(2)}) collective-permute-start(bf16[512,512]{1,0:T(8,128)(2,1)S(1)} %fusion.7), channel_id=1, source_target_pairs={{0,1},{1,0},{2,3},{3,2},{4,5},{5,4},{6,7},{7,6},{8,9},{9,8},{10,11... | collective-permute-start | bytes 1572872 | tf_op jit(solution)/shard_map/ppermute | solution.py:106
  42.4 2.2 %copy-start.1 = (bf16[1,768,512]{2,1,0:T(8,128)(2,1)S(1)}, bf16[1,768,512]{2,1,0:T(8,128)(2,1)}, u32[]{:S(2)}) copy-start(bf16[1,768,512]{2,1,0:T(8,128)(2,1)} %param.13) | copy-start | bytes 2359300
  42.6 13.0 %collective-permute-start.18 = (bf16[192,1024]{1,0:T(8,128)(2,1)S(1)}, bf16[192,1024]{1,0:T(8,128)(2,1)S(1)}, u32[]{:S(2)}, u32[]{:S(2)}) collective-permute-start(bf16[192,1024]{1,0:T(8,128)(2,1)S(1)} %pad_maximum_fusion.10), channel_id=1, source_target_pairs={{0,16},{8,24},{16,0},{24,8},{1,17},{9,25},{17,1},{25,9},{2,18},{10... | collective-permute-start | bytes 1179656 | tf_op jit(solution)/shard_map/ppermute | solution.py:106
  44.1 13.1 %collective-permute-start.17 = (bf16[192,1024]{1,0:T(8,128)(2,1)S(1)}, bf16[192,1024]{1,0:T(8,128)(2,1)S(1)}, u32[]{:S(2)}, u32[]{:S(2)}) collective-permute-start(bf16[192,1024]{1,0:T(8,128)(2,1)S(1)} %pad_maximum_fusion.10), channel_id=1, source_target_pairs={{0,8},{8,0},{16,24},{24,16},{1,9},{9,1},{17,25},{25,17},{2,10},{10... | collective-permute-start | bytes 1179656 | tf_op jit(solution)/shard_map/ppermute | solution.py:106
  44.7 8.6 %collective-permute-start.15 = (bf16[144,512]{1,0:T(8,128)(2,1)S(1)}, bf16[144,512]{1,0:T(8,128)(2,1)S(1)}, u32[]{:S(2)}, u32[]{:S(2)}) collective-permute-start(bf16[144,512]{1,0:T(8,128)(2,1)S(1)} %pad_maximum_fusion.16), channel_id=1, source_target_pairs={{0,6},{2,4},{4,2},{6,0},{1,7},{3,5},{5,3},{7,1},{8,14},{10,12},{12... | collective-permute-start | bytes 442376 | tf_op jit(solution)/shard_map/ppermute | solution.py:106
  47.1 8.3 %collective-permute-start.13 = (bf16[144,512]{1,0:T(8,128)(2,1)S(1)}, bf16[144,512]{1,0:T(8,128)(2,1)S(1)}, u32[]{:S(2)}, u32[]{:S(2)}) collective-permute-start(bf16[144,512]{1,0:T(8,128)(2,1)S(1)} %pad_maximum_fusion.16), channel_id=1, source_target_pairs={{0,2},{2,0},{4,6},{6,4},{1,3},{3,1},{5,7},{7,5},{8,10},{10,8},{12,... | collective-permute-start | bytes 442376 | tf_op jit(solution)/shard_map/ppermute | solution.py:106
  55.5 2.4 %collective-permute-start.16 = (bf16[4,144,512]{2,1,0:T(8,128)(2,1)S(1)}, bf16[4,144,512]{2,1,0:T(8,128)(2,1)S(1)}, u32[]{:S(2)}, u32[]{:S(2)}) collective-permute-start(bf16[4,144,512]{2,1,0:T(8,128)(2,1)S(1)} %pad_maximum_fusion.6), channel_id=1, source_target_pairs={{0,1},{1,0},{2,3},{3,2},{4,5},{5,4},{6,7},{7,6},{8,9},{9,8},{10,11... | collective-permute-start | bytes 1769480 | tf_op jit(solution)/shard_map/ppermute | solution.py:106
  55.6 7.4 %collective-permute-start.20 = (bf16[96,1024]{1,0:T(8,128)(2,1)S(1)}, bf16[96,1024]{1,0:T(8,128)(2,1)S(1)}, u32[]{:S(2)}, u32[]{:S(2)}) collective-permute-start(bf16[96,1024]{1,0:T(8,128)(2,1)S(1)} %slice.150), channel_id=1, source_target_pairs={{0,8},{8,0},{16,24},{24,16},{1,9},{9,1},{17,25},{25,17},{2,10},{10... | collective-permute-start | bytes 589832 | tf_op jit(solution)/shard_map/ppermute | solution.py:106
  57.2 7.1 %collective-permute-start.19 = (bf16[96,1024]{1,0:T(8,128)(2,1)S(1)}, bf16[96,1024]{1,0:T(8,128)(2,1)S(1)}, u32[]{:S(2)}, u32[]{:S(2)}) collective-permute-start(bf16[96,1024]{1,0:T(8,128)(2,1)S(1)} %slice.149), channel_id=1, source_target_pairs={{0,16},{8,24},{16,0},{24,8},{1,17},{9,25},{17,1},{25,9},{2,18},{10... | collective-permute-start | bytes 589832 | tf_op jit(solution)/shard_map/ppermute | solution.py:106
  66.5 6.3 %collective-permute-start.24 = (bf16[96,1024]{1,0:T(8,128)(2,1)S(1)}, bf16[96,1024]{1,0:T(8,128)(2,1)S(1)}, u32[]{:S(2)}, u32[]{:S(2)}) collective-permute-start(bf16[96,1024]{1,0:T(8,128)(2,1)S(1)} %get-tuple-element.89), channel_id=1, source_target_pairs={{0,8},{8,0},{16,24},{24,16},{1,9},{9,1},{17,25},{25,17},{2,10},{10... | collective-permute-start | bytes 589832 | tf_op jit(solution)/shard_map/ppermute | solution.py:106
  67.1 5.9 %collective-permute-start.22 = (bf16[96,1024]{1,0:T(8,128)(2,1)S(1)}, bf16[96,1024]{1,0:T(8,128)(2,1)S(1)}, u32[]{:S(2)}, u32[]{:S(2)}) collective-permute-start(bf16[96,1024]{1,0:T(8,128)(2,1)S(1)} %get-tuple-element.91), channel_id=1, source_target_pairs={{0,16},{8,24},{16,0},{24,8},{1,17},{9,25},{17,1},{25,9},{2,18},{10... | collective-permute-start | bytes 589832 | tf_op jit(solution)/shard_map/ppermute | solution.py:106
  68.6 6.9 %collective-permute-start.21 = (bf16[512,512]{1,0:T(8,128)(2,1)S(1)}, bf16[512,512]{1,0:T(8,128)(2,1)S(1)}, u32[]{:S(2)}, u32[]{:S(2)}) collective-permute-start(bf16[512,512]{1,0:T(8,128)(2,1)S(1)} %slice.198), channel_id=1, source_target_pairs={{0,1},{1,0},{2,3},{3,2},{4,5},{5,4},{6,7},{7,6},{8,9},{9,8},{10,11... | collective-permute-start | bytes 1572872 | tf_op jit(solution)/shard_map/ppermute | solution.py:106
  73.2 9.3 %collective-permute-start.23 = (bf16[192,1024]{1,0:T(8,128)(2,1)S(1)}, bf16[192,1024]{1,0:T(8,128)(2,1)S(1)}, u32[]{:S(2)}, u32[]{:S(2)}) collective-permute-start(bf16[192,1024]{1,0:T(8,128)(2,1)S(1)} %pad_maximum_fusion.11), channel_id=1, source_target_pairs={{0,8},{8,0},{16,24},{24,16},{1,9},{9,1},{17,25},{25,17},{2,10},{10... | collective-permute-start | bytes 1179656 | tf_op jit(solution)/shard_map/ppermute | solution.py:106
  74.8 9.0 %collective-permute-start.25 = (bf16[192,1024]{1,0:T(8,128)(2,1)S(1)}, bf16[192,1024]{1,0:T(8,128)(2,1)S(1)}, u32[]{:S(2)}, u32[]{:S(2)}) collective-permute-start(bf16[192,1024]{1,0:T(8,128)(2,1)S(1)} %pad_maximum_fusion.12), channel_id=1, source_target_pairs={{0,16},{8,24},{16,0},{24,8},{1,17},{9,25},{17,1},{25,9},{2,18},{10... | collective-permute-start | bytes 1179656 | tf_op jit(solution)/shard_map/ppermute | solution.py:106
  75.7 13.5 %collective-permute-start.26 = (bf16[128,512]{1,0:T(8,128)(2,1)S(1)}, bf16[128,512]{1,0:T(8,128)(2,1)S(1)}, u32[]{:S(2)}, u32[]{:S(2)}) collective-permute-start(bf16[128,512]{1,0:T(8,128)(2,1)S(1)} %get-tuple-element.102), channel_id=1, source_target_pairs={{0,4},{2,6},{4,0},{6,2},{1,5},{3,7},{5,1},{7,3},{8,12},{10,14},{12... | collective-permute-start | bytes 393224 | tf_op jit(solution)/shard_map/ppermute | solution.py:106
  76.2 13.0 %collective-permute-start.28 = (bf16[128,512]{1,0:T(8,128)(2,1)S(1)}, bf16[128,512]{1,0:T(8,128)(2,1)S(1)}, u32[]{:S(2)}, u32[]{:S(2)}) collective-permute-start(bf16[128,512]{1,0:T(8,128)(2,1)S(1)} %get-tuple-element.103), channel_id=1, source_target_pairs={{0,6},{2,4},{4,2},{6,0},{1,7},{3,5},{5,3},{7,1},{8,14},{10,12},{12... | collective-permute-start | bytes 393224 | tf_op jit(solution)/shard_map/ppermute | solution.py:106
  78.6 10.6 %collective-permute-start.27 = (bf16[128,512]{1,0:T(8,128)(2,1)S(1)}, bf16[128,512]{1,0:T(8,128)(2,1)S(1)}, u32[]{:S(2)}, u32[]{:S(2)}) collective-permute-start(bf16[128,512]{1,0:T(8,128)(2,1)S(1)} %get-tuple-element.104), channel_id=1, source_target_pairs={{0,2},{2,0},{4,6},{6,4},{1,3},{3,1},{5,7},{7,5},{8,10},{10,8},{12,... | collective-permute-start | bytes 393224 | tf_op jit(solution)/shard_map/ppermute | solution.py:106

commit v3 on v2

--- a/solution.py
+++ b/solution.py
@@ -1,6 +1,8 @@
 import jax
 import jax.numpy as jnp
 from jax import lax
+from jax.experimental import pallas as pl
+from jax.experimental.pallas import tpu as pltpu
 from jax.sharding import PartitionSpec as P
 
 
@@ -141,6 +143,34 @@
     return (activated * up_pre).astype(jnp.bfloat16), up_pre * sig * (1.0 + gate_pre * (1.0 - sig)), activated
 
 
+def in_gradients(place, own_share, sums, factors, parts, parts_there):
+    units, width = factors[0].shape
+    quarter = parts[0].shape[1]
+
+    def kernel(place_ref, share_ref, x_ref, y_ref, *refs):
+        factor_refs, part_refs, (gate_ref, up_ref) = refs[:4], refs[4:12], refs[12:]
+        total = share_ref[...] + x_ref[...].astype(jnp.float32) + y_ref[...].astype(jnp.float32)
+        sides = []
+        for k in range(2):
+            side = total[:, k * width : (k + 1) * width]
+            sides.append([(side * factor_refs[2 * k + i][...]).astype(jnp.bfloat16) for i in range(2)])
+        for j in range(4):
+            columns = pl.ds(pl.multiple_of((place_ref[0] ^ j) * quarter, quarter), quarter)
+            for i, out_ref in enumerate((gate_ref, up_ref)):
+                value = jnp.dot(sides[0][i], part_refs[j][...], preferred_element_type=jnp.float32)
+                value += jnp.dot(sides[1][i], part_refs[4 + j][...], preferred_element_type=jnp.float32)
+                out_ref[:, columns] = value.astype(jnp.bfloat16)
+
+    vmem = pl.BlockSpec(memory_space=pltpu.VMEM)
+    return pl.pallas_call(
+        kernel,
+        out_shape=[jax.ShapeDtypeStruct((units, 4 * quarter), jnp.bfloat16)] * 2,
+        in_specs=[pl.BlockSpec(memory_space=pltpu.SMEM)] + [vmem] * 15,
+        out_specs=[vmem] * 2,
+        compiler_params=pltpu.CompilerParams(vmem_limit_bytes=20 * 2**20),
+    )(place, own_share, *sums, *factors, *parts, *parts_there)
+
+
 def dense_body(tokens, grad_out, expert_ids, gate_scale, gate_weight, up_weight, down_weight):
     rows, quarter = tokens.shape
     experts = lax.axis_size(("grp", "loc"))
@@ -162,11 +192,11 @@
     table = stack(high, scales - high).astype(half_type)
     table = jnp.pad(table, ((0, 0), (0, quarter - rows)))
     payload = stack(grad_out, table)
-    far, payload, in_weights, *p0 = phase(stack(t2, t3), payload, in_weights, *p0)
-
+    own, far, payload, in_weights, *p0 = phase(stack(*p0), stack(t2, t3), payload, in_weights, *p0)
+
+    p1 = swap(own, "grp", 1)
     p2 = [far] + spread(far)
-    p1 = swap(stack(*p0), "grp", 1)
-    p1, payload, *p2 = phase(p1, payload, *p2)
+    *p2, payload, p1 = phase(*p2, payload, p1)
 
     g2 = swap(payload, "grp", 2)
     parts = [stack(p0[j], p1[j * rows : (j + 1) * rows], p2[j]) for j in range(4)]
@@ -182,10 +212,11 @@
     hidden, payload, down_weight, parts, parts_there = values[0], values[1], values[2], values[3:7], values[7:]
 
     hx, hy = swap(hidden, "dp", 1), swap(hidden, "dp", 2)
-    last_x, last_y = swap(hy[half:], "dp", 1), swap(hx[:half], "dp", 2)
     down_rows, payload = phase(regroup(down_weight[0], 0, place), payload)
     g1, g3 = swap(payload, "grp", 1), swap(payload, "grp", 3)
+    hx, hy, g1, g3 = phase(hx, hy, g1, g3)
     blocks = jnp.stack([payload, g1, g2, g3])
+    last_x, last_y = swap(hy[half:], "dp", 1), swap(hx[:half], "dp", 2)
     blocks = stack(blocks, to_core(blocks))
     table = blocks[:, rows:, :rows].astype(wide_type).reshape(8, 2, experts, rows)
     scale = lax.dynamic_index_in_dim(table, expert, 2, keepdims=False)
@@ -203,8 +234,14 @@
     own_share, *hidden = phase(shares[0], hidden, hx, hy, last_y, last_x)
     hidden = stack(*hidden)
 
-    out = lax.dot_general(hidden, down_rows, contract_first, **wide).astype(half_type).astype(wide_type) * scale
-    out = out[: 4 * rows] + to_core(out[4 * rows :].astype(half_type)).astype(wide_type)
+    out = [
+        lax.dot_general(hidden[:, k * 4 * rows : (k + 1) * 4 * rows], down_rows, contract_first, **wide)
+        .astype(half_type)
+        .astype(wide_type)
+        * scale[k * 4 * rows : (k + 1) * 4 * rows]
+        for k in range(2)
+    ]
+    out, hidden, grads = phase(out[0] + to_core(out[1].astype(half_type)).astype(wide_type), hidden, grads)
     back = out[rows:].astype(half_type)
     back = [swap(back[k * rows : (k + 1) * rows], "grp", k + 1) for k in (1, 0, 2)]
     total, *sums = phase(out[:rows], *sums)
@@ -212,16 +249,11 @@
     down_gradient = jnp.dot(hidden, grads, **wide)
     down_gradient = regroup(down_gradient.astype(half_type), 0, place)
 
-    hidden_grad = own_share + sums[0].astype(wide_type) + sums[1].astype(wide_type)
-    both = []
-    for k in range(2):
-        side_grad = hidden_grad[:, 4 * k * rows : 4 * (k + 1) * rows]
-        both.append(stack(*((side_grad * factor).astype(half_type) for factor in acts[k][1:])))
-    in_gradient = [
-        jnp.dot(both[0], mine, **wide) + jnp.dot(both[1], other, **wide) for mine, other in zip(parts, parts_there)
-    ]
-    in_gradient = regroup(beside(*in_gradient).astype(half_type), 1, place)
-    return (layer_out.astype(half_type), in_gradient[None, :units], in_gradient[None, units:], down_gradient[None])
+    factors = [f for a in acts for f in a[1:]]
+    gate_gradient, up_gradient = in_gradients(
+        place.reshape(1).astype(jnp.int32), own_share, sums, factors, parts, parts_there
+    )
+    return (layer_out.astype(half_type), gate_gradient[None], up_gradient[None], down_gradient[None])
 
 
 def body(tokens, grad_out, expert_ids, *rest):

time: 90.1 us -> 84.6 us (0.939)
  waiting for transfers between devices: 38.9 us -> 32.5 us
  starting transfers between devices: 29.7 us -> 32.8 us
  Pallas kernels: 0 us -> 2.85 us
  matrix products: 10.1 us -> 7.45 us
  local copies, waits for them, and re-layouts: 2.11 us -> 0.65 us
  other arithmetic: 7.91 us -> 6.98 us
    ppermute x29, waiting for transfers between devices: 38.9 us -> 32.5 us  [swap(): return lax.ppermute(value, axis, pairs)]
    ppermute x29, starting transfers between devices: 29.7 us -> 32.8 us  [swap(): return lax.ppermute(value, axis, pairs)]
    pallas_call x0 -> x1, Pallas kernels: none -> 2.85 us  [in_gradients(): pl.pallas_call(kernel, out_shape=[jax.ShapeDtypeStruct((units, 4 * quarte...]
    dot_general x9 -> x2, matrix products: 3.93 us -> 1.24 us  [dense_body(): lax.dot_general(hidden[:, k * 4 * rows:(k + 1) * 4 * rows], down_rows, co...]
    broadcast_in_dim x1 -> x0, local copies, waits for them, and re-layouts: 1.25 us -> none  [dense_body(): in_gradient[None, units:]]
  transfers between devices with their start and end apart: 29 -> 29, of which waited for: 13 -> 15; matrix products, arithmetic and copies ran while one was open for 18% -> 16% of each run, Pallas kernels for 0% -> 3%
where the time goes in v3:
time: 84.6 us; the launch traced here: 84.4 us
  starting transfers between devices  32.8 us (39%)
  waiting for transfers between devices  32.5 us (38%)
  matrix products  7.45 us (9%)
  other arithmetic  6.98 us (8%)
  Pallas kernels  2.85 us (3%)
  between operations  1.15 us (1%)
    ppermute x29, starting transfers between devices, swap(): return lax.ppermute(value, axis, pairs)  32.8 us
    ppermute x29, waiting for transfers between devices, swap(): return lax.ppermute(value, axis, pairs)  32.5 us
    dot_general x8, matrix products, dense_body(): pre = pre + lax.dot_general(w_part, part, contract_last, **wide)  4.22 us
    concatenate x11, other arithmetic, stack(): return jnp.concatenate(values, axis=0)  3.53 us
    pallas_call x1, Pallas kernels, in_gradients(): pl.pallas_call(kernel, out_shape=[jax.ShapeDtypeStruct((units, 4 * quarte...  2.85 us
  transfers between devices with their start and end apart: 29, of which 15 were waited for; matrix products, arithmetic and copies ran while one was open for 16% of the time, Pallas kernels for 3%

profile of v3, /device:TPU:0, one launch (start us, length us, event | category | flops | bytes accessed | tf_op | source)
XLA Modules:
  0.0 84.4 jit_solution(17018510749059703362)
XLA Ops:
  0.6 4.1 %collective-permute-start.3 = (bf16[128,512]{1,0:T(8,128)(2,1)}, bf16[128,512]{1,0:T(8,128)(2,1)S(1)}, u32[]{:S(2)}, u32[]{:S(2)}) collective-permute-start(bf16[128,512]{1,0:T(8,128)(2,1)} %param.7), channel_id=1, source_target_pairs={{0,4},{2,6},{4,0},{6,2},{1,5},{3,7},{5,1},{7,3},{8,12},{10,14},{12... | collective-permute-start | bytes 393224 | tf_op jit(solution)/shard_map/ppermute | solution.py:108
  4.7 2.4 %collective-permute-start.2 = (bf16[128,512]{1,0:T(8,128)(2,1)}, bf16[128,512]{1,0:T(8,128)(2,1)S(1)}, u32[]{:S(2)}, u32[]{:S(2)}) collective-permute-start(bf16[128,512]{1,0:T(8,128)(2,1)} %param.7), channel_id=1, source_target_pairs={{0,24},{8,16},{16,8},{24,0},{1,25},{9,17},{17,9},{25,1},{2,26},{10... | collective-permute-start | bytes 393224 | tf_op jit(solution)/shard_map/ppermute | solution.py:108
  7.2 0.5 collective-permute-start.1
  7.7 0.5 collective-permute-start
  8.2 1.3 %collective-permute-start.4 = (bf16[128,512]{1,0:T(8,128)(2,1)}, bf16[128,512]{1,0:T(8,128)(2,1)S(1)}, u32[]{:S(2)}, u32[]{:S(2)}) collective-permute-start(bf16[128,512]{1,0:T(8,128)(2,1)} %param.7), channel_id=1, source_target_pairs={{0,6},{2,4},{4,2},{6,0},{1,7},{3,5},{5,3},{7,1},{8,14},{10,12},{12... | collective-permute-start | bytes 393224 | tf_op jit(solution)/shard_map/ppermute | solution.py:108
  9.6 0.7 select_reduce_fusion
  10.3 1.5 %pad_maximum_fusion = bf16[384,2048]{1,0:T(8,128)(2,1)S(1)} fusion(bf16[192,2048]{1,0:T(8,128)(2,1)} %bitcast.45, bf16[192,2048]{1,0:T(8,128)(2,1)} %bitcast.46), kind=kLoop, calls=%fused_computation.2 | loop fusion | flops 3145728 | bytes 3145728 | tf_op jit(solution)/shard_map/concatenate | solution.py:120
  11.9 1.2 %collective-permute-done.3 = bf16[128,512]{1,0:T(8,128)(2,1)S(1)} collective-permute-done((bf16[128,512]{1,0:T(8,128)(2,1)}, bf16[128,512]{1,0:T(8,128)(2,1)S(1)}, u32[]{:S(2)}, u32[]{:S(2)}) %collective-permute-start.3) | collective-permute-done | bytes 131104 | tf_op jit(solution)/shard_map/ppermute | solution.py:108
  13.1 2.2 %collective-permute-done.4 = bf16[128,512]{1,0:T(8,128)(2,1)S(1)} collective-permute-done((bf16[128,512]{1,0:T(8,128)(2,1)}, bf16[128,512]{1,0:T(8,128)(2,1)S(1)}, u32[]{:S(2)}, u32[]{:S(2)}) %collective-permute-start.4) | collective-permute-done | bytes 131104 | tf_op jit(solution)/shard_map/ppermute | solution.py:108
  15.4 0.8 pad_maximum_fusion.3
  16.2 2.4 %collective-permute-start.8 = (bf16[512,512]{1,0:T(8,128)(2,1)}, bf16[512,512]{1,0:T(8,128)(2,1)S(1)}, u32[]{:S(2)}, u32[]{:S(2)}) collective-permute-start(bf16[512,512]{1,0:T(8,128)(2,1)} %pad_maximum_fusion.3), channel_id=1, source_target_pairs={{0,2},{2,0},{4,6},{6,4},{1,3},{3,1},{5,7},{7,5},{8,10},{10,8},{12,... | collective-permute-start | bytes 1572872 | tf_op jit(solution)/shard_map/ppermute | solution.py:108
  18.6 2.4 %collective-permute-start.7 = (bf16[256,512]{1,0:T(8,128)(2,1)S(1)}, bf16[256,512]{1,0:T(8,128)(2,1)S(1)}, u32[]{:S(2)}, u32[]{:S(2)}) collective-permute-start(bf16[256,512]{1,0:T(8,128)(2,1)S(1)} %pad_maximum_fusion.11), channel_id=1, source_target_pairs={{0,24},{8,16},{16,8},{24,0},{1,25},{9,17},{17,9},{25,1},{2,26},{10... | collective-permute-start | bytes 786440 | tf_op jit(solution)/shard_map/ppermute | solution.py:108
  21.0 0.5 collective-permute-start.6
  21.5 0.5 collective-permute-start.5
  22.1 6.7 %collective-permute-done.7 = bf16[256,512]{1,0:T(8,128)(2,1)S(1)} collective-permute-done((bf16[256,512]{1,0:T(8,128)(2,1)S(1)}, bf16[256,512]{1,0:T(8,128)(2,1)S(1)}, u32[]{:S(2)}, u32[]{:S(2)}) %collective-permute-start.7) | collective-permute-done | bytes 262176 | tf_op jit(solution)/shard_map/ppermute | solution.py:108
  28.7 4.3 %collective-permute-done.6 = bf16[256,512]{1,0:T(8,128)(2,1)S(1)} collective-permute-done((bf16[256,512]{1,0:T(8,128)(2,1)S(1)}, bf16[256,512]{1,0:T(8,128)(2,1)S(1)}, u32[]{:S(2)}, u32[]{:S(2)}) %collective-permute-start.6) | collective-permute-done | bytes 262176 | tf_op jit(solution)/shard_map/ppermute | solution.py:108
  33.3 2.2 %collective-permute-start.17 = (bf16[144,512]{1,0:T(8,128)(2,1)S(1)}, bf16[144,512]{1,0:T(8,128)(2,1)S(1)}, u32[]{:S(2)}, u32[]{:S(2)}) collective-permute-start(bf16[144,512]{1,0:T(8,128)(2,1)S(1)} %pad_maximum_fusion.12), channel_id=1, source_target_pairs={{0,4},{2,6},{4,0},{6,2},{1,5},{3,7},{5,1},{7,3},{8,12},{10,14},{12... | collective-permute-start | bytes 442376 | tf_op jit(solution)/shard_map/ppermute | solution.py:108
  35.5 1.0 %pad_maximum_fusion.5.refs_5_ = bf16[512,512]{1,0:T(8,128)(2,1)S(1)} fusion(bf16[256,512]{1,0:T(8,128)(2,1)} %collective-permute-done.5, bf16[128,512]{1,0:T(8,128)(2,1)S(1)} %get-tuple-element.120, bf16[128,512]{1,0:T(8,128)(2,1)S(1)} %collective-permute-done), kind=kLoop, calls=%fused_computation.25 | loop fusion | flops 1572864 | bytes 1048576 | tf_op jit(solution)/shard_map/concatenate | solution.py:120
  36.6 0.6 collective-permute-start.11
  37.3 1.3 %fusion.24 = f32[384,512]{1,0:T(8,128)S(1)} fusion(bf16[384,2048]{1,0:T(8,128)(2,1)S(1)} %pad_maximum_fusion, s32[]{:T(128)S(6)} %select_n.42, bf16[256,512]{1,0:T(8,128)(2,1)} %collective-permute-done.5, bf16[128,512]{1,0:T(8,128)(2,1)S(1)} %get-tuple-element.120, bf16[128,512]{1,0:T(8,128)(2,1)S(1)} %collective-permute-done), kind=kOutput, calls=%fused_computation.51 | convolution fusion | flops 202899456 | bytes 1703940 | tf_op jit(solution)/shard_map/dot_general | solution.py:209
  40.1 0.6 collective-permute-start.9
  42.9 1.4 %collective-permute-start.14 = (bf16[192,1024]{1,0:T(8,128)(2,1)S(1)}, bf16[192,1024]{1,0:T(8,128)(2,1)S(1)}, u32[]{:S(2)}, u32[]{:S(2)}) collective-permute-start(bf16[192,1024]{1,0:T(8,128)(2,1)S(1)} %pad_maximum_fusion.8), channel_id=1, source_target_pairs={{0,16},{8,24},{16,0},{24,8},{1,17},{9,25},{17,1},{25,9},{2,18},{10... | collective-permute-start | bytes 1179656 | tf_op jit(solution)/shard_map/ppermute | solution.py:108
  44.3 0.8 collective-permute-start.13
  45.2 1.3 %collective-permute-start.16 = (bf16[144,512]{1,0:T(8,128)(2,1)S(1)}, bf16[144,512]{1,0:T(8,128)(2,1)S(1)}, u32[]{:S(2)}, u32[]{:S(2)}) collective-permute-start(bf16[144,512]{1,0:T(8,128)(2,1)S(1)} %pad_maximum_fusion.12), channel_id=1, source_target_pairs={{0,6},{2,4},{4,2},{6,0},{1,7},{3,5},{5,3},{7,1},{8,14},{10,12},{12... | collective-permute-start | bytes 442376 | tf_op jit(solution)/shard_map/ppermute | solution.py:108
  46.5 0.6 collective-permute-start.15
  47.1 6.7 %collective-permute-done.16 = bf16[144,512]{1,0:T(8,128)(2,1)S(1)} collective-permute-done((bf16[144,512]{1,0:T(8,128)(2,1)S(1)}, bf16[144,512]{1,0:T(8,128)(2,1)S(1)}, u32[]{:S(2)}, u32[]{:S(2)}) %collective-permute-start.16) | collective-permute-done | bytes 147488 | tf_op jit(solution)/shard_map/ppermute | solution.py:108
  53.8 1.1 %collective-permute-done.15 = bf16[144,512]{1,0:T(8,128)(2,1)S(1)} collective-permute-done((bf16[144,512]{1,0:T(8,128)(2,1)S(1)}, bf16[144,512]{1,0:T(8,128)(2,1)S(1)}, u32[]{:S(2)}, u32[]{:S(2)}) %collective-permute-start.15) | collective-permute-done | bytes 147488 | tf_op jit(solution)/shard_map/ppermute | solution.py:108
  54.9 0.5 collective-permute-done.13
  55.4 0.9 %collective-permute-start.20 = (bf16[96,1024]{1,0:T(8,128)(2,1)S(1)}, bf16[96,1024]{1,0:T(8,128)(2,1)S(1)}, u32[]{:S(2)}, u32[]{:S(2)}) collective-permute-start(bf16[96,1024]{1,0:T(8,128)(2,1)S(1)} %slice.120), channel_id=1, source_target_pairs={{0,8},{8,0},{16,24},{24,16},{1,9},{9,1},{17,25},{25,17},{2,10},{10... | collective-permute-start | bytes 589832 | tf_op jit(solution)/shard_map/ppermute | solution.py:108
  56.3 1.4 %collective-permute-start.19 = (bf16[96,1024]{1,0:T(8,128)(2,1)S(1)}, bf16[96,1024]{1,0:T(8,128)(2,1)S(1)}, u32[]{:S(2)}, u32[]{:S(2)}) collective-permute-start(bf16[96,1024]{1,0:T(8,128)(2,1)S(1)} %slice.119), channel_id=1, source_target_pairs={{0,16},{8,24},{16,0},{24,8},{1,17},{9,25},{17,1},{25,9},{2,18},{10... | collective-permute-start | bytes 589832 | tf_op jit(solution)/shard_map/ppermute | solution.py:108
  57.9 1.9 %collective-permute-done.18 = bf16[4,144,512]{2,1,0:T(8,128)(2,1)S(1)} collective-permute-done((bf16[4,144,512]{2,1,0:T(8,128)(2,1)S(1)}, bf16[4,144,512]{2,1,0:T(8,128)(2,1)S(1)}, u32[]{:S(2)}, u32[]{:S(2)}) %collective-permute-start.18) | collective-permute-done | bytes 589856 | tf_op jit(solution)/shard_map/ppermute | solution.py:108
  60.4 1.0 %fusion.44 = (bf16[768,1024]{1,0:T(8,128)(2,1)S(1)}, f32[768,1024]{1,0:T(8,128)S(1)}) fusion(bf16[768,512]{1,0:T(8,128)(2,1)S(1)} %pad_maximum_fusion.1, bf16[1024,512]{1,0:T(8,128)(2,1)S(1)} %fusion), kind=kOutput, calls=%fused_computation.101 | convolution fusion | flops 806092800 | bytes 6553600 | tf_op jit(solution)/shard_map/dot_general | solution.py:226
  61.4 0.8 collective-permute-start.24
  62.2 1.1 %collective-permute-start.22 = (bf16[96,1024]{1,0:T(8,128)(2,1)S(1)}, bf16[96,1024]{1,0:T(8,128)(2,1)S(1)}, u32[]{:S(2)}, u32[]{:S(2)}) collective-permute-start(bf16[96,1024]{1,0:T(8,128)(2,1)S(1)} %get-tuple-element.99), channel_id=1, source_target_pairs={{0,16},{8,24},{16,0},{24,8},{1,17},{9,25},{17,1},{25,9},{2,18},{10... | collective-permute-start | bytes 589832 | tf_op jit(solution)/shard_map/ppermute | solution.py:108
  63.6 0.6 fusion.3
  64.3 4.1 %collective-permute-done.24 = bf16[96,1024]{1,0:T(8,128)(2,1)S(1)} collective-permute-done((bf16[96,1024]{1,0:T(8,128)(2,1)S(1)}, bf16[96,1024]{1,0:T(8,128)(2,1)S(1)}, u32[]{:S(2)}, u32[]{:S(2)}) %collective-permute-start.24) | collective-permute-done | bytes 196640 | tf_op jit(solution)/shard_map/ppermute | solution.py:108
  69.1 1.3 %collective-permute-start.23 = (bf16[192,1024]{1,0:T(8,128)(2,1)S(1)}, bf16[192,1024]{1,0:T(8,128)(2,1)S(1)}, u32[]{:S(2)}, u32[]{:S(2)}) collective-permute-start(bf16[192,1024]{1,0:T(8,128)(2,1)S(1)} %pad_maximum_fusion.9), channel_id=1, source_target_pairs={{0,8},{8,0},{16,24},{24,16},{1,9},{9,1},{17,25},{25,17},{2,10},{10... | collective-permute-start | bytes 1179656 | tf_op jit(solution)/shard_map/ppermute | solution.py:108
  70.4 0.7 collective-permute-start.25
  71.1 0.6 convert_add_fusion
  71.9 1.5 %collective-permute-start.26 = (bf16[128,512]{1,0:T(8,128)(2,1)S(1)}, bf16[128,512]{1,0:T(8,128)(2,1)S(1)}, u32[]{:S(2)}, u32[]{:S(2)}) collective-permute-start(bf16[128,512]{1,0:T(8,128)(2,1)S(1)} %get-tuple-element.114), channel_id=1, source_target_pairs={{0,4},{2,6},{4,0},{6,2},{1,5},{3,7},{5,1},{7,3},{8,12},{10,14},{12... | collective-permute-start | bytes 393224 | tf_op jit(solution)/shard_map/ppermute | solution.py:108
  73.4 2.7 %collective-permute-start.28 = (bf16[128,512]{1,0:T(8,128)(2,1)S(1)}, bf16[128,512]{1,0:T(8,128)(2,1)S(1)}, u32[]{:S(2)}, u32[]{:S(2)}) collective-permute-start(bf16[128,512]{1,0:T(8,128)(2,1)S(1)} %get-tuple-element.115), channel_id=1, source_target_pairs={{0,6},{2,4},{4,2},{6,0},{1,7},{3,5},{5,3},{7,1},{8,14},{10,12},{12... | collective-permute-start | bytes 393224 | tf_op jit(solution)/shard_map/ppermute | solution.py:108
  76.0 1.0 %convolution_convert_fusion = bf16[768,512]{1,0:T(8,128)(2,1)S(1)} fusion(bf16[768,1024]{1,0:T(8,128)(2,1)S(1)} %constant_dynamic-update-slice_fusion.5, bf16[1024,512]{1,0:T(8,128)(2,1)S(1)} %fusion), kind=kOutput, calls=%fused_computation.3 | convolution fusion | flops 805699584 | bytes 3407872 | tf_op jit(solution)/shard_map/dot_general | solution.py:249
  77.1 0.9 %maximum_bitcast_fusion = bf16[1,768,512]{2,1,0:T(8,128)(2,1)} fusion(bf16[192,512]{1,0:T(8,128)(2,1)S(1)} %get-tuple-element.101, bf16[192,512]{1,0:T(8,128)(2,1)S(1)} %get-tuple-element.102, bf16[192,512]{1,0:T(8,128)(2,1)S(1)} %get-tuple-element.103, bf16[192,512]{1,0:T(8,128)(2,1)S(1)} %get-tuple-element.100), kind=kLoop, calls=%fused_computation.21 | loop fusion | flops 3145728 | bytes 1572864 | tf_op jit(solution)/shard_map/broadcast_in_dim | solution.py:256
  78.1 1.1 %collective-permute-done.23.x_ref = bf16[192,1024]{1,0:T(8,128)(2,1)S(1)} collective-permute-done((bf16[192,1024]{1,0:T(8,128)(2,1)S(1)}, bf16[192,1024]{1,0:T(8,128)(2,1)S(1)}, u32[]{:S(2)}, u32[]{:S(2)}) %collective-permute-start.23) | collective-permute-done | bytes 393248 | tf_op jit(solution)/shard_map/ppermute | solution.py:108
  79.1 1.1 %collective-permute-done.25.y_ref = bf16[192,1024]{1,0:T(8,128)(2,1)S(1)} collective-permute-done((bf16[192,1024]{1,0:T(8,128)(2,1)S(1)}, bf16[192,1024]{1,0:T(8,128)(2,1)S(1)}, u32[]{:S(2)}, u32[]{:S(2)}) %collective-permute-start.25) | collective-permute-done | bytes 393248 | tf_op jit(solution)/shard_map/ppermute | solution.py:108
  80.2 2.8 %shard_map.102 = (bf16[192,2048]{1,0:T(8,128)(2,1)}, bf16[192,2048]{1,0:T(8,128)(2,1)}) custom-call(s32[1]{0:T(128)} %bitcast.15.place_ref, f32[192,1024]{1,0:T(8,128)S(1)} %slice.141.share_ref, bf16[192,1024]{1,0:T(8,128)(2,1)S(1)} %collective-permute-done.23.x_ref, bf16[192,1024]{1,0:T(8,128)(2,1)S(1)} %collective-permute-done.25.y_ref, ...), custom_call_target="tpu_custom_call" | custom-call | tf_op jit(solution)/shard_map/pallas_call | solution.py:165
  83.1 0.6 collective-permute-done.26
  83.7 0.7 add_convert_fusion
  (78 shorter events, 6.1 us)
Async XLA Ops:
  0.6 12.5 %collective-permute-start.3 = (bf16[128,512]{1,0:T(8,128)(2,1)}, bf16[128,512]{1,0:T(8,128)(2,1)S(1)}, u32[]{:S(2)}, u32[]{:S(2)}) collective-permute-start(bf16[128,512]{1,0:T(8,128)(2,1)} %param.7), channel_id=1, source_target_pairs={{0,4},{2,6},{4,0},{6,2},{1,5},{3,7},{5,1},{7,3},{8,12},{10,14},{12... | collective-permute-start | bytes 393224 | tf_op jit(solution)/shard_map/ppermute | solution.py:108
  4.7 10.6 %collective-permute-start.2 = (bf16[128,512]{1,0:T(8,128)(2,1)}, bf16[128,512]{1,0:T(8,128)(2,1)S(1)}, u32[]{:S(2)}, u32[]{:S(2)}) collective-permute-start(bf16[128,512]{1,0:T(8,128)(2,1)} %param.7), channel_id=1, source_target_pairs={{0,24},{8,16},{16,8},{24,0},{1,25},{9,17},{17,9},{25,1},{2,26},{10... | collective-permute-start | bytes 393224 | tf_op jit(solution)/shard_map/ppermute | solution.py:108
  7.2 8.2 %collective-permute-start.1 = (bf16[128,512]{1,0:T(8,128)(2,1)}, bf16[128,512]{1,0:T(8,128)(2,1)S(1)}, u32[]{:S(2)}, u32[]{:S(2)}) collective-permute-start(bf16[128,512]{1,0:T(8,128)(2,1)} %param.7), channel_id=1, source_target_pairs={{0,16},{8,24},{16,0},{24,8},{1,17},{9,25},{17,1},{25,9},{2,18},{10... | collective-permute-start | bytes 393224 | tf_op jit(solution)/shard_map/ppermute | solution.py:108
  7.7 7.7 %collective-permute-start = (bf16[128,512]{1,0:T(8,128)(2,1)}, bf16[128,512]{1,0:T(8,128)(2,1)S(1)}, u32[]{:S(2)}, u32[]{:S(2)}) collective-permute-start(bf16[128,512]{1,0:T(8,128)(2,1)} %param.7), channel_id=1, source_target_pairs={{0,8},{8,0},{16,24},{24,16},{1,9},{9,1},{17,25},{25,17},{2,10},{10... | collective-permute-start | bytes 393224 | tf_op jit(solution)/shard_map/ppermute | solution.py:108
  8.2 7.1 %collective-permute-start.4 = (bf16[128,512]{1,0:T(8,128)(2,1)}, bf16[128,512]{1,0:T(8,128)(2,1)S(1)}, u32[]{:S(2)}, u32[]{:S(2)}) collective-permute-start(bf16[128,512]{1,0:T(8,128)(2,1)} %param.7), channel_id=1, source_target_pairs={{0,6},{2,4},{4,2},{6,0},{1,7},{3,5},{5,3},{7,1},{8,14},{10,12},{12... | collective-permute-start | bytes 393224 | tf_op jit(solution)/shard_map/ppermute | solution.py:108
  10.3 1.6 %copy-start.3 = (bf16[128,512]{1,0:T(8,128)(2,1)S(1)}, bf16[128,512]{1,0:T(8,128)(2,1)}, u32[]{:S(2)}) copy-start(bf16[128,512]{1,0:T(8,128)(2,1)} %param.8) | copy-start | bytes 393220
  10.3 5.1 %copy-start.1 = (bf16[128,512]{1,0:T(8,128)(2,1)S(1)}, bf16[128,512]{1,0:T(8,128)(2,1)}, u32[]{:S(2)}) copy-start(bf16[128,512]{1,0:T(8,128)(2,1)} %param.7) | copy-start | bytes 393220
  16.2 17.1 %collective-permute-start.8 = (bf16[512,512]{1,0:T(8,128)(2,1)}, bf16[512,512]{1,0:T(8,128)(2,1)S(1)}, u32[]{:S(2)}, u32[]{:S(2)}) collective-permute-start(bf16[512,512]{1,0:T(8,128)(2,1)} %pad_maximum_fusion.3), channel_id=1, source_target_pairs={{0,2},{2,0},{4,6},{6,4},{1,3},{3,1},{5,7},{7,5},{8,10},{10,8},{12,... | collective-permute-start | bytes 1572872 | tf_op jit(solution)/shard_map/ppermute | solution.py:108
  18.6 10.2 %collective-permute-start.7 = (bf16[256,512]{1,0:T(8,128)(2,1)S(1)}, bf16[256,512]{1,0:T(8,128)(2,1)S(1)}, u32[]{:S(2)}, u32[]{:S(2)}) collective-permute-start(bf16[256,512]{1,0:T(8,128)(2,1)S(1)} %pad_maximum_fusion.11), channel_id=1, source_target_pairs={{0,24},{8,16},{16,8},{24,0},{1,25},{9,17},{17,9},{25,1},{2,26},{10... | collective-permute-start | bytes 786440 | tf_op jit(solution)/shard_map/ppermute | solution.py:108
  21.0 12.0 %collective-permute-start.6 = (bf16[256,512]{1,0:T(8,128)(2,1)S(1)}, bf16[256,512]{1,0:T(8,128)(2,1)S(1)}, u32[]{:S(2)}, u32[]{:S(2)}) collective-permute-start(bf16[256,512]{1,0:T(8,128)(2,1)S(1)} %pad_maximum_fusion.11), channel_id=1, source_target_pairs={{0,16},{8,24},{16,0},{24,8},{1,17},{9,25},{17,1},{25,9},{2,18},{10... | collective-permute-start | bytes 786440 | tf_op jit(solution)/shard_map/ppermute | solution.py:108
  21.5 11.7 %collective-permute-start.5 = (bf16[256,512]{1,0:T(8,128)(2,1)S(1)}, bf16[256,512]{1,0:T(8,128)(2,1)}, u32[]{:S(2)}, u32[]{:S(2)}) collective-permute-start(bf16[256,512]{1,0:T(8,128)(2,1)S(1)} %pad_maximum_fusion.11), channel_id=1, source_target_pairs={{0,8},{8,0},{16,24},{24,16},{1,9},{9,1},{17,25},{25,17},{2,10},{10... | collective-permute-start | bytes 786440 | tf_op jit(solution)/shard_map/ppermute | solution.py:108
  33.3 24.4 %collective-permute-start.17 = (bf16[144,512]{1,0:T(8,128)(2,1)S(1)}, bf16[144,512]{1,0:T(8,128)(2,1)S(1)}, u32[]{:S(2)}, u32[]{:S(2)}) collective-permute-start(bf16[144,512]{1,0:T(8,128)(2,1)S(1)} %pad_maximum_fusion.12), channel_id=1, source_target_pairs={{0,4},{2,6},{4,0},{6,2},{1,5},{3,7},{5,1},{7,3},{8,12},{10,14},{12... | collective-permute-start | bytes 442376 | tf_op jit(solution)/shard_map/ppermute | solution.py:108
  36.4 5.0 %collective-permute-start.10 = (bf16[512,512]{1,0:T(8,128)(2,1)S(1)}, bf16[512,512]{1,0:T(8,128)(2,1)S(1)}, u32[]{:S(2)}, u32[]{:S(2)}) collective-permute-start(bf16[512,512]{1,0:T(8,128)(2,1)S(1)} %pad_maximum_fusion.5.refs_5_), channel_id=1, source_target_pairs={{0,1},{1,0},{2,3},{3,2},{4,5},{5,4},{6,7},{7,6},{8,9},{9,8},{10,11... | collective-permute-start | bytes 1572872 | tf_op jit(solution)/shard_map/ppermute | solution.py:108
  36.6 4.5 %collective-permute-start.11 = (bf16[512,512]{1,0:T(8,128)(2,1)S(1)}, bf16[512,512]{1,0:T(8,128)(2,1)S(1)}, u32[]{:S(2)}, u32[]{:S(2)}) collective-permute-start(bf16[512,512]{1,0:T(8,128)(2,1)S(1)} %pad_maximum_fusion.6.refs_6_), channel_id=1, source_target_pairs={{0,1},{1,0},{2,3},{3,2},{4,5},{5,4},{6,7},{7,6},{8,9},{9,8},{10,11... | collective-permute-start | bytes 1572872 | tf_op jit(solution)/shard_map/ppermute | solution.py:108
  37.2 3.5 %collective-permute-start.12 = (bf16[512,512]{1,0:T(8,128)(2,1)S(1)}, bf16[512,512]{1,0:T(8,128)(2,1)S(1)}, u32[]{:S(2)}, u32[]{:S(2)}) collective-permute-start(bf16[512,512]{1,0:T(8,128)(2,1)S(1)} %pad_maximum_fusion.7.refs_7_), channel_id=1, source_target_pairs={{0,1},{1,0},{2,3},{3,2},{4,5},{5,4},{6,7},{7,6},{8,9},{9,8},{10,11... | collective-permute-start | bytes 1572872 | tf_op jit(solution)/shard_map/ppermute | solution.py:108
  40.1 2.1 %collective-permute-start.9 = (bf16[512,512]{1,0:T(8,128)(2,1)S(1)}, bf16[512,512]{1,0:T(8,128)(2,1)S(1)}, u32[]{:S(2)}, u32[]{:S(2)}) collective-permute-start(bf16[512,512]{1,0:T(8,128)(2,1)S(1)} %pad_maximum_fusion.4.refs_4_), channel_id=1, source_target_pairs={{0,1},{1,0},{2,3},{3,2},{4,5},{5,4},{6,7},{7,6},{8,9},{9,8},{10,11... | collective-permute-start | bytes 1572872 | tf_op jit(solution)/shard_map/ppermute | solution.py:108
  42.6 2.5 %copy-start.2 = (bf16[1,768,512]{2,1,0:T(8,128)(2,1)S(1)}, bf16[1,768,512]{2,1,0:T(8,128)(2,1)}, u32[]{:S(2)}) copy-start(bf16[1,768,512]{2,1,0:T(8,128)(2,1)} %param.13) | copy-start | bytes 2359300
  42.9 12.0 %collective-permute-start.14 = (bf16[192,1024]{1,0:T(8,128)(2,1)S(1)}, bf16[192,1024]{1,0:T(8,128)(2,1)S(1)}, u32[]{:S(2)}, u32[]{:S(2)}) collective-permute-start(bf16[192,1024]{1,0:T(8,128)(2,1)S(1)} %pad_maximum_fusion.8), channel_id=1, source_target_pairs={{0,16},{8,24},{16,0},{24,8},{1,17},{9,25},{17,1},{25,9},{2,18},{10... | collective-permute-start | bytes 1179656 | tf_op jit(solution)/shard_map/ppermute | solution.py:108
  44.3 11.1 %collective-permute-start.13 = (bf16[192,1024]{1,0:T(8,128)(2,1)S(1)}, bf16[192,1024]{1,0:T(8,128)(2,1)S(1)}, u32[]{:S(2)}, u32[]{:S(2)}) collective-permute-start(bf16[192,1024]{1,0:T(8,128)(2,1)S(1)} %pad_maximum_fusion.8), channel_id=1, source_target_pairs={{0,8},{8,0},{16,24},{24,16},{1,9},{9,1},{17,25},{25,17},{2,10},{10... | collective-permute-start | bytes 1179656 | tf_op jit(solution)/shard_map/ppermute | solution.py:108
  45.2 8.6 %collective-permute-start.16 = (bf16[144,512]{1,0:T(8,128)(2,1)S(1)}, bf16[144,512]{1,0:T(8,128)(2,1)S(1)}, u32[]{:S(2)}, u32[]{:S(2)}) collective-permute-start(bf16[144,512]{1,0:T(8,128)(2,1)S(1)} %pad_maximum_fusion.12), channel_id=1, source_target_pairs={{0,6},{2,4},{4,2},{6,0},{1,7},{3,5},{5,3},{7,1},{8,14},{10,12},{12... | collective-permute-start | bytes 442376 | tf_op jit(solution)/shard_map/ppermute | solution.py:108
  46.5 8.4 %collective-permute-start.15 = (bf16[144,512]{1,0:T(8,128)(2,1)S(1)}, bf16[144,512]{1,0:T(8,128)(2,1)S(1)}, u32[]{:S(2)}, u32[]{:S(2)}) collective-permute-start(bf16[144,512]{1,0:T(8,128)(2,1)S(1)} %pad_maximum_fusion.12), channel_id=1, source_target_pairs={{0,2},{2,0},{4,6},{6,4},{1,3},{3,1},{5,7},{7,5},{8,10},{10,8},{12,... | collective-permute-start | bytes 442376 | tf_op jit(solution)/shard_map/ppermute | solution.py:108
  55.4 8.0 %collective-permute-start.20 = (bf16[96,1024]{1,0:T(8,128)(2,1)S(1)}, bf16[96,1024]{1,0:T(8,128)(2,1)S(1)}, u32[]{:S(2)}, u32[]{:S(2)}) collective-permute-start(bf16[96,1024]{1,0:T(8,128)(2,1)S(1)} %slice.120), channel_id=1, source_target_pairs={{0,8},{8,0},{16,24},{24,16},{1,9},{9,1},{17,25},{25,17},{2,10},{10... | collective-permute-start | bytes 589832 | tf_op jit(solution)/shard_map/ppermute | solution.py:108
  56.3 7.1 %collective-permute-start.19 = (bf16[96,1024]{1,0:T(8,128)(2,1)S(1)}, bf16[96,1024]{1,0:T(8,128)(2,1)S(1)}, u32[]{:S(2)}, u32[]{:S(2)}) collective-permute-start(bf16[96,1024]{1,0:T(8,128)(2,1)S(1)} %slice.119), channel_id=1, source_target_pairs={{0,16},{8,24},{16,0},{24,8},{1,17},{9,25},{17,1},{25,9},{2,18},{10... | collective-permute-start | bytes 589832 | tf_op jit(solution)/shard_map/ppermute | solution.py:108
  57.8 2.1 %collective-permute-start.18 = (bf16[4,144,512]{2,1,0:T(8,128)(2,1)S(1)}, bf16[4,144,512]{2,1,0:T(8,128)(2,1)S(1)}, u32[]{:S(2)}, u32[]{:S(2)}) collective-permute-start(bf16[4,144,512]{2,1,0:T(8,128)(2,1)S(1)} %pad_maximum_fusion.2), channel_id=1, source_target_pairs={{0,1},{1,0},{2,3},{3,2},{4,5},{5,4},{6,7},{7,6},{8,9},{9,8},{10,11... | collective-permute-start | bytes 1769480 | tf_op jit(solution)/shard_map/ppermute | solution.py:108
  61.4 7.0 %collective-permute-start.24 = (bf16[96,1024]{1,0:T(8,128)(2,1)S(1)}, bf16[96,1024]{1,0:T(8,128)(2,1)S(1)}, u32[]{:S(2)}, u32[]{:S(2)}) collective-permute-start(bf16[96,1024]{1,0:T(8,128)(2,1)S(1)} %get-tuple-element.97), channel_id=1, source_target_pairs={{0,8},{8,0},{16,24},{24,16},{1,9},{9,1},{17,25},{25,17},{2,10},{10... | collective-permute-start | bytes 589832 | tf_op jit(solution)/shard_map/ppermute | solution.py:108
  62.2 6.7 %collective-permute-start.22 = (bf16[96,1024]{1,0:T(8,128)(2,1)S(1)}, bf16[96,1024]{1,0:T(8,128)(2,1)S(1)}, u32[]{:S(2)}, u32[]{:S(2)}) collective-permute-start(bf16[96,1024]{1,0:T(8,128)(2,1)S(1)} %get-tuple-element.99), channel_id=1, source_target_pairs={{0,16},{8,24},{16,0},{24,8},{1,17},{9,25},{17,1},{25,9},{2,18},{10... | collective-permute-start | bytes 589832 | tf_op jit(solution)/shard_map/ppermute | solution.py:108
  64.2 6.9 %collective-permute-start.21 = (bf16[512,512]{1,0:T(8,128)(2,1)S(1)}, bf16[512,512]{1,0:T(8,128)(2,1)S(1)}, u32[]{:S(2)}, u32[]{:S(2)}) collective-permute-start(bf16[512,512]{1,0:T(8,128)(2,1)S(1)} %fusion.3), channel_id=1, source_target_pairs={{0,1},{1,0},{2,3},{3,2},{4,5},{5,4},{6,7},{7,6},{8,9},{9,8},{10,11... | collective-permute-start | bytes 1572872 | tf_op jit(solution)/shard_map/ppermute | solution.py:108
  69.1 10.1 %collective-permute-start.23 = (bf16[192,1024]{1,0:T(8,128)(2,1)S(1)}, bf16[192,1024]{1,0:T(8,128)(2,1)S(1)}, u32[]{:S(2)}, u32[]{:S(2)}) collective-permute-start(bf16[192,1024]{1,0:T(8,128)(2,1)S(1)} %pad_maximum_fusion.9), channel_id=1, source_target_pairs={{0,8},{8,0},{16,24},{24,16},{1,9},{9,1},{17,25},{25,17},{2,10},{10... | collective-permute-start | bytes 1179656 | tf_op jit(solution)/shard_map/ppermute | solution.py:108
  70.4 9.8 %collective-permute-start.25 = (bf16[192,1024]{1,0:T(8,128)(2,1)S(1)}, bf16[192,1024]{1,0:T(8,128)(2,1)S(1)}, u32[]{:S(2)}, u32[]{:S(2)}) collective-permute-start(bf16[192,1024]{1,0:T(8,128)(2,1)S(1)} %pad_maximum_fusion.10), channel_id=1, source_target_pairs={{0,16},{8,24},{16,0},{24,8},{1,17},{9,25},{17,1},{25,9},{2,18},{10... | collective-permute-start | bytes 1179656 | tf_op jit(solution)/shard_map/ppermute | solution.py:108
  71.8 5.3 %copy-start = (f32[512,512]{1,0:T(8,128)}, f32[512,512]{1,0:T(8,128)S(1)}, u32[]{:S(2)}) copy-start(f32[512,512]{1,0:T(8,128)S(1)} %convert_add_fusion) | copy-start | bytes 3145732
  71.9 11.8 %collective-permute-start.26 = (bf16[128,512]{1,0:T(8,128)(2,1)S(1)}, bf16[128,512]{1,0:T(8,128)(2,1)S(1)}, u32[]{:S(2)}, u32[]{:S(2)}) collective-permute-start(bf16[128,512]{1,0:T(8,128)(2,1)S(1)} %get-tuple-element.114), channel_id=1, source_target_pairs={{0,4},{2,6},{4,0},{6,2},{1,5},{3,7},{5,1},{7,3},{8,12},{10,14},{12... | collective-permute-start | bytes 393224 | tf_op jit(solution)/shard_map/ppermute | solution.py:108
  73.4 10.3 %collective-permute-start.28 = (bf16[128,512]{1,0:T(8,128)(2,1)S(1)}, bf16[128,512]{1,0:T(8,128)(2,1)S(1)}, u32[]{:S(2)}, u32[]{:S(2)}) collective-permute-start(bf16[128,512]{1,0:T(8,128)(2,1)S(1)} %get-tuple-element.115), channel_id=1, source_target_pairs={{0,6},{2,4},{4,2},{6,0},{1,7},{3,5},{5,3},{7,1},{8,14},{10,12},{12... | collective-permute-start | bytes 393224 | tf_op jit(solution)/shard_map/ppermute | solution.py:108
  76.0 7.6 %collective-permute-start.27 = (bf16[128,512]{1,0:T(8,128)(2,1)S(1)}, bf16[128,512]{1,0:T(8,128)(2,1)S(1)}, u32[]{:S(2)}, u32[]{:S(2)}) collective-permute-start(bf16[128,512]{1,0:T(8,128)(2,1)S(1)} %get-tuple-element.116), channel_id=1, source_target_pairs={{0,2},{2,0},{4,6},{6,4},{1,3},{3,1},{5,7},{7,5},{8,10},{10,8},{12,... | collective-permute-start | bytes 393224 | tf_op jit(solution)/shard_map/ppermute | solution.py:108
  80.2 3.4 %slice-start = ((f32[512,512]{1,0:T(8,128)}), f32[128,512]{1,0:T(8,128)S(1)}, s32[]{:S(2)}) async-start(f32[512,512]{1,0:T(8,128)} %copy-done), calls=%async_computation | async-start | bytes 524288 | tf_op jit(solution)/shard_map/slice | solution.py:247

commit v4 on v3

--- a/solution.py
+++ b/solution.py
@@ -192,13 +192,16 @@
     table = stack(high, scales - high).astype(half_type)
     table = jnp.pad(table, ((0, 0), (0, quarter - rows)))
     payload = stack(grad_out, table)
-    own, far, payload, in_weights, *p0 = phase(stack(*p0), stack(t2, t3), payload, in_weights, *p0)
-
+    own = stack(*p0)
     p1 = swap(own, "grp", 1)
+    own, far, payload, in_weights = phase(own, stack(t2, t3), payload, in_weights)
+    p0 = [own[j * rows : (j + 1) * rows] for j in range(4)]
+
     p2 = [far] + spread(far)
+    late, p1 = phase(payload, p1)
+    g2, g3 = swap(late, "grp", 2), swap(late, "grp", 3)
     *p2, payload, p1 = phase(*p2, payload, p1)
 
-    g2 = swap(payload, "grp", 2)
     parts = [stack(p0[j], p1[j * rows : (j + 1) * rows], p2[j]) for j in range(4)]
     parts_there = [to_core(p) for p in parts]
     acts = []
@@ -213,10 +216,9 @@
 
     hx, hy = swap(hidden, "dp", 1), swap(hidden, "dp", 2)
     down_rows, payload = phase(regroup(down_weight[0], 0, place), payload)
-    g1, g3 = swap(payload, "grp", 1), swap(payload, "grp", 3)
-    hx, hy, g1, g3 = phase(hx, hy, g1, g3)
+    g1 = swap(payload, "grp", 1)
+    last_x, last_y = swap(hy[half:], "dp", 1), swap(hx[:half], "dp", 2)
     blocks = jnp.stack([payload, g1, g2, g3])
-    last_x, last_y = swap(hy[half:], "dp", 1), swap(hx[:half], "dp", 2)
     blocks = stack(blocks, to_core(blocks))
     table = blocks[:, rows:, :rows].astype(wide_type).reshape(8, 2, experts, rows)
     scale = lax.dynamic_index_in_dim(table, expert, 2, keepdims=False)

time: 84.6 us -> 77.9 us (0.921)
  starting transfers between devices: 32.8 us -> 30 us
  waiting for transfers between devices: 32.5 us -> 30.2 us
  other arithmetic: 6.98 us -> 5.2 us
  local copies, waits for them, and re-layouts: 0.65 us -> 1.82 us
  matrix products: 7.45 us -> 6.52 us
    ppermute x29, starting transfers between devices: 32.8 us -> 30 us  [swap(): return lax.ppermute(value, axis, pairs)]
    ppermute x29, waiting for transfers between devices: 32.5 us -> 30.2 us  [swap(): return lax.ppermute(value, axis, pairs)]
    concatenate x11 -> x10, other arithmetic: 3.53 us -> 1.75 us  [stack(): return jnp.concatenate(values, axis=0)]
    slice x1, local copies, waits for them, and re-layouts: 0.03 us -> 1.13 us  [dense_body(): parts = [stack(p0[j], p1[j * rows:(j + 1) * rows], p2[j]) for j in range(4)]]
    dot_general x8, matrix products: 4.22 us -> 3.27 us  [dense_body(): pre = pre + lax.dot_general(w_part, part, contract_last, **wide)]
  transfers between devices with their start and end apart: 29 -> 29, of which waited for: 15 -> 16; matrix products, arithmetic and copies ran while one was open for 16% -> 16% of each run, Pallas kernels for 3% -> 4%
where the time goes in v4:
time: 77.9 us; the launch traced here: 77.7 us
  waiting for transfers between devices  30.2 us (39%)
  starting transfers between devices  30 us (39%)
  matrix products  6.52 us (8%)
  other arithmetic  5.2 us (7%)
  Pallas kernels  2.85 us (4%)
  local copies, waits for them, and re-layouts  1.82 us (2%)
  between operations  1.16 us (1%)
    ppermute x29, waiting for transfers between devices, swap(): return lax.ppermute(value, axis, pairs)  30.2 us
    ppermute x29, starting transfers between devices, swap(): return lax.ppermute(value, axis, pairs)  30 us
    dot_general x8, matrix products, dense_body(): pre = pre + lax.dot_general(w_part, part, contract_last, **wide)  3.27 us
    pallas_call x1, Pallas kernels, in_gradients(): pl.pallas_call(kernel, out_shape=[jax.ShapeDtypeStruct((units, 4 * quarte...  2.85 us
    concatenate x10, other arithmetic, stack(): return jnp.concatenate(values, axis=0)  1.75 us
  transfers between devices with their start and end apart: 29, of which 16 were waited for; matrix products, arithmetic and copies ran while one was open for 16% of the time, Pallas kernels for 4%

profile of v4, /device:TPU:0, one launch (start us, length us, event | category | flops | bytes accessed | tf_op | source)
XLA Modules:
  0.0 77.7 jit_solution(8403772874383405661)
XLA Ops:
  0.6 4.0 %collective-permute-start.2 = (bf16[128,512]{1,0:T(8,128)(2,1)}, bf16[128,512]{1,0:T(8,128)(2,1)S(1)}, u32[]{:S(2)}, u32[]{:S(2)}) collective-permute-start(bf16[128,512]{1,0:T(8,128)(2,1)} %param.7), channel_id=1, source_target_pairs={{0,24},{8,16},{16,8},{24,0},{1,25},{9,17},{17,9},{25,1},{2,26},{10... | collective-permute-start | bytes 393224 | tf_op jit(solution)/shard_map/ppermute | solution.py:108
  4.6 0.5 collective-permute-start.1
  5.2 4.0 %collective-permute-start.4 = (bf16[128,512]{1,0:T(8,128)(2,1)}, bf16[128,512]{1,0:T(8,128)(2,1)S(1)}, u32[]{:S(2)}, u32[]{:S(2)}) collective-permute-start(bf16[128,512]{1,0:T(8,128)(2,1)} %param.7), channel_id=1, source_target_pairs={{0,6},{2,4},{4,2},{6,0},{1,7},{3,5},{5,3},{7,1},{8,14},{10,12},{12... | collective-permute-start | bytes 393224 | tf_op jit(solution)/shard_map/ppermute | solution.py:108
  9.2 0.7 select_reduce_fusion
  10.0 1.5 %pad_maximum_fusion = bf16[384,2048]{1,0:T(8,128)(2,1)S(1)} fusion(bf16[192,2048]{1,0:T(8,128)(2,1)} %bitcast.45, bf16[192,2048]{1,0:T(8,128)(2,1)} %bitcast.46), kind=kLoop, calls=%fused_computation.2 | loop fusion | flops 3145728 | bytes 3145728 | tf_op jit(solution)/shard_map/concatenate | solution.py:120
  11.6 1.5 %collective-permute-start.8 = (bf16[512,512]{1,0:T(8,128)(2,1)S(1)}, bf16[512,512]{1,0:T(8,128)(2,1)}, u32[]{:S(2)}, u32[]{:S(2)}) collective-permute-start(bf16[512,512]{1,0:T(8,128)(2,1)S(1)} %constant_dynamic-update-slice_fusion), channel_id=1, source_target_pairs={{0,2},{2,0},{4,6},{6,4},{1,3},{3,1},{5,7},{7,5},{8,10},{10,8},{12,... | collective-permute-start | bytes 1572872 | tf_op jit(solution)/shard_map/ppermute | solution.py:108
  13.1 0.5 collective-permute-done.4
  13.6 6.1 %collective-permute-done.3 = bf16[128,512]{1,0:T(8,128)(2,1)S(1)} collective-permute-done((bf16[128,512]{1,0:T(8,128)(2,1)}, bf16[128,512]{1,0:T(8,128)(2,1)S(1)}, u32[]{:S(2)}, u32[]{:S(2)}) %collective-permute-start.3) | collective-permute-done | bytes 131104 | tf_op jit(solution)/shard_map/ppermute | solution.py:108
  19.8 2.5 %collective-permute-start.7 = (bf16[256,512]{1,0:T(8,128)(2,1)S(1)}, bf16[256,512]{1,0:T(8,128)(2,1)S(1)}, u32[]{:S(2)}, u32[]{:S(2)}) collective-permute-start(bf16[256,512]{1,0:T(8,128)(2,1)S(1)} %pad_maximum_fusion.10), channel_id=1, source_target_pairs={{0,24},{8,16},{16,8},{24,0},{1,25},{9,17},{17,9},{25,1},{2,26},{10... | collective-permute-start | bytes 786440 | tf_op jit(solution)/shard_map/ppermute | solution.py:108
  22.3 0.5 collective-permute-start.6
  22.8 0.5 collective-permute-start.5
  23.4 4.6 %collective-permute-done.8 = bf16[512,512]{1,0:T(8,128)(2,1)} collective-permute-done((bf16[512,512]{1,0:T(8,128)(2,1)S(1)}, bf16[512,512]{1,0:T(8,128)(2,1)}, u32[]{:S(2)}, u32[]{:S(2)}) %collective-permute-start.8) | collective-permute-done | bytes 524320 | tf_op jit(solution)/shard_map/ppermute | solution.py:108
  28.0 3.1 %collective-permute-start.15 = (bf16[144,512]{1,0:T(8,128)(2,1)S(1)}, bf16[144,512]{1,0:T(8,128)(2,1)S(1)}, u32[]{:S(2)}, u32[]{:S(2)}) collective-permute-start(bf16[144,512]{1,0:T(8,128)(2,1)S(1)} %pad_maximum_fusion.11), channel_id=1, source_target_pairs={{0,6},{2,4},{4,2},{6,0},{1,7},{3,5},{5,3},{7,1},{8,14},{10,12},{12... | collective-permute-start | bytes 442376 | tf_op jit(solution)/shard_map/ppermute | solution.py:108
  31.1 2.4 %collective-permute-done.6 = bf16[256,512]{1,0:T(8,128)(2,1)S(1)} collective-permute-done((bf16[256,512]{1,0:T(8,128)(2,1)S(1)}, bf16[256,512]{1,0:T(8,128)(2,1)S(1)}, u32[]{:S(2)}, u32[]{:S(2)}) %collective-permute-start.6) | collective-permute-done | bytes 262176 | tf_op jit(solution)/shard_map/ppermute | solution.py:108
  33.7 1.1 %fusion.44 = (bf16[128,512]{1,0:T(8,128)(2,1)S(1)}, bf16[128,512]{1,0:T(8,128)(2,1)S(1)}, bf16[128,512]{1,0:T(8,128)(2,1)S(1)}, bf16[128,512]{1,0:T(8,128)(2,1)S(1)}) fusion(bf16[512,512]{1,0:T(8,128)(2,1)} %collective-permute-done.8), kind=kLoop, calls=%fused_computation.104 | loop fusion | bytes 1048576 | tf_op jit(solution)/shard_map/slice | solution.py:205
  35.0 0.6 collective-permute-start.11
  36.0 0.4 convolution_add_fusion.3
  36.5 0.4 convolution_add_fusion.2
  36.9 0.4 convolution_add_fusion.1
  37.5 0.8 collective-permute-done.10.refs_9_
  38.9 0.4 fusion.19
  39.7 0.5 collective-permute-done.9.refs_8_
  40.2 0.4 fusion.7
  40.9 1.5 %collective-permute-start.18 = (bf16[192,1024]{1,0:T(8,128)(2,1)S(1)}, bf16[192,1024]{1,0:T(8,128)(2,1)S(1)}, u32[]{:S(2)}, u32[]{:S(2)}) collective-permute-start(bf16[192,1024]{1,0:T(8,128)(2,1)S(1)} %pad_maximum_fusion.7), channel_id=1, source_target_pairs={{0,16},{8,24},{16,0},{24,8},{1,17},{9,25},{17,1},{25,9},{2,18},{10... | collective-permute-start | bytes 1179656 | tf_op jit(solution)/shard_map/ppermute | solution.py:108
  42.4 0.8 %collective-permute-start.17 = (bf16[192,1024]{1,0:T(8,128)(2,1)S(1)}, bf16[192,1024]{1,0:T(8,128)(2,1)S(1)}, u32[]{:S(2)}, u32[]{:S(2)}) collective-permute-start(bf16[192,1024]{1,0:T(8,128)(2,1)S(1)} %pad_maximum_fusion.7), channel_id=1, source_target_pairs={{0,8},{8,0},{16,24},{24,16},{1,9},{9,1},{17,25},{25,17},{2,10},{10... | collective-permute-start | bytes 1179656 | tf_op jit(solution)/shard_map/ppermute | solution.py:108
  43.5 5.3 %collective-permute-done.13 = bf16[144,512]{1,0:T(8,128)(2,1)S(1)} collective-permute-done((bf16[144,512]{1,0:T(8,128)(2,1)S(1)}, bf16[144,512]{1,0:T(8,128)(2,1)S(1)}, u32[]{:S(2)}, u32[]{:S(2)}) %collective-permute-start.13) | collective-permute-done | bytes 147488 | tf_op jit(solution)/shard_map/ppermute | solution.py:108
  49.0 3.2 %collective-permute-done.18 = bf16[192,1024]{1,0:T(8,128)(2,1)S(1)} collective-permute-done((bf16[192,1024]{1,0:T(8,128)(2,1)S(1)}, bf16[192,1024]{1,0:T(8,128)(2,1)S(1)}, u32[]{:S(2)}, u32[]{:S(2)}) %collective-permute-start.18) | collective-permute-done | bytes 393248 | tf_op jit(solution)/shard_map/ppermute | solution.py:108
  52.2 1.6 %collective-permute-start.20 = (bf16[96,1024]{1,0:T(8,128)(2,1)S(1)}, bf16[96,1024]{1,0:T(8,128)(2,1)S(1)}, u32[]{:S(2)}, u32[]{:S(2)}) collective-permute-start(bf16[96,1024]{1,0:T(8,128)(2,1)S(1)} %slice.159), channel_id=1, source_target_pairs={{0,8},{8,0},{16,24},{24,16},{1,9},{9,1},{17,25},{25,17},{2,10},{10... | collective-permute-start | bytes 589832 | tf_op jit(solution)/shard_map/ppermute | solution.py:108
  53.8 0.8 %collective-permute-start.19 = (bf16[96,1024]{1,0:T(8,128)(2,1)S(1)}, bf16[96,1024]{1,0:T(8,128)(2,1)S(1)}, u32[]{:S(2)}, u32[]{:S(2)}) collective-permute-start(bf16[96,1024]{1,0:T(8,128)(2,1)S(1)} %slice.158), channel_id=1, source_target_pairs={{0,16},{8,24},{16,0},{24,8},{1,17},{9,25},{17,1},{25,9},{2,18},{10... | collective-permute-start | bytes 589832 | tf_op jit(solution)/shard_map/ppermute | solution.py:108
  55.0 1.0 %fusion.45 = (bf16[768,1024]{1,0:T(8,128)(2,1)S(1)}, f32[768,1024]{1,0:T(8,128)S(1)}) fusion(bf16[768,512]{1,0:T(8,128)(2,1)S(1)} %pad_maximum_fusion.1, bf16[1024,512]{1,0:T(8,128)(2,1)S(1)} %fusion), kind=kOutput, calls=%fused_computation.105 | convolution fusion | flops 806092800 | bytes 6553600 | tf_op jit(solution)/shard_map/dot_general | solution.py:228
  56.1 1.3 %collective-permute-start.24 = (bf16[96,1024]{1,0:T(8,128)(2,1)S(1)}, bf16[96,1024]{1,0:T(8,128)(2,1)S(1)}, u32[]{:S(2)}, u32[]{:S(2)}) collective-permute-start(bf16[96,1024]{1,0:T(8,128)(2,1)S(1)} %get-tuple-element.85), channel_id=1, source_target_pairs={{0,8},{8,0},{16,24},{24,16},{1,9},{9,1},{17,25},{25,17},{2,10},{10... | collective-permute-start | bytes 589832 | tf_op jit(solution)/shard_map/ppermute | solution.py:108
  57.4 0.6 collective-permute-start.22
  58.1 1.0 %collective-permute-done.20 = bf16[96,1024]{1,0:T(8,128)(2,1)S(1)} collective-permute-done((bf16[96,1024]{1,0:T(8,128)(2,1)S(1)}, bf16[96,1024]{1,0:T(8,128)(2,1)S(1)}, u32[]{:S(2)}, u32[]{:S(2)}) %collective-permute-start.20) | collective-permute-done | bytes 196640 | tf_op jit(solution)/shard_map/ppermute | solution.py:108
  59.1 1.7 %collective-permute-done.19 = bf16[96,1024]{1,0:T(8,128)(2,1)S(1)} collective-permute-done((bf16[96,1024]{1,0:T(8,128)(2,1)S(1)}, bf16[96,1024]{1,0:T(8,128)(2,1)S(1)}, u32[]{:S(2)}, u32[]{:S(2)}) %collective-permute-start.19) | collective-permute-done | bytes 196640 | tf_op jit(solution)/shard_map/ppermute | solution.py:108
  61.0 0.6 fusion.3
  61.7 0.9 %collective-permute-done.24 = bf16[96,1024]{1,0:T(8,128)(2,1)S(1)} collective-permute-done((bf16[96,1024]{1,0:T(8,128)(2,1)S(1)}, bf16[96,1024]{1,0:T(8,128)(2,1)S(1)}, u32[]{:S(2)}, u32[]{:S(2)}) %collective-permute-start.24) | collective-permute-done | bytes 196640 | tf_op jit(solution)/shard_map/ppermute | solution.py:108
  62.6 1.3 %collective-permute-done.22 = bf16[96,1024]{1,0:T(8,128)(2,1)S(1)} collective-permute-done((bf16[96,1024]{1,0:T(8,128)(2,1)S(1)}, bf16[96,1024]{1,0:T(8,128)(2,1)S(1)}, u32[]{:S(2)}, u32[]{:S(2)}) %collective-permute-start.22) | collective-permute-done | bytes 196640 | tf_op jit(solution)/shard_map/ppermute | solution.py:108
  64.0 0.6 collective-permute-start.23
  64.6 1.5 %collective-permute-start.25 = (bf16[192,1024]{1,0:T(8,128)(2,1)S(1)}, bf16[192,1024]{1,0:T(8,128)(2,1)S(1)}, u32[]{:S(2)}, u32[]{:S(2)}) collective-permute-start(bf16[192,1024]{1,0:T(8,128)(2,1)S(1)} %pad_maximum_fusion.9), channel_id=1, source_target_pairs={{0,16},{8,24},{16,0},{24,8},{1,17},{9,25},{17,1},{25,9},{2,18},{10... | collective-permute-start | bytes 1179656 | tf_op jit(solution)/shard_map/ppermute | solution.py:108
  66.1 0.6 convert_add_fusion
  66.9 0.6 collective-permute-start.26
  67.5 0.8 %collective-permute-start.28 = (bf16[128,512]{1,0:T(8,128)(2,1)S(1)}, bf16[128,512]{1,0:T(8,128)(2,1)S(1)}, u32[]{:S(2)}, u32[]{:S(2)}) collective-permute-start(bf16[128,512]{1,0:T(8,128)(2,1)S(1)} %get-tuple-element.103), channel_id=1, source_target_pairs={{0,6},{2,4},{4,2},{6,0},{1,7},{3,5},{5,3},{7,1},{8,14},{10,12},{12... | collective-permute-start | bytes 393224 | tf_op jit(solution)/shard_map/ppermute | solution.py:108
  68.3 2.1 %collective-permute-start.27 = (bf16[128,512]{1,0:T(8,128)(2,1)S(1)}, bf16[128,512]{1,0:T(8,128)(2,1)S(1)}, u32[]{:S(2)}, u32[]{:S(2)}) collective-permute-start(bf16[128,512]{1,0:T(8,128)(2,1)S(1)} %get-tuple-element.104), channel_id=1, source_target_pairs={{0,2},{2,0},{4,6},{6,4},{1,3},{3,1},{5,7},{7,5},{8,10},{10,8},{12,... | collective-permute-start | bytes 393224 | tf_op jit(solution)/shard_map/ppermute | solution.py:108
  70.5 1.0 %convolution_convert_fusion = bf16[768,512]{1,0:T(8,128)(2,1)S(1)} fusion(bf16[768,1024]{1,0:T(8,128)(2,1)S(1)} %constant_dynamic-update-slice_fusion.9, bf16[1024,512]{1,0:T(8,128)(2,1)S(1)} %fusion), kind=kOutput, calls=%fused_computation.3 | convolution fusion | flops 805699584 | bytes 3407872 | tf_op jit(solution)/shard_map/dot_general | solution.py:251
  71.5 0.9 %maximum_bitcast_fusion = bf16[1,768,512]{2,1,0:T(8,128)(2,1)} fusion(bf16[192,512]{1,0:T(8,128)(2,1)S(1)} %get-tuple-element.89, bf16[192,512]{1,0:T(8,128)(2,1)S(1)} %get-tuple-element.90, bf16[192,512]{1,0:T(8,128)(2,1)S(1)} %get-tuple-element.91, bf16[192,512]{1,0:T(8,128)(2,1)S(1)} %get-tuple-element.88), kind=kLoop, calls=%fused_computation.21 | loop fusion | flops 3145728 | bytes 1572864 | tf_op jit(solution)/shard_map/broadcast_in_dim | solution.py:258
  72.5 1.4 %collective-permute-done.23.x_ref = bf16[192,1024]{1,0:T(8,128)(2,1)S(1)} collective-permute-done((bf16[192,1024]{1,0:T(8,128)(2,1)S(1)}, bf16[192,1024]{1,0:T(8,128)(2,1)S(1)}, u32[]{:S(2)}, u32[]{:S(2)}) %collective-permute-start.23) | collective-permute-done | bytes 393248 | tf_op jit(solution)/shard_map/ppermute | solution.py:108
  74.0 2.8 %shard_map.102 = (bf16[192,2048]{1,0:T(8,128)(2,1)}, bf16[192,2048]{1,0:T(8,128)(2,1)}) custom-call(s32[1]{0:T(128)} %bitcast.15.place_ref, f32[192,1024]{1,0:T(8,128)S(1)} %slice.157.share_ref, bf16[192,1024]{1,0:T(8,128)(2,1)S(1)} %collective-permute-done.23.x_ref, bf16[192,1024]{1,0:T(8,128)(2,1)S(1)} %collective-permute-done.25.y_ref, ...), custom_call_target="tpu_custom_call" | custom-call | tf_op jit(solution)/shard_map/pallas_call | solution.py:165
  77.0 0.7 add_convert_fusion
  (82 shorter events, 4.3 us)
Async XLA Ops:
  0.6 10.9 %collective-permute-start.2 = (bf16[128,512]{1,0:T(8,128)(2,1)}, bf16[128,512]{1,0:T(8,128)(2,1)S(1)}, u32[]{:S(2)}, u32[]{:S(2)}) collective-permute-start(bf16[128,512]{1,0:T(8,128)(2,1)} %param.7), channel_id=1, source_target_pairs={{0,24},{8,16},{16,8},{24,0},{1,25},{9,17},{17,9},{25,1},{2,26},{10... | collective-permute-start | bytes 393224 | tf_op jit(solution)/shard_map/ppermute | solution.py:108
  4.6 7.0 %collective-permute-start.1 = (bf16[128,512]{1,0:T(8,128)(2,1)}, bf16[128,512]{1,0:T(8,128)(2,1)S(1)}, u32[]{:S(2)}, u32[]{:S(2)}) collective-permute-start(bf16[128,512]{1,0:T(8,128)(2,1)} %param.7), channel_id=1, source_target_pairs={{0,16},{8,24},{16,0},{24,8},{1,17},{9,25},{17,1},{25,9},{2,18},{10... | collective-permute-start | bytes 393224 | tf_op jit(solution)/shard_map/ppermute | solution.py:108
  5.1 6.4 %collective-permute-start = (bf16[128,512]{1,0:T(8,128)(2,1)}, bf16[128,512]{1,0:T(8,128)(2,1)S(1)}, u32[]{:S(2)}, u32[]{:S(2)}) collective-permute-start(bf16[128,512]{1,0:T(8,128)(2,1)} %param.7), channel_id=1, source_target_pairs={{0,8},{8,0},{16,24},{24,16},{1,9},{9,1},{17,25},{25,17},{2,10},{10... | collective-permute-start | bytes 393224 | tf_op jit(solution)/shard_map/ppermute | solution.py:108
  5.2 8.4 %collective-permute-start.4 = (bf16[128,512]{1,0:T(8,128)(2,1)}, bf16[128,512]{1,0:T(8,128)(2,1)S(1)}, u32[]{:S(2)}, u32[]{:S(2)}) collective-permute-start(bf16[128,512]{1,0:T(8,128)(2,1)} %param.7), channel_id=1, source_target_pairs={{0,6},{2,4},{4,2},{6,0},{1,7},{3,5},{5,3},{7,1},{8,14},{10,12},{12... | collective-permute-start | bytes 393224 | tf_op jit(solution)/shard_map/ppermute | solution.py:108
  9.2 10.5 %collective-permute-start.3 = (bf16[128,512]{1,0:T(8,128)(2,1)}, bf16[128,512]{1,0:T(8,128)(2,1)S(1)}, u32[]{:S(2)}, u32[]{:S(2)}) collective-permute-start(bf16[128,512]{1,0:T(8,128)(2,1)} %param.7), channel_id=1, source_target_pairs={{0,4},{2,6},{4,0},{6,2},{1,5},{3,7},{5,1},{7,3},{8,12},{10,14},{12... | collective-permute-start | bytes 393224 | tf_op jit(solution)/shard_map/ppermute | solution.py:108
  9.9 1.5 %copy-start.3 = (bf16[128,512]{1,0:T(8,128)(2,1)S(1)}, bf16[128,512]{1,0:T(8,128)(2,1)}, u32[]{:S(2)}) copy-start(bf16[128,512]{1,0:T(8,128)(2,1)} %param.7) | copy-start | bytes 393220
  9.9 3.1 %copy-start.2 = (bf16[128,512]{1,0:T(8,128)(2,1)S(1)}, bf16[128,512]{1,0:T(8,128)(2,1)}, u32[]{:S(2)}) copy-start(bf16[128,512]{1,0:T(8,128)(2,1)} %param.8) | copy-start | bytes 393220
  11.6 16.4 %collective-permute-start.8 = (bf16[512,512]{1,0:T(8,128)(2,1)S(1)}, bf16[512,512]{1,0:T(8,128)(2,1)}, u32[]{:S(2)}, u32[]{:S(2)}) collective-permute-start(bf16[512,512]{1,0:T(8,128)(2,1)S(1)} %constant_dynamic-update-slice_fusion), channel_id=1, source_target_pairs={{0,2},{2,0},{4,6},{6,4},{1,3},{3,1},{5,7},{7,5},{8,10},{10,8},{12,... | collective-permute-start | bytes 1572872 | tf_op jit(solution)/shard_map/ppermute | solution.py:108
  19.8 11.3 %collective-permute-start.7 = (bf16[256,512]{1,0:T(8,128)(2,1)S(1)}, bf16[256,512]{1,0:T(8,128)(2,1)S(1)}, u32[]{:S(2)}, u32[]{:S(2)}) collective-permute-start(bf16[256,512]{1,0:T(8,128)(2,1)S(1)} %pad_maximum_fusion.10), channel_id=1, source_target_pairs={{0,24},{8,16},{16,8},{24,0},{1,25},{9,17},{17,9},{25,1},{2,26},{10... | collective-permute-start | bytes 786440 | tf_op jit(solution)/shard_map/ppermute | solution.py:108
  22.3 11.2 %collective-permute-start.6 = (bf16[256,512]{1,0:T(8,128)(2,1)S(1)}, bf16[256,512]{1,0:T(8,128)(2,1)S(1)}, u32[]{:S(2)}, u32[]{:S(2)}) collective-permute-start(bf16[256,512]{1,0:T(8,128)(2,1)S(1)} %pad_maximum_fusion.10), channel_id=1, source_target_pairs={{0,16},{8,24},{16,0},{24,8},{1,17},{9,25},{17,1},{25,9},{2,18},{10... | collective-permute-start | bytes 786440 | tf_op jit(solution)/shard_map/ppermute | solution.py:108
  22.8 10.8 %collective-permute-start.5 = (bf16[256,512]{1,0:T(8,128)(2,1)S(1)}, bf16[256,512]{1,0:T(8,128)(2,1)S(1)}, u32[]{:S(2)}, u32[]{:S(2)}) collective-permute-start(bf16[256,512]{1,0:T(8,128)(2,1)S(1)} %pad_maximum_fusion.10), channel_id=1, source_target_pairs={{0,8},{8,0},{16,24},{24,16},{1,9},{9,1},{17,25},{25,17},{2,10},{10... | collective-permute-start | bytes 786440 | tf_op jit(solution)/shard_map/ppermute | solution.py:108
  28.0 15.4 %collective-permute-start.15 = (bf16[144,512]{1,0:T(8,128)(2,1)S(1)}, bf16[144,512]{1,0:T(8,128)(2,1)S(1)}, u32[]{:S(2)}, u32[]{:S(2)}) collective-permute-start(bf16[144,512]{1,0:T(8,128)(2,1)S(1)} %pad_maximum_fusion.11), channel_id=1, source_target_pairs={{0,6},{2,4},{4,2},{6,0},{1,7},{3,5},{5,3},{7,1},{8,14},{10,12},{12... | collective-permute-start | bytes 442376 | tf_op jit(solution)/shard_map/ppermute | solution.py:108
  31.1 12.3 %collective-permute-start.14 = (bf16[144,512]{1,0:T(8,128)(2,1)S(1)}, bf16[144,512]{1,0:T(8,128)(2,1)S(1)}, u32[]{:S(2)}, u32[]{:S(2)}) collective-permute-start(bf16[144,512]{1,0:T(8,128)(2,1)S(1)} %pad_maximum_fusion.11), channel_id=1, source_target_pairs={{0,4},{2,6},{4,0},{6,2},{1,5},{3,7},{5,1},{7,3},{8,12},{10,14},{12... | collective-permute-start | bytes 442376 | tf_op jit(solution)/shard_map/ppermute | solution.py:108
  34.8 4.4 %collective-permute-start.12 = (bf16[512,512]{1,0:T(8,128)(2,1)S(1)}, bf16[512,512]{1,0:T(8,128)(2,1)S(1)}, u32[]{:S(2)}, u32[]{:S(2)}) collective-permute-start(bf16[512,512]{1,0:T(8,128)(2,1)S(1)} %pad_maximum_fusion.6.refs_7_), channel_id=1, source_target_pairs={{0,1},{1,0},{2,3},{3,2},{4,5},{5,4},{6,7},{7,6},{8,9},{9,8},{10,11... | collective-permute-start | bytes 1572872 | tf_op jit(solution)/shard_map/ppermute | solution.py:108
  35.0 3.9 %collective-permute-start.11 = (bf16[512,512]{1,0:T(8,128)(2,1)S(1)}, bf16[512,512]{1,0:T(8,128)(2,1)S(1)}, u32[]{:S(2)}, u32[]{:S(2)}) collective-permute-start(bf16[512,512]{1,0:T(8,128)(2,1)S(1)} %pad_maximum_fusion.5.refs_6_), channel_id=1, source_target_pairs={{0,1},{1,0},{2,3},{3,2},{4,5},{5,4},{6,7},{7,6},{8,9},{9,8},{10,11... | collective-permute-start | bytes 1572872 | tf_op jit(solution)/shard_map/ppermute | solution.py:108
  35.6 2.8 %collective-permute-start.10 = (bf16[512,512]{1,0:T(8,128)(2,1)S(1)}, bf16[512,512]{1,0:T(8,128)(2,1)S(1)}, u32[]{:S(2)}, u32[]{:S(2)}) collective-permute-start(bf16[512,512]{1,0:T(8,128)(2,1)S(1)} %pad_maximum_fusion.4.refs_5_), channel_id=1, source_target_pairs={{0,1},{1,0},{2,3},{3,2},{4,5},{5,4},{6,7},{7,6},{8,9},{9,8},{10,11... | collective-permute-start | bytes 1572872 | tf_op jit(solution)/shard_map/ppermute | solution.py:108
  38.3 1.9 %collective-permute-start.9 = (bf16[512,512]{1,0:T(8,128)(2,1)S(1)}, bf16[512,512]{1,0:T(8,128)(2,1)S(1)}, u32[]{:S(2)}, u32[]{:S(2)}) collective-permute-start(bf16[512,512]{1,0:T(8,128)(2,1)S(1)} %pad_maximum_fusion.3.refs_4_), channel_id=1, source_target_pairs={{0,1},{1,0},{2,3},{3,2},{4,5},{5,4},{6,7},{7,6},{8,9},{9,8},{10,11... | collective-permute-start | bytes 1572872 | tf_op jit(solution)/shard_map/ppermute | solution.py:108
  40.7 2.5 %copy-start.1 = (bf16[1,768,512]{2,1,0:T(8,128)(2,1)S(1)}, bf16[1,768,512]{2,1,0:T(8,128)(2,1)}, u32[]{:S(2)}) copy-start(bf16[1,768,512]{2,1,0:T(8,128)(2,1)} %param.13) | copy-start | bytes 2359300
  40.9 11.2 %collective-permute-start.18 = (bf16[192,1024]{1,0:T(8,128)(2,1)S(1)}, bf16[192,1024]{1,0:T(8,128)(2,1)S(1)}, u32[]{:S(2)}, u32[]{:S(2)}) collective-permute-start(bf16[192,1024]{1,0:T(8,128)(2,1)S(1)} %pad_maximum_fusion.7), channel_id=1, source_target_pairs={{0,16},{8,24},{16,0},{24,8},{1,17},{9,25},{17,1},{25,9},{2,18},{10... | collective-permute-start | bytes 1179656 | tf_op jit(solution)/shard_map/ppermute | solution.py:108
  42.4 11.3 %collective-permute-start.17 = (bf16[192,1024]{1,0:T(8,128)(2,1)S(1)}, bf16[192,1024]{1,0:T(8,128)(2,1)S(1)}, u32[]{:S(2)}, u32[]{:S(2)}) collective-permute-start(bf16[192,1024]{1,0:T(8,128)(2,1)S(1)} %pad_maximum_fusion.7), channel_id=1, source_target_pairs={{0,8},{8,0},{16,24},{24,16},{1,9},{9,1},{17,25},{25,17},{2,10},{10... | collective-permute-start | bytes 1179656 | tf_op jit(solution)/shard_map/ppermute | solution.py:108
  43.3 5.4 %collective-permute-start.13 = (bf16[144,512]{1,0:T(8,128)(2,1)S(1)}, bf16[144,512]{1,0:T(8,128)(2,1)S(1)}, u32[]{:S(2)}, u32[]{:S(2)}) collective-permute-start(bf16[144,512]{1,0:T(8,128)(2,1)S(1)} %pad_maximum_fusion.11), channel_id=1, source_target_pairs={{0,2},{2,0},{4,6},{6,4},{1,3},{3,1},{5,7},{7,5},{8,10},{10,8},{12,... | collective-permute-start | bytes 442376 | tf_op jit(solution)/shard_map/ppermute | solution.py:108
  48.8 5.7 %collective-permute-start.16 = (bf16[4,144,512]{2,1,0:T(8,128)(2,1)S(1)}, bf16[4,144,512]{2,1,0:T(8,128)(2,1)S(1)}, u32[]{:S(2)}, u32[]{:S(2)}) collective-permute-start(bf16[4,144,512]{2,1,0:T(8,128)(2,1)S(1)} %pad_maximum_fusion.2), channel_id=1, source_target_pairs={{0,1},{1,0},{2,3},{3,2},{4,5},{5,4},{6,7},{7,6},{8,9},{9,8},{10,11... | collective-permute-start | bytes 1769480 | tf_op jit(solution)/shard_map/ppermute | solution.py:108
  52.2 6.9 %collective-permute-start.20 = (bf16[96,1024]{1,0:T(8,128)(2,1)S(1)}, bf16[96,1024]{1,0:T(8,128)(2,1)S(1)}, u32[]{:S(2)}, u32[]{:S(2)}) collective-permute-start(bf16[96,1024]{1,0:T(8,128)(2,1)S(1)} %slice.159), channel_id=1, source_target_pairs={{0,8},{8,0},{16,24},{24,16},{1,9},{9,1},{17,25},{25,17},{2,10},{10... | collective-permute-start | bytes 589832 | tf_op jit(solution)/shard_map/ppermute | solution.py:108
  53.8 7.1 %collective-permute-start.19 = (bf16[96,1024]{1,0:T(8,128)(2,1)S(1)}, bf16[96,1024]{1,0:T(8,128)(2,1)S(1)}, u32[]{:S(2)}, u32[]{:S(2)}) collective-permute-start(bf16[96,1024]{1,0:T(8,128)(2,1)S(1)} %slice.158), channel_id=1, source_target_pairs={{0,16},{8,24},{16,0},{24,8},{1,17},{9,25},{17,1},{25,9},{2,18},{10... | collective-permute-start | bytes 589832 | tf_op jit(solution)/shard_map/ppermute | solution.py:108
  56.1 6.4 %collective-permute-start.24 = (bf16[96,1024]{1,0:T(8,128)(2,1)S(1)}, bf16[96,1024]{1,0:T(8,128)(2,1)S(1)}, u32[]{:S(2)}, u32[]{:S(2)}) collective-permute-start(bf16[96,1024]{1,0:T(8,128)(2,1)S(1)} %get-tuple-element.85), channel_id=1, source_target_pairs={{0,8},{8,0},{16,24},{24,16},{1,9},{9,1},{17,25},{25,17},{2,10},{10... | collective-permute-start | bytes 589832 | tf_op jit(solution)/shard_map/ppermute | solution.py:108
  57.4 6.5 %collective-permute-start.22 = (bf16[96,1024]{1,0:T(8,128)(2,1)S(1)}, bf16[96,1024]{1,0:T(8,128)(2,1)S(1)}, u32[]{:S(2)}, u32[]{:S(2)}) collective-permute-start(bf16[96,1024]{1,0:T(8,128)(2,1)S(1)} %get-tuple-element.87), channel_id=1, source_target_pairs={{0,16},{8,24},{16,0},{24,8},{1,17},{9,25},{17,1},{25,9},{2,18},{10... | collective-permute-start | bytes 589832 | tf_op jit(solution)/shard_map/ppermute | solution.py:108
  61.6 4.5 %collective-permute-start.21 = (bf16[512,512]{1,0:T(8,128)(2,1)S(1)}, bf16[512,512]{1,0:T(8,128)(2,1)S(1)}, u32[]{:S(2)}, u32[]{:S(2)}) collective-permute-start(bf16[512,512]{1,0:T(8,128)(2,1)S(1)} %fusion.3), channel_id=1, source_target_pairs={{0,1},{1,0},{2,3},{3,2},{4,5},{5,4},{6,7},{7,6},{8,9},{9,8},{10,11... | collective-permute-start | bytes 1572872 | tf_op jit(solution)/shard_map/ppermute | solution.py:108
  64.0 9.8 %collective-permute-start.23 = (bf16[192,1024]{1,0:T(8,128)(2,1)S(1)}, bf16[192,1024]{1,0:T(8,128)(2,1)S(1)}, u32[]{:S(2)}, u32[]{:S(2)}) collective-permute-start(bf16[192,1024]{1,0:T(8,128)(2,1)S(1)} %pad_maximum_fusion.8), channel_id=1, source_target_pairs={{0,8},{8,0},{16,24},{24,16},{1,9},{9,1},{17,25},{25,17},{2,10},{10... | collective-permute-start | bytes 1179656 | tf_op jit(solution)/shard_map/ppermute | solution.py:108
  64.6 9.4 %collective-permute-start.25 = (bf16[192,1024]{1,0:T(8,128)(2,1)S(1)}, bf16[192,1024]{1,0:T(8,128)(2,1)S(1)}, u32[]{:S(2)}, u32[]{:S(2)}) collective-permute-start(bf16[192,1024]{1,0:T(8,128)(2,1)S(1)} %pad_maximum_fusion.9), channel_id=1, source_target_pairs={{0,16},{8,24},{16,0},{24,8},{1,17},{9,25},{17,1},{25,9},{2,18},{10... | collective-permute-start | bytes 1179656 | tf_op jit(solution)/shard_map/ppermute | solution.py:108
  66.8 4.7 %copy-start = (f32[512,512]{1,0:T(8,128)}, f32[512,512]{1,0:T(8,128)S(1)}, u32[]{:S(2)}) copy-start(f32[512,512]{1,0:T(8,128)S(1)} %convert_add_fusion) | copy-start | bytes 3145732
  66.9 10.0 %collective-permute-start.26 = (bf16[128,512]{1,0:T(8,128)(2,1)S(1)}, bf16[128,512]{1,0:T(8,128)(2,1)S(1)}, u32[]{:S(2)}, u32[]{:S(2)}) collective-permute-start(bf16[128,512]{1,0:T(8,128)(2,1)S(1)} %get-tuple-element.102), channel_id=1, source_target_pairs={{0,4},{2,6},{4,0},{6,2},{1,5},{3,7},{5,1},{7,3},{8,12},{10,14},{12... | collective-permute-start | bytes 393224 | tf_op jit(solution)/shard_map/ppermute | solution.py:108
  67.5 9.4 %collective-permute-start.28 = (bf16[128,512]{1,0:T(8,128)(2,1)S(1)}, bf16[128,512]{1,0:T(8,128)(2,1)S(1)}, u32[]{:S(2)}, u32[]{:S(2)}) collective-permute-start(bf16[128,512]{1,0:T(8,128)(2,1)S(1)} %get-tuple-element.103), channel_id=1, source_target_pairs={{0,6},{2,4},{4,2},{6,0},{1,7},{3,5},{5,3},{7,1},{8,14},{10,12},{12... | collective-permute-start | bytes 393224 | tf_op jit(solution)/shard_map/ppermute | solution.py:108
  68.3 8.6 %collective-permute-start.27 = (bf16[128,512]{1,0:T(8,128)(2,1)S(1)}, bf16[128,512]{1,0:T(8,128)(2,1)S(1)}, u32[]{:S(2)}, u32[]{:S(2)}) collective-permute-start(bf16[128,512]{1,0:T(8,128)(2,1)S(1)} %get-tuple-element.104), channel_id=1, source_target_pairs={{0,2},{2,0},{4,6},{6,4},{1,3},{3,1},{5,7},{7,5},{8,10},{10,8},{12,... | collective-permute-start | bytes 393224 | tf_op jit(solution)/shard_map/ppermute | solution.py:108
  74.0 2.9 %slice-start = ((f32[512,512]{1,0:T(8,128)}), f32[128,512]{1,0:T(8,128)S(1)}, s32[]{:S(2)}) async-start(f32[512,512]{1,0:T(8,128)} %copy-done), calls=%async_computation | async-start | bytes 524288 | tf_op jit(solution)/shard_map/slice | solution.py:249

commit v5 on v4

--- a/solution.py
+++ b/solution.py
@@ -143,32 +143,37 @@
     return (activated * up_pre).astype(jnp.bfloat16), up_pre * sig * (1.0 + gate_pre * (1.0 - sig)), activated
 
 
-def in_gradients(place, own_share, sums, factors, parts, parts_there):
+def in_gradients(place, own_share, sums, factors, sides):
     units, width = factors[0].shape
-    quarter = parts[0].shape[1]
+    quarter = sides[0][0].shape[1]
+    rows = sides[0][0].shape[0] // 4
 
     def kernel(place_ref, share_ref, x_ref, y_ref, *refs):
-        factor_refs, part_refs, (gate_ref, up_ref) = refs[:4], refs[4:12], refs[12:]
+        factor_refs, side_refs, (gate_ref, up_ref) = refs[:4], (refs[4:10], refs[10:16]), refs[16:]
         total = share_ref[...] + x_ref[...].astype(jnp.float32) + y_ref[...].astype(jnp.float32)
-        sides = []
+        lefts = []
         for k in range(2):
             side = total[:, k * width : (k + 1) * width]
-            sides.append([(side * factor_refs[2 * k + i][...]).astype(jnp.bfloat16) for i in range(2)])
+            lefts.append([(side * factor_refs[2 * k + i][...]).astype(jnp.bfloat16) for i in range(2)])
         for j in range(4):
             columns = pl.ds(pl.multiple_of((place_ref[0] ^ j) * quarter, quarter), quarter)
+            rights = []
+            for own_ref, near_ref, *far_refs in side_refs:
+                block = pl.ds(j * rows, rows)
+                rights.append(jnp.concatenate([own_ref[block], near_ref[block], far_refs[j][...]], axis=0))
             for i, out_ref in enumerate((gate_ref, up_ref)):
-                value = jnp.dot(sides[0][i], part_refs[j][...], preferred_element_type=jnp.float32)
-                value += jnp.dot(sides[1][i], part_refs[4 + j][...], preferred_element_type=jnp.float32)
+                value = jnp.dot(lefts[0][i], rights[0], preferred_element_type=jnp.float32)
+                value += jnp.dot(lefts[1][i], rights[1], preferred_element_type=jnp.float32)
                 out_ref[:, columns] = value.astype(jnp.bfloat16)
 
     vmem = pl.BlockSpec(memory_space=pltpu.VMEM)
     return pl.pallas_call(
         kernel,
         out_shape=[jax.ShapeDtypeStruct((units, 4 * quarter), jnp.bfloat16)] * 2,
-        in_specs=[pl.BlockSpec(memory_space=pltpu.SMEM)] + [vmem] * 15,
+        in_specs=[pl.BlockSpec(memory_space=pltpu.SMEM)] + [vmem] * 19,
         out_specs=[vmem] * 2,
         compiler_params=pltpu.CompilerParams(vmem_limit_bytes=20 * 2**20),
-    )(place, own_share, *sums, *factors, *parts, *parts_there)
+    )(place, own_share, *sums, *factors, *sides[0], *sides[1])
 
 
 def dense_body(tokens, grad_out, expert_ids, gate_scale, gate_weight, up_weight, down_weight):
@@ -183,6 +188,13 @@
     wide = dict(preferred_element_type=jnp.float32)
     half_type, wide_type = jnp.bfloat16, jnp.float32
 
+    def dot_part(weights, j, part):
+        weights = lax.dynamic_slice_in_dim(weights, (place ^ j) * quarter, quarter, 1)
+        return lax.dot_general(weights, part, contract_last, **wide)
+
+    def block_part(weights, block):
+        return sum(dot_part(weights, j, block[j * rows : (j + 1) * rows]) for j in range(4))
+
     t2, t3 = swap(tokens, "grp", 2), swap(tokens, "grp", 3)
     p0 = [tokens] + spread(tokens)
     in_weights = stack(gate_weight[0], up_weight[0])
@@ -194,25 +206,33 @@
     payload = stack(grad_out, table)
     own = stack(*p0)
     p1 = swap(own, "grp", 1)
-    own, far, payload, in_weights = phase(own, stack(t2, t3), payload, in_weights)
-    p0 = [own[j * rows : (j + 1) * rows] for j in range(4)]
+    own, far, payload, in_weights, *p0 = phase(own, stack(t2, t3), payload, in_weights, *p0)
+    own_there, far_there = to_core(own), to_core(far)
+    pre_own = [block_part(in_weights, block) for block in (own, own_there)]
+    pre_far = [dot_part(in_weights, 0, block) for block in (far, far_there)]
 
     p2 = [far] + spread(far)
+    late, own_there = phase(payload, own_there)
+    g3 = swap(late, "grp", 3)
     late, p1 = phase(payload, p1)
-    g2, g3 = swap(late, "grp", 2), swap(late, "grp", 3)
-    *p2, payload, p1 = phase(*p2, payload, p1)
-
-    parts = [stack(p0[j], p1[j * rows : (j + 1) * rows], p2[j]) for j in range(4)]
-    parts_there = [to_core(p) for p in parts]
+    g2 = swap(late, "grp", 2)
+    p1_there = to_core(p1)
+    pre_near = [block_part(in_weights, block) for block in (p1, p1_there)]
+    values = phase(*p2, payload, p1, p1_there, far_there, *pre_far, *pre_own, *pre_near)
+    p2, (payload, p1, p1_there, far_there), pre_far = values[:4], values[4:8], list(values[8:10])
+    pre_own, pre_near = values[10:12], values[12:]
+
+    p2_there = [far_there] + [to_core(block) for block in p2[1:]]
     acts = []
-    for side in (parts, parts_there):
-        pre = 0.0
-        for j, part in enumerate(side):
-            w_part = lax.dynamic_slice_in_dim(in_weights, (place ^ j) * quarter, quarter, 1)
-            pre = pre + lax.dot_general(w_part, part, contract_last, **wide)
-        acts.append(activate(pre))
-    values = phase(beside(*(a[0] for a in acts)), payload, down_weight, *parts, *parts_there)
-    hidden, payload, down_weight, parts, parts_there = values[0], values[1], values[2], values[3:7], values[7:]
+    for k, (near, far_parts) in enumerate(((p1, p2), (p1_there, p2_there))):
+        for j in (1, 2, 3):
+            pre_far[k] = pre_far[k] + dot_part(in_weights, j, far_parts[j])
+        acts.append([activate(pre) for pre in (pre_own[k], pre_near[k], pre_far[k])])
+    sides = ((own, p1, *p2), (own_there, p1_there, *p2_there))
+    hidden, payload, down_weight, *values = phase(
+        beside(*(a[0] for side in acts for a in side)), payload, down_weight, *sides[0], *sides[1]
+    )
+    sides = (values[:6], values[6:])
 
     hx, hy = swap(hidden, "dp", 1), swap(hidden, "dp", 2)
     down_rows, payload = phase(regroup(down_weight[0], 0, place), payload)
@@ -251,9 +271,9 @@
     down_gradient = jnp.dot(hidden, grads, **wide)
     down_gradient = regroup(down_gradient.astype(half_type), 0, place)
 
-    factors = [f for a in acts for f in a[1:]]
+    factors = [beside(*(a[i] for a in side)) for side in acts for i in (1, 2)]
     gate_gradient, up_gradient = in_gradients(
-        place.reshape(1).astype(jnp.int32), own_share, sums, factors, parts, parts_there
+        place.reshape(1).astype(jnp.int32), own_share, sums, factors, sides
     )
     return (layer_out.astype(half_type), gate_gradient[None], up_gradient[None], down_gradient[None])
 

time: 77.9 us -> 76.8 us (0.986)
  waiting for transfers between devices: 30.2 us -> 25.3 us
  matrix products: 6.52 us -> 9.78 us
  starting transfers between devices: 30 us -> 31.3 us
  local copies, waits for them, and re-layouts: 1.82 us -> 0.65 us
    ppermute x29 -> x31, waiting for transfers between devices: 30.2 us -> 25.3 us  [swap(): return lax.ppermute(value, axis, pairs)]
    dot_general x8 -> x24, matrix products: 3.27 us -> 6.54 us  [dot_part(): return lax.dot_general(weights, part, contract_last, **wide)]
    ppermute x29 -> x31, starting transfers between devices: 30 us -> 31.3 us  [swap(): return lax.ppermute(value, axis, pairs)]
    slice x2 -> x0, local copies, waits for them, and re-layouts: 1.16 us -> none  [the longest x1 1.13 us: dense_body(): parts = [stack(p0[j], p1[j * rows:(j + 1) * rows], p2[j]) for j in range(4)]]
    concatenate x10 -> x6, other arithmetic: 1.75 us -> 1.61 us  [stack(): return jnp.concatenate(values, axis=0)]
  transfers between devices with their start and end apart: 29 -> 31, of which waited for: 16 -> 12; matrix products, arithmetic and copies ran while one was open for 16% -> 20% of each run, Pallas kernels for 4% -> 4%
where the time goes in v5:
time: 76.8 us; the launch traced here: 76.6 us
  starting transfers between devices  31.3 us (41%)
  waiting for transfers between devices  25.3 us (33%)
  matrix products  9.78 us (13%)
  other arithmetic  5.41 us (7%)
  Pallas kernels  2.82 us (4%)
  between operations  1.39 us (2%)
    ppermute x31, starting transfers between devices, swap(): return lax.ppermute(value, axis, pairs)  31.3 us
    ppermute x31, waiting for transfers between devices, swap(): return lax.ppermute(value, axis, pairs)  25.3 us
    dot_general x24, matrix products, dot_part(): return lax.dot_general(weights, part, contract_last, **wide)  6.54 us
    pallas_call x1, Pallas kernels, in_gradients(): pl.pallas_call(kernel, out_shape=[jax.ShapeDtypeStruct((units, 4 * quarte...  2.82 us
    concatenate x6, other arithmetic, stack(): return jnp.concatenate(values, axis=0)  1.61 us
  transfers between devices with their start and end apart: 31, of which 12 were waited for; matrix products, arithmetic and copies ran while one was open for 20% of the time, Pallas kernels for 4%

profile of v5, /device:TPU:0, one launch (start us, length us, event | category | flops | bytes accessed | tf_op | source)
XLA Modules:
  0.0 76.6 jit_solution(3705136323602924633)
XLA Ops:
  0.6 4.1 %collective-permute-start.3 = (bf16[128,512]{1,0:T(8,128)(2,1)}, bf16[128,512]{1,0:T(8,128)(2,1)S(1)}, u32[]{:S(2)}, u32[]{:S(2)}) collective-permute-start(bf16[128,512]{1,0:T(8,128)(2,1)} %param.7), channel_id=1, source_target_pairs={{0,4},{2,6},{4,0},{6,2},{1,5},{3,7},{5,1},{7,3},{8,12},{10,14},{12... | collective-permute-start | bytes 393224 | tf_op jit(solution)/shard_map/ppermute | solution.py:108
  4.7 2.4 %collective-permute-start.2 = (bf16[128,512]{1,0:T(8,128)(2,1)}, bf16[128,512]{1,0:T(8,128)(2,1)S(1)}, u32[]{:S(2)}, u32[]{:S(2)}) collective-permute-start(bf16[128,512]{1,0:T(8,128)(2,1)} %param.7), channel_id=1, source_target_pairs={{0,24},{8,16},{16,8},{24,0},{1,25},{9,17},{17,9},{25,1},{2,26},{10... | collective-permute-start | bytes 393224 | tf_op jit(solution)/shard_map/ppermute | solution.py:108
  7.2 0.5 collective-permute-start.1
  7.7 0.5 collective-permute-start
  8.2 1.3 %collective-permute-start.4 = (bf16[128,512]{1,0:T(8,128)(2,1)}, bf16[128,512]{1,0:T(8,128)(2,1)S(1)}, u32[]{:S(2)}, u32[]{:S(2)}) collective-permute-start(bf16[128,512]{1,0:T(8,128)(2,1)} %param.7), channel_id=1, source_target_pairs={{0,6},{2,4},{4,2},{6,0},{1,7},{3,5},{5,3},{7,1},{8,14},{10,12},{12... | collective-permute-start | bytes 393224 | tf_op jit(solution)/shard_map/ppermute | solution.py:108
  9.6 0.7 select_reduce_fusion
  10.3 1.5 %pad_maximum_fusion = bf16[384,2048]{1,0:T(8,128)(2,1)S(1)} fusion(bf16[192,2048]{1,0:T(8,128)(2,1)} %bitcast.49, bf16[192,2048]{1,0:T(8,128)(2,1)} %bitcast.50), kind=kLoop, calls=%fused_computation.2 | loop fusion | flops 3145728 | bytes 3145728 | tf_op jit(solution)/shard_map/concatenate | solution.py:120
  11.9 1.7 %collective-permute-done = bf16[128,512]{1,0:T(8,128)(2,1)S(1)} collective-permute-done((bf16[128,512]{1,0:T(8,128)(2,1)}, bf16[128,512]{1,0:T(8,128)(2,1)S(1)}, u32[]{:S(2)}, u32[]{:S(2)}) %collective-permute-start) | collective-permute-done | bytes 131104 | tf_op jit(solution)/shard_map/ppermute | solution.py:108
  13.7 1.6 %collective-permute-start.8 = (bf16[512,512]{1,0:T(8,128)(2,1)S(1)}, bf16[512,512]{1,0:T(8,128)(2,1)S(1)}, u32[]{:S(2)}, u32[]{:S(2)}) collective-permute-start(bf16[512,512]{1,0:T(8,128)(2,1)S(1)} %constant_dynamic-update-slice_fusion.refs_4_), channel_id=1, source_target_pairs={{0,2},{2,0},{4,6},{6,4},{1,3},{3,1},{5,7},{7,5},{8,10},{10,8},{12,... | collective-permute-start | bytes 1572872 | tf_op jit(solution)/shard_map/ppermute | solution.py:108
  15.5 3.1 %collective-permute-start.7 = (bf16[256,512]{1,0:T(8,128)(2,1)S(1)}, bf16[256,512]{1,0:T(8,128)(2,1)S(1)}, u32[]{:S(2)}, u32[]{:S(2)}) collective-permute-start(bf16[256,512]{1,0:T(8,128)(2,1)S(1)} %pad_maximum_fusion.9.refs_6_), channel_id=1, source_target_pairs={{0,24},{8,16},{16,8},{24,0},{1,25},{9,17},{17,9},{25,1},{2,26},{10... | collective-permute-start | bytes 786440 | tf_op jit(solution)/shard_map/ppermute | solution.py:108
  18.6 0.6 collective-permute-start.5
  20.3 0.3 fusion.60
  20.7 0.3 fusion.58
  21.0 6.4 %collective-permute-done.8.refs_5_ = bf16[512,512]{1,0:T(8,128)(2,1)S(1)} collective-permute-done((bf16[512,512]{1,0:T(8,128)(2,1)S(1)}, bf16[512,512]{1,0:T(8,128)(2,1)S(1)}, u32[]{:S(2)}, u32[]{:S(2)}) %collective-permute-start.8) | collective-permute-done | bytes 524320 | tf_op jit(solution)/shard_map/ppermute | solution.py:108
  28.3 0.5 collective-permute-start.16
  30.1 3.6 %collective-permute-start.17 = (bf16[144,512]{1,0:T(8,128)(2,1)S(1)}, bf16[144,512]{1,0:T(8,128)(2,1)S(1)}, u32[]{:S(2)}, u32[]{:S(2)}) collective-permute-start(bf16[144,512]{1,0:T(8,128)(2,1)S(1)} %pad_maximum_fusion.10), channel_id=1, source_target_pairs={{0,6},{2,4},{4,2},{6,0},{1,7},{3,5},{5,3},{7,1},{8,14},{10,12},{12... | collective-permute-start | bytes 442376 | tf_op jit(solution)/shard_map/ppermute | solution.py:108
  34.9 0.3 fusion.34
  35.2 0.6 collective-permute-start.12
  36.3 0.3 add_add_fusion.1
  37.1 0.3 fusion.32
  37.7 0.3 add_add_fusion
  38.2 1.6 %collective-permute-start.20 = (bf16[192,1024]{1,0:T(8,128)(2,1)S(1)}, bf16[192,1024]{1,0:T(8,128)(2,1)S(1)}, u32[]{:S(2)}, u32[]{:S(2)}) collective-permute-start(bf16[192,1024]{1,0:T(8,128)(2,1)S(1)} %fusion.79), channel_id=1, source_target_pairs={{0,16},{8,24},{16,0},{24,8},{1,17},{9,25},{17,1},{25,9},{2,18},{10... | collective-permute-start | bytes 1179656 | tf_op jit(solution)/shard_map/ppermute | solution.py:108
  40.2 2.0 %collective-permute-done.16 = bf16[144,512]{1,0:T(8,128)(2,1)S(1)} collective-permute-done((bf16[144,512]{1,0:T(8,128)(2,1)S(1)}, bf16[144,512]{1,0:T(8,128)(2,1)S(1)}, u32[]{:S(2)}, u32[]{:S(2)}) %collective-permute-start.16) | collective-permute-done | bytes 147488 | tf_op jit(solution)/shard_map/ppermute | solution.py:108
  42.2 3.8 %collective-permute-done.15 = bf16[144,512]{1,0:T(8,128)(2,1)S(1)} collective-permute-done((bf16[144,512]{1,0:T(8,128)(2,1)S(1)}, bf16[144,512]{1,0:T(8,128)(2,1)S(1)}, u32[]{:S(2)}, u32[]{:S(2)}) %collective-permute-start.15) | collective-permute-done | bytes 147488 | tf_op jit(solution)/shard_map/ppermute | solution.py:108
  46.2 3.6 %collective-permute-done.20 = bf16[192,1024]{1,0:T(8,128)(2,1)S(1)} collective-permute-done((bf16[192,1024]{1,0:T(8,128)(2,1)S(1)}, bf16[192,1024]{1,0:T(8,128)(2,1)S(1)}, u32[]{:S(2)}, u32[]{:S(2)}) %collective-permute-start.20) | collective-permute-done | bytes 393248 | tf_op jit(solution)/shard_map/ppermute | solution.py:108
  49.8 1.5 %collective-permute-start.22 = (bf16[96,1024]{1,0:T(8,128)(2,1)S(1)}, bf16[96,1024]{1,0:T(8,128)(2,1)S(1)}, u32[]{:S(2)}, u32[]{:S(2)}) collective-permute-start(bf16[96,1024]{1,0:T(8,128)(2,1)S(1)} %slice.231), channel_id=1, source_target_pairs={{0,8},{8,0},{16,24},{24,16},{1,9},{9,1},{17,25},{25,17},{2,10},{10... | collective-permute-start | bytes 589832 | tf_op jit(solution)/shard_map/ppermute | solution.py:108
  51.4 0.4 collective-permute-start.21
  51.9 0.3 fusion
  52.2 1.0 %fusion.119 = (bf16[768,1024]{1,0:T(8,128)(2,1)S(1)}, f32[768,1024]{1,0:T(8,128)S(1)}) fusion(bf16[768,512]{1,0:T(8,128)(2,1)S(1)} %pad_maximum_fusion.1, bf16[1024,512]{1,0:T(8,128)(2,1)S(1)} %fusion), kind=kOutput, calls=%fused_computation.192 | convolution fusion | flops 806092800 | bytes 6553600 | tf_op jit(solution)/shard_map/dot_general | solution.py:248
  53.3 1.8 %collective-permute-start.26 = (bf16[96,1024]{1,0:T(8,128)(2,1)S(1)}, bf16[96,1024]{1,0:T(8,128)(2,1)S(1)}, u32[]{:S(2)}, u32[]{:S(2)}) collective-permute-start(bf16[96,1024]{1,0:T(8,128)(2,1)S(1)} %get-tuple-element.113), channel_id=1, source_target_pairs={{0,8},{8,0},{16,24},{24,16},{1,9},{9,1},{17,25},{25,17},{2,10},{10... | collective-permute-start | bytes 589832 | tf_op jit(solution)/shard_map/ppermute | solution.py:108
  55.1 0.5 collective-permute-start.24
  55.7 1.6 %collective-permute-done.22 = bf16[96,1024]{1,0:T(8,128)(2,1)S(1)} collective-permute-done((bf16[96,1024]{1,0:T(8,128)(2,1)S(1)}, bf16[96,1024]{1,0:T(8,128)(2,1)S(1)}, u32[]{:S(2)}, u32[]{:S(2)}) %collective-permute-start.22) | collective-permute-done | bytes 196640 | tf_op jit(solution)/shard_map/ppermute | solution.py:108
  57.4 1.3 %collective-permute-done.21 = bf16[96,1024]{1,0:T(8,128)(2,1)S(1)} collective-permute-done((bf16[96,1024]{1,0:T(8,128)(2,1)S(1)}, bf16[96,1024]{1,0:T(8,128)(2,1)S(1)}, u32[]{:S(2)}, u32[]{:S(2)}) %collective-permute-start.21) | collective-permute-done | bytes 196640 | tf_op jit(solution)/shard_map/ppermute | solution.py:108
  58.8 0.6 fusion.3
  59.6 1.0 %collective-permute-done.26 = bf16[96,1024]{1,0:T(8,128)(2,1)S(1)} collective-permute-done((bf16[96,1024]{1,0:T(8,128)(2,1)S(1)}, bf16[96,1024]{1,0:T(8,128)(2,1)S(1)}, u32[]{:S(2)}, u32[]{:S(2)}) %collective-permute-start.26) | collective-permute-done | bytes 196640 | tf_op jit(solution)/shard_map/ppermute | solution.py:108
  60.6 1.3 %collective-permute-done.24 = bf16[96,1024]{1,0:T(8,128)(2,1)S(1)} collective-permute-done((bf16[96,1024]{1,0:T(8,128)(2,1)S(1)}, bf16[96,1024]{1,0:T(8,128)(2,1)S(1)}, u32[]{:S(2)}, u32[]{:S(2)}) %collective-permute-start.24) | collective-permute-done | bytes 196640 | tf_op jit(solution)/shard_map/ppermute | solution.py:108
  62.0 0.6 collective-permute-start.25
  62.6 1.6 %collective-permute-start.27 = (bf16[192,1024]{1,0:T(8,128)(2,1)S(1)}, bf16[192,1024]{1,0:T(8,128)(2,1)S(1)}, u32[]{:S(2)}, u32[]{:S(2)}) collective-permute-start(bf16[192,1024]{1,0:T(8,128)(2,1)S(1)} %pad_maximum_fusion.4), channel_id=1, source_target_pairs={{0,16},{8,24},{16,0},{24,8},{1,17},{9,25},{17,1},{25,9},{2,18},{10... | collective-permute-start | bytes 1179656 | tf_op jit(solution)/shard_map/ppermute | solution.py:108
  64.2 0.6 convert_add_fusion
  65.0 1.9 %collective-permute-start.30 = (bf16[128,512]{1,0:T(8,128)(2,1)S(1)}, bf16[128,512]{1,0:T(8,128)(2,1)S(1)}, u32[]{:S(2)}, u32[]{:S(2)}) collective-permute-start(bf16[128,512]{1,0:T(8,128)(2,1)S(1)} %get-tuple-element.125), channel_id=1, source_target_pairs={{0,6},{2,4},{4,2},{6,0},{1,7},{3,5},{5,3},{7,1},{8,14},{10,12},{12... | collective-permute-start | bytes 393224 | tf_op jit(solution)/shard_map/ppermute | solution.py:108
  67.0 1.5 %collective-permute-start.29 = (bf16[128,512]{1,0:T(8,128)(2,1)S(1)}, bf16[128,512]{1,0:T(8,128)(2,1)S(1)}, u32[]{:S(2)}, u32[]{:S(2)}) collective-permute-start(bf16[128,512]{1,0:T(8,128)(2,1)S(1)} %get-tuple-element.126), channel_id=1, source_target_pairs={{0,2},{2,0},{4,6},{6,4},{1,3},{3,1},{5,7},{7,5},{8,10},{10,8},{12,... | collective-permute-start | bytes 393224 | tf_op jit(solution)/shard_map/ppermute | solution.py:108
  68.5 1.0 %convolution_convert_fusion = bf16[768,512]{1,0:T(8,128)(2,1)S(1)} fusion(bf16[768,1024]{1,0:T(8,128)(2,1)S(1)} %constant_dynamic-update-slice_fusion.9, bf16[1024,512]{1,0:T(8,128)(2,1)S(1)} %fusion), kind=kOutput, calls=%fused_computation.3 | convolution fusion | flops 805699584 | bytes 3407872 | tf_op jit(solution)/shard_map/dot_general | solution.py:271
  69.6 0.9 %maximum_bitcast_fusion = bf16[1,768,512]{2,1,0:T(8,128)(2,1)} fusion(bf16[192,512]{1,0:T(8,128)(2,1)S(1)} %get-tuple-element.117, bf16[192,512]{1,0:T(8,128)(2,1)S(1)} %get-tuple-element.118, bf16[192,512]{1,0:T(8,128)(2,1)S(1)} %get-tuple-element.119, bf16[192,512]{1,0:T(8,128)(2,1)S(1)} %get-tuple-element.116), kind=kLoop, calls=%fused_computation.27 | loop fusion | flops 3145728 | bytes 1572864 | tf_op jit(solution)/shard_map/broadcast_in_dim | solution.py:278
  70.5 1.6 %collective-permute-done.25.x_ref = bf16[192,1024]{1,0:T(8,128)(2,1)S(1)} collective-permute-done((bf16[192,1024]{1,0:T(8,128)(2,1)S(1)}, bf16[192,1024]{1,0:T(8,128)(2,1)S(1)}, u32[]{:S(2)}, u32[]{:S(2)}) %collective-permute-start.25) | collective-permute-done | bytes 393248 | tf_op jit(solution)/shard_map/ppermute | solution.py:108
  72.1 0.4 collective-permute-done.27.y_ref
  72.5 2.8 %shard_map.102 = (bf16[192,2048]{1,0:T(8,128)(2,1)}, bf16[192,2048]{1,0:T(8,128)(2,1)}) custom-call(s32[1]{0:T(128)} %bitcast.15.place_ref, f32[192,1024]{1,0:T(8,128)S(1)} %slice.229.share_ref, bf16[192,1024]{1,0:T(8,128)(2,1)S(1)} %collective-permute-done.25.x_ref, bf16[192,1024]{1,0:T(8,128)(2,1)S(1)} %collective-permute-done.27.y_ref, ...), custom_call_target="tpu_custom_call" | custom-call | tf_op jit(solution)/shard_map/pallas_call | solution.py:170
  75.3 0.6 collective-permute-done.29
  75.9 0.7 add_convert_fusion
  (107 shorter events, 7.5 us)
Async XLA Ops:
  0.6 14.8 %collective-permute-start.3 = (bf16[128,512]{1,0:T(8,128)(2,1)}, bf16[128,512]{1,0:T(8,128)(2,1)S(1)}, u32[]{:S(2)}, u32[]{:S(2)}) collective-permute-start(bf16[128,512]{1,0:T(8,128)(2,1)} %param.7), channel_id=1, source_target_pairs={{0,4},{2,6},{4,0},{6,2},{1,5},{3,7},{5,1},{7,3},{8,12},{10,14},{12... | collective-permute-start | bytes 393224 | tf_op jit(solution)/shard_map/ppermute | solution.py:108
  4.7 9.0 %collective-permute-start.2 = (bf16[128,512]{1,0:T(8,128)(2,1)}, bf16[128,512]{1,0:T(8,128)(2,1)S(1)}, u32[]{:S(2)}, u32[]{:S(2)}) collective-permute-start(bf16[128,512]{1,0:T(8,128)(2,1)} %param.7), channel_id=1, source_target_pairs={{0,24},{8,16},{16,8},{24,0},{1,25},{9,17},{17,9},{25,1},{2,26},{10... | collective-permute-start | bytes 393224 | tf_op jit(solution)/shard_map/ppermute | solution.py:108
  7.2 6.5 %collective-permute-start.1 = (bf16[128,512]{1,0:T(8,128)(2,1)}, bf16[128,512]{1,0:T(8,128)(2,1)S(1)}, u32[]{:S(2)}, u32[]{:S(2)}) collective-permute-start(bf16[128,512]{1,0:T(8,128)(2,1)} %param.7), channel_id=1, source_target_pairs={{0,16},{8,24},{16,0},{24,8},{1,17},{9,25},{17,1},{25,9},{2,18},{10... | collective-permute-start | bytes 393224 | tf_op jit(solution)/shard_map/ppermute | solution.py:108
  7.7 6.0 %collective-permute-start = (bf16[128,512]{1,0:T(8,128)(2,1)}, bf16[128,512]{1,0:T(8,128)(2,1)S(1)}, u32[]{:S(2)}, u32[]{:S(2)}) collective-permute-start(bf16[128,512]{1,0:T(8,128)(2,1)} %param.7), channel_id=1, source_target_pairs={{0,8},{8,0},{16,24},{24,16},{1,9},{9,1},{17,25},{25,17},{2,10},{10... | collective-permute-start | bytes 393224 | tf_op jit(solution)/shard_map/ppermute | solution.py:108
  8.2 7.2 %collective-permute-start.4 = (bf16[128,512]{1,0:T(8,128)(2,1)}, bf16[128,512]{1,0:T(8,128)(2,1)S(1)}, u32[]{:S(2)}, u32[]{:S(2)}) collective-permute-start(bf16[128,512]{1,0:T(8,128)(2,1)} %param.7), channel_id=1, source_target_pairs={{0,6},{2,4},{4,2},{6,0},{1,7},{3,5},{5,3},{7,1},{8,14},{10,12},{12... | collective-permute-start | bytes 393224 | tf_op jit(solution)/shard_map/ppermute | solution.py:108
  10.3 1.5 %copy-start.2 = (bf16[128,512]{1,0:T(8,128)(2,1)S(1)}, bf16[128,512]{1,0:T(8,128)(2,1)}, u32[]{:S(2)}) copy-start(bf16[128,512]{1,0:T(8,128)(2,1)} %param.8) | copy-start | bytes 393220
  10.3 1.6 %copy-start.3 = (bf16[128,512]{1,0:T(8,128)(2,1)S(1)}, bf16[128,512]{1,0:T(8,128)(2,1)}, u32[]{:S(2)}) copy-start(bf16[128,512]{1,0:T(8,128)(2,1)} %param.7) | copy-start | bytes 393220
  13.7 13.6 %collective-permute-start.8 = (bf16[512,512]{1,0:T(8,128)(2,1)S(1)}, bf16[512,512]{1,0:T(8,128)(2,1)S(1)}, u32[]{:S(2)}, u32[]{:S(2)}) collective-permute-start(bf16[512,512]{1,0:T(8,128)(2,1)S(1)} %constant_dynamic-update-slice_fusion.refs_4_), channel_id=1, source_target_pairs={{0,2},{2,0},{4,6},{6,4},{1,3},{3,1},{5,7},{7,5},{8,10},{10,8},{12,... | collective-permute-start | bytes 1572872 | tf_op jit(solution)/shard_map/ppermute | solution.py:108
  15.4 5.2 %collective-permute-start.10 = (bf16[256,512]{1,0:T(8,128)(2,1)S(1)}, bf16[256,512]{1,0:T(8,128)(2,1)S(1)}, u32[]{:S(2)}, u32[]{:S(2)}) collective-permute-start(bf16[256,512]{1,0:T(8,128)(2,1)S(1)} %pad_maximum_fusion.9.refs_6_), channel_id=1, source_target_pairs={{0,1},{1,0},{2,3},{3,2},{4,5},{5,4},{6,7},{7,6},{8,9},{9,8},{10,11... | collective-permute-start | bytes 786440 | tf_op jit(solution)/shard_map/ppermute | solution.py:108
  15.5 19.3 %collective-permute-start.7 = (bf16[256,512]{1,0:T(8,128)(2,1)S(1)}, bf16[256,512]{1,0:T(8,128)(2,1)S(1)}, u32[]{:S(2)}, u32[]{:S(2)}) collective-permute-start(bf16[256,512]{1,0:T(8,128)(2,1)S(1)} %pad_maximum_fusion.9.refs_6_), channel_id=1, source_target_pairs={{0,24},{8,16},{16,8},{24,0},{1,25},{9,17},{17,9},{25,1},{2,26},{10... | collective-permute-start | bytes 786440 | tf_op jit(solution)/shard_map/ppermute | solution.py:108
  18.6 16.2 %collective-permute-start.6 = (bf16[256,512]{1,0:T(8,128)(2,1)S(1)}, bf16[256,512]{1,0:T(8,128)(2,1)S(1)}, u32[]{:S(2)}, u32[]{:S(2)}) collective-permute-start(bf16[256,512]{1,0:T(8,128)(2,1)S(1)} %pad_maximum_fusion.9.refs_6_), channel_id=1, source_target_pairs={{0,16},{8,24},{16,0},{24,8},{1,17},{9,25},{17,1},{25,9},{2,18},{10... | collective-permute-start | bytes 786440 | tf_op jit(solution)/shard_map/ppermute | solution.py:108
  18.6 16.2 %collective-permute-start.5 = (bf16[256,512]{1,0:T(8,128)(2,1)S(1)}, bf16[256,512]{1,0:T(8,128)(2,1)S(1)}, u32[]{:S(2)}, u32[]{:S(2)}) collective-permute-start(bf16[256,512]{1,0:T(8,128)(2,1)S(1)} %pad_maximum_fusion.9.refs_6_), channel_id=1, source_target_pairs={{0,8},{8,0},{16,24},{24,16},{1,9},{9,1},{17,25},{25,17},{2,10},{10... | collective-permute-start | bytes 786440 | tf_op jit(solution)/shard_map/ppermute | solution.py:108
  20.6 7.6 %collective-permute-start.11 = (bf16[512,512]{1,0:T(8,128)(2,1)S(1)}, bf16[512,512]{1,0:T(8,128)(2,1)S(1)}, u32[]{:S(2)}, u32[]{:S(2)}) collective-permute-start(bf16[512,512]{1,0:T(8,128)(2,1)S(1)} %constant_dynamic-update-slice_fusion.refs_4_), channel_id=1, source_target_pairs={{0,1},{1,0},{2,3},{3,2},{4,5},{5,4},{6,7},{7,6},{8,9},{9,8},{10,11... | collective-permute-start | bytes 1572872 | tf_op jit(solution)/shard_map/ppermute | solution.py:108
  27.6 2.5 %collective-permute-start.9 = (bf16[512,512]{1,0:T(8,128)(2,1)S(1)}, bf16[512,512]{1,0:T(8,128)(2,1)S(1)}, u32[]{:S(2)}, u32[]{:S(2)}) collective-permute-start(bf16[512,512]{1,0:T(8,128)(2,1)S(1)} %collective-permute-done.8.refs_5_), channel_id=1, source_target_pairs={{0,1},{1,0},{2,3},{3,2},{4,5},{5,4},{6,7},{7,6},{8,9},{9,8},{10,11... | collective-permute-start | bytes 1572872 | tf_op jit(solution)/shard_map/ppermute | solution.py:108
  28.3 13.9 %collective-permute-start.16 = (bf16[144,512]{1,0:T(8,128)(2,1)S(1)}, bf16[144,512]{1,0:T(8,128)(2,1)S(1)}, u32[]{:S(2)}, u32[]{:S(2)}) collective-permute-start(bf16[144,512]{1,0:T(8,128)(2,1)S(1)} %pad_maximum_fusion.10), channel_id=1, source_target_pairs={{0,4},{2,6},{4,0},{6,2},{1,5},{3,7},{5,1},{7,3},{8,12},{10,14},{12... | collective-permute-start | bytes 442376 | tf_op jit(solution)/shard_map/ppermute | solution.py:108
  30.1 12.1 %collective-permute-start.17 = (bf16[144,512]{1,0:T(8,128)(2,1)S(1)}, bf16[144,512]{1,0:T(8,128)(2,1)S(1)}, u32[]{:S(2)}, u32[]{:S(2)}) collective-permute-start(bf16[144,512]{1,0:T(8,128)(2,1)S(1)} %pad_maximum_fusion.10), channel_id=1, source_target_pairs={{0,6},{2,4},{4,2},{6,0},{1,7},{3,5},{5,3},{7,1},{8,14},{10,12},{12... | collective-permute-start | bytes 442376 | tf_op jit(solution)/shard_map/ppermute | solution.py:108
  34.8 2.3 %collective-permute-start.13 = (bf16[256,512]{1,0:T(8,128)(2,1)S(1)}, bf16[256,512]{1,0:T(8,128)(2,1)S(1)}, u32[]{:S(2)}, u32[]{:S(2)}) collective-permute-start(bf16[256,512]{1,0:T(8,128)(2,1)S(1)} %collective-permute-done.6.refs_8_), channel_id=1, source_target_pairs={{0,1},{1,0},{2,3},{3,2},{4,5},{5,4},{6,7},{7,6},{8,9},{9,8},{10,11... | collective-permute-start | bytes 786440 | tf_op jit(solution)/shard_map/ppermute | solution.py:108
  35.2 2.2 %collective-permute-start.12 = (bf16[256,512]{1,0:T(8,128)(2,1)S(1)}, bf16[256,512]{1,0:T(8,128)(2,1)S(1)}, u32[]{:S(2)}, u32[]{:S(2)}) collective-permute-start(bf16[256,512]{1,0:T(8,128)(2,1)S(1)} %collective-permute-done.5.refs_7_), channel_id=1, source_target_pairs={{0,1},{1,0},{2,3},{3,2},{4,5},{5,4},{6,7},{7,6},{8,9},{9,8},{10,11... | collective-permute-start | bytes 786440 | tf_op jit(solution)/shard_map/ppermute | solution.py:108
  36.0 1.7 %collective-permute-start.14 = (bf16[256,512]{1,0:T(8,128)(2,1)S(1)}, bf16[256,512]{1,0:T(8,128)(2,1)S(1)}, u32[]{:S(2)}, u32[]{:S(2)}) collective-permute-start(bf16[256,512]{1,0:T(8,128)(2,1)S(1)} %collective-permute-done.7.refs_9_), channel_id=1, source_target_pairs={{0,1},{1,0},{2,3},{3,2},{4,5},{5,4},{6,7},{7,6},{8,9},{9,8},{10,11... | collective-permute-start | bytes 786440 | tf_op jit(solution)/shard_map/ppermute | solution.py:108
  37.7 2.1 %copy-start.1 = (bf16[1,768,512]{2,1,0:T(8,128)(2,1)S(1)}, bf16[1,768,512]{2,1,0:T(8,128)(2,1)}, u32[]{:S(2)}) copy-start(bf16[1,768,512]{2,1,0:T(8,128)(2,1)} %param.13) | copy-start | bytes 2359300
  38.2 11.6 %collective-permute-start.20 = (bf16[192,1024]{1,0:T(8,128)(2,1)S(1)}, bf16[192,1024]{1,0:T(8,128)(2,1)S(1)}, u32[]{:S(2)}, u32[]{:S(2)}) collective-permute-start(bf16[192,1024]{1,0:T(8,128)(2,1)S(1)} %fusion.79), channel_id=1, source_target_pairs={{0,16},{8,24},{16,0},{24,8},{1,17},{9,25},{17,1},{25,9},{2,18},{10... | collective-permute-start | bytes 1179656 | tf_op jit(solution)/shard_map/ppermute | solution.py:108
  39.8 11.6 %collective-permute-start.19 = (bf16[192,1024]{1,0:T(8,128)(2,1)S(1)}, bf16[192,1024]{1,0:T(8,128)(2,1)S(1)}, u32[]{:S(2)}, u32[]{:S(2)}) collective-permute-start(bf16[192,1024]{1,0:T(8,128)(2,1)S(1)} %fusion.79), channel_id=1, source_target_pairs={{0,8},{8,0},{16,24},{24,16},{1,9},{9,1},{17,25},{25,17},{2,10},{10... | collective-permute-start | bytes 1179656 | tf_op jit(solution)/shard_map/ppermute | solution.py:108
  39.9 6.0 %collective-permute-start.15 = (bf16[144,512]{1,0:T(8,128)(2,1)S(1)}, bf16[144,512]{1,0:T(8,128)(2,1)S(1)}, u32[]{:S(2)}, u32[]{:S(2)}) collective-permute-start(bf16[144,512]{1,0:T(8,128)(2,1)S(1)} %pad_maximum_fusion.10), channel_id=1, source_target_pairs={{0,2},{2,0},{4,6},{6,4},{1,3},{3,1},{5,7},{7,5},{8,10},{10,8},{12,... | collective-permute-start | bytes 442376 | tf_op jit(solution)/shard_map/ppermute | solution.py:108
  46.1 5.7 %collective-permute-start.18 = (bf16[4,144,512]{2,1,0:T(8,128)(2,1)S(1)}, bf16[4,144,512]{2,1,0:T(8,128)(2,1)S(1)}, u32[]{:S(2)}, u32[]{:S(2)}) collective-permute-start(bf16[4,144,512]{2,1,0:T(8,128)(2,1)S(1)} %pad_maximum_fusion.2), channel_id=1, source_target_pairs={{0,1},{1,0},{2,3},{3,2},{4,5},{5,4},{6,7},{7,6},{8,9},{9,8},{10,11... | collective-permute-start | bytes 1769480 | tf_op jit(solution)/shard_map/ppermute | solution.py:108
  49.8 7.6 %collective-permute-start.22 = (bf16[96,1024]{1,0:T(8,128)(2,1)S(1)}, bf16[96,1024]{1,0:T(8,128)(2,1)S(1)}, u32[]{:S(2)}, u32[]{:S(2)}) collective-permute-start(bf16[96,1024]{1,0:T(8,128)(2,1)S(1)} %slice.231), channel_id=1, source_target_pairs={{0,8},{8,0},{16,24},{24,16},{1,9},{9,1},{17,25},{25,17},{2,10},{10... | collective-permute-start | bytes 589832 | tf_op jit(solution)/shard_map/ppermute | solution.py:108
  51.4 7.3 %collective-permute-start.21 = (bf16[96,1024]{1,0:T(8,128)(2,1)S(1)}, bf16[96,1024]{1,0:T(8,128)(2,1)S(1)}, u32[]{:S(2)}, u32[]{:S(2)}) collective-permute-start(bf16[96,1024]{1,0:T(8,128)(2,1)S(1)} %slice.230), channel_id=1, source_target_pairs={{0,16},{8,24},{16,0},{24,8},{1,17},{9,25},{17,1},{25,9},{2,18},{10... | collective-permute-start | bytes 589832 | tf_op jit(solution)/shard_map/ppermute | solution.py:108
  53.3 7.3 %collective-permute-start.26 = (bf16[96,1024]{1,0:T(8,128)(2,1)S(1)}, bf16[96,1024]{1,0:T(8,128)(2,1)S(1)}, u32[]{:S(2)}, u32[]{:S(2)}) collective-permute-start(bf16[96,1024]{1,0:T(8,128)(2,1)S(1)} %get-tuple-element.113), channel_id=1, source_target_pairs={{0,8},{8,0},{16,24},{24,16},{1,9},{9,1},{17,25},{25,17},{2,10},{10... | collective-permute-start | bytes 589832 | tf_op jit(solution)/shard_map/ppermute | solution.py:108
  55.1 6.7 %collective-permute-start.24 = (bf16[96,1024]{1,0:T(8,128)(2,1)S(1)}, bf16[96,1024]{1,0:T(8,128)(2,1)S(1)}, u32[]{:S(2)}, u32[]{:S(2)}) collective-permute-start(bf16[96,1024]{1,0:T(8,128)(2,1)S(1)} %get-tuple-element.115), channel_id=1, source_target_pairs={{0,16},{8,24},{16,0},{24,8},{1,17},{9,25},{17,1},{25,9},{2,18},{10... | collective-permute-start | bytes 589832 | tf_op jit(solution)/shard_map/ppermute | solution.py:108
  59.5 4.8 %collective-permute-start.23 = (bf16[512,512]{1,0:T(8,128)(2,1)S(1)}, bf16[512,512]{1,0:T(8,128)(2,1)S(1)}, u32[]{:S(2)}, u32[]{:S(2)}) collective-permute-start(bf16[512,512]{1,0:T(8,128)(2,1)S(1)} %fusion.3), channel_id=1, source_target_pairs={{0,1},{1,0},{2,3},{3,2},{4,5},{5,4},{6,7},{7,6},{8,9},{9,8},{10,11... | collective-permute-start | bytes 1572872 | tf_op jit(solution)/shard_map/ppermute | solution.py:108
  62.0 10.1 %collective-permute-start.25 = (bf16[192,1024]{1,0:T(8,128)(2,1)S(1)}, bf16[192,1024]{1,0:T(8,128)(2,1)S(1)}, u32[]{:S(2)}, u32[]{:S(2)}) collective-permute-start(bf16[192,1024]{1,0:T(8,128)(2,1)S(1)} %pad_maximum_fusion.3), channel_id=1, source_target_pairs={{0,8},{8,0},{16,24},{24,16},{1,9},{9,1},{17,25},{25,17},{2,10},{10... | collective-permute-start | bytes 1179656 | tf_op jit(solution)/shard_map/ppermute | solution.py:108
  62.6 9.8 %collective-permute-start.27 = (bf16[192,1024]{1,0:T(8,128)(2,1)S(1)}, bf16[192,1024]{1,0:T(8,128)(2,1)S(1)}, u32[]{:S(2)}, u32[]{:S(2)}) collective-permute-start(bf16[192,1024]{1,0:T(8,128)(2,1)S(1)} %pad_maximum_fusion.4), channel_id=1, source_target_pairs={{0,16},{8,24},{16,0},{24,8},{1,17},{9,25},{17,1},{25,9},{2,18},{10... | collective-permute-start | bytes 1179656 | tf_op jit(solution)/shard_map/ppermute | solution.py:108
  64.8 4.7 %copy-start = (f32[512,512]{1,0:T(8,128)}, f32[512,512]{1,0:T(8,128)S(1)}, u32[]{:S(2)}) copy-start(f32[512,512]{1,0:T(8,128)S(1)} %convert_add_fusion) | copy-start | bytes 3145732
  65.0 10.3 %collective-permute-start.28 = (bf16[128,512]{1,0:T(8,128)(2,1)S(1)}, bf16[128,512]{1,0:T(8,128)(2,1)S(1)}, u32[]{:S(2)}, u32[]{:S(2)}) collective-permute-start(bf16[128,512]{1,0:T(8,128)(2,1)S(1)} %get-tuple-element.124), channel_id=1, source_target_pairs={{0,4},{2,6},{4,0},{6,2},{1,5},{3,7},{5,1},{7,3},{8,12},{10,14},{12... | collective-permute-start | bytes 393224 | tf_op jit(solution)/shard_map/ppermute | solution.py:108
  65.0 10.3 %collective-permute-start.30 = (bf16[128,512]{1,0:T(8,128)(2,1)S(1)}, bf16[128,512]{1,0:T(8,128)(2,1)S(1)}, u32[]{:S(2)}, u32[]{:S(2)}) collective-permute-start(bf16[128,512]{1,0:T(8,128)(2,1)S(1)} %get-tuple-element.125), channel_id=1, source_target_pairs={{0,6},{2,4},{4,2},{6,0},{1,7},{3,5},{5,3},{7,1},{8,14},{10,12},{12... | collective-permute-start | bytes 393224 | tf_op jit(solution)/shard_map/ppermute | solution.py:108
  67.0 8.9 %collective-permute-start.29 = (bf16[128,512]{1,0:T(8,128)(2,1)S(1)}, bf16[128,512]{1,0:T(8,128)(2,1)S(1)}, u32[]{:S(2)}, u32[]{:S(2)}) collective-permute-start(bf16[128,512]{1,0:T(8,128)(2,1)S(1)} %get-tuple-element.126), channel_id=1, source_target_pairs={{0,2},{2,0},{4,6},{6,4},{1,3},{3,1},{5,7},{7,5},{8,10},{10,8},{12,... | collective-permute-start | bytes 393224 | tf_op jit(solution)/shard_map/ppermute | solution.py:108
  72.5 3.4 %slice-start = ((f32[512,512]{1,0:T(8,128)}), f32[128,512]{1,0:T(8,128)S(1)}, s32[]{:S(2)}) async-start(f32[512,512]{1,0:T(8,128)} %copy-done), calls=%async_computation | async-start | bytes 524288 | tf_op jit(solution)/shard_map/slice | solution.py:269

commit v6 on v5

--- a/solution.py
+++ b/solution.py
@@ -214,7 +214,7 @@
     p2 = [far] + spread(far)
     late, own_there = phase(payload, own_there)
     g3 = swap(late, "grp", 3)
-    late, p1 = phase(payload, p1)
+    late, p1, *pre_own = phase(payload, p1, *pre_own)
     g2 = swap(late, "grp", 2)
     p1_there = to_core(p1)
     pre_near = [block_part(in_weights, block) for block in (p1, p1_there)]

time: 76.8 us -> 76.2 us (level)
  waiting for transfers between devices: 25.3 us -> 23.8 us
  starting transfers between devices: 31.3 us -> 32.2 us
    ppermute x31, waiting for transfers between devices: 25.3 us -> 23.8 us  [swap(): return lax.ppermute(value, axis, pairs)]
    ppermute x31, starting transfers between devices: 31.3 us -> 32.2 us  [swap(): return lax.ppermute(value, axis, pairs)]
  transfers between devices with their start and end apart: 31 -> 31, of which waited for: 12 -> 13; matrix products, arithmetic and copies ran while one was open for 20% -> 20% of each run, Pallas kernels for 4% -> 4%
where the time goes in v6:
time: 76.2 us; the launch traced here: 76 us
  starting transfers between devices  32.2 us (42%)
  waiting for transfers between devices  23.8 us (31%)
  matrix products  9.74 us (13%)
  other arithmetic  5.41 us (7%)
  Pallas kernels  2.82 us (4%)
  between operations  1.39 us (2%)
    ppermute x31, starting transfers between devices, swap(): return lax.ppermute(value, axis, pairs)  32.2 us
    ppermute x31, waiting for transfers between devices, swap(): return lax.ppermute(value, axis, pairs)  23.8 us
    dot_general x24, matrix products, dot_part(): return lax.dot_general(weights, part, contract_last, **wide)  6.5 us
    pallas_call x1, Pallas kernels, in_gradients(): pl.pallas_call(kernel, out_shape=[jax.ShapeDtypeStruct((units, 4 * quarte...  2.82 us
    concatenate x6, other arithmetic, stack(): return jnp.concatenate(values, axis=0)  1.61 us
  transfers between devices with their start and end apart: 31, of which 13 were waited for; matrix products, arithmetic and copies ran while one was open for 20% of the time, Pallas kernels for 4%

profile of v6, /device:TPU:0, one launch (start us, length us, event | category | flops | bytes accessed | tf_op | source)
XLA Modules:
  0.0 76.0 jit_solution(826800985878122996)
XLA Ops:
  0.6 4.1 %collective-permute-start.3 = (bf16[128,512]{1,0:T(8,128)(2,1)}, bf16[128,512]{1,0:T(8,128)(2,1)S(1)}, u32[]{:S(2)}, u32[]{:S(2)}) collective-permute-start(bf16[128,512]{1,0:T(8,128)(2,1)} %param.7), channel_id=1, source_target_pairs={{0,4},{2,6},{4,0},{6,2},{1,5},{3,7},{5,1},{7,3},{8,12},{10,14},{12... | collective-permute-start | bytes 393224 | tf_op jit(solution)/shard_map/ppermute | solution.py:108
  4.7 2.4 %collective-permute-start.2 = (bf16[128,512]{1,0:T(8,128)(2,1)}, bf16[128,512]{1,0:T(8,128)(2,1)S(1)}, u32[]{:S(2)}, u32[]{:S(2)}) collective-permute-start(bf16[128,512]{1,0:T(8,128)(2,1)} %param.7), channel_id=1, source_target_pairs={{0,24},{8,16},{16,8},{24,0},{1,25},{9,17},{17,9},{25,1},{2,26},{10... | collective-permute-start | bytes 393224 | tf_op jit(solution)/shard_map/ppermute | solution.py:108
  7.2 0.5 collective-permute-start.1
  7.7 0.5 collective-permute-start
  8.2 1.3 %collective-permute-start.4 = (bf16[128,512]{1,0:T(8,128)(2,1)}, bf16[128,512]{1,0:T(8,128)(2,1)S(1)}, u32[]{:S(2)}, u32[]{:S(2)}) collective-permute-start(bf16[128,512]{1,0:T(8,128)(2,1)} %param.7), channel_id=1, source_target_pairs={{0,6},{2,4},{4,2},{6,0},{1,7},{3,5},{5,3},{7,1},{8,14},{10,12},{12... | collective-permute-start | bytes 393224 | tf_op jit(solution)/shard_map/ppermute | solution.py:108
  9.6 0.7 select_reduce_fusion
  10.3 1.5 %pad_maximum_fusion = bf16[384,2048]{1,0:T(8,128)(2,1)S(1)} fusion(bf16[192,2048]{1,0:T(8,128)(2,1)} %bitcast.49, bf16[192,2048]{1,0:T(8,128)(2,1)} %bitcast.50), kind=kLoop, calls=%fused_computation.2 | loop fusion | flops 3145728 | bytes 3145728 | tf_op jit(solution)/shard_map/concatenate | solution.py:120
  11.9 1.7 %collective-permute-done = bf16[128,512]{1,0:T(8,128)(2,1)S(1)} collective-permute-done((bf16[128,512]{1,0:T(8,128)(2,1)}, bf16[128,512]{1,0:T(8,128)(2,1)S(1)}, u32[]{:S(2)}, u32[]{:S(2)}) %collective-permute-start) | collective-permute-done | bytes 131104 | tf_op jit(solution)/shard_map/ppermute | solution.py:108
  13.7 1.6 %collective-permute-start.8 = (bf16[512,512]{1,0:T(8,128)(2,1)S(1)}, bf16[512,512]{1,0:T(8,128)(2,1)S(1)}, u32[]{:S(2)}, u32[]{:S(2)}) collective-permute-start(bf16[512,512]{1,0:T(8,128)(2,1)S(1)} %constant_dynamic-update-slice_fusion.refs_4_), channel_id=1, source_target_pairs={{0,2},{2,0},{4,6},{6,4},{1,3},{3,1},{5,7},{7,5},{8,10},{10,8},{12,... | collective-permute-start | bytes 1572872 | tf_op jit(solution)/shard_map/ppermute | solution.py:108
  15.5 3.1 %collective-permute-start.7 = (bf16[256,512]{1,0:T(8,128)(2,1)S(1)}, bf16[256,512]{1,0:T(8,128)(2,1)S(1)}, u32[]{:S(2)}, u32[]{:S(2)}) collective-permute-start(bf16[256,512]{1,0:T(8,128)(2,1)S(1)} %pad_maximum_fusion.9.refs_6_), channel_id=1, source_target_pairs={{0,24},{8,16},{16,8},{24,0},{1,25},{9,17},{17,9},{25,1},{2,26},{10... | collective-permute-start | bytes 786440 | tf_op jit(solution)/shard_map/ppermute | solution.py:108
  19.8 0.3 fusion.58
  20.1 0.6 collective-permute-start.5
  22.1 5.2 %collective-permute-done.8.refs_5_ = bf16[512,512]{1,0:T(8,128)(2,1)S(1)} collective-permute-done((bf16[512,512]{1,0:T(8,128)(2,1)S(1)}, bf16[512,512]{1,0:T(8,128)(2,1)S(1)}, u32[]{:S(2)}, u32[]{:S(2)}) %collective-permute-start.8) | collective-permute-done | bytes 524320 | tf_op jit(solution)/shard_map/ppermute | solution.py:108
  27.7 1.5 %collective-permute-start.17 = (bf16[144,512]{1,0:T(8,128)(2,1)S(1)}, bf16[144,512]{1,0:T(8,128)(2,1)S(1)}, u32[]{:S(2)}, u32[]{:S(2)}) collective-permute-start(bf16[144,512]{1,0:T(8,128)(2,1)S(1)} %pad_maximum_fusion.10), channel_id=1, source_target_pairs={{0,6},{2,4},{4,2},{6,0},{1,7},{3,5},{5,3},{7,1},{8,14},{10,12},{12... | collective-permute-start | bytes 442376 | tf_op jit(solution)/shard_map/ppermute | solution.py:108
  30.1 1.6 %collective-permute-start.16 = (bf16[144,512]{1,0:T(8,128)(2,1)S(1)}, bf16[144,512]{1,0:T(8,128)(2,1)S(1)}, u32[]{:S(2)}, u32[]{:S(2)}) collective-permute-start(bf16[144,512]{1,0:T(8,128)(2,1)S(1)} %pad_maximum_fusion.10), channel_id=1, source_target_pairs={{0,4},{2,6},{4,0},{6,2},{1,5},{3,7},{5,1},{7,3},{8,12},{10,14},{12... | collective-permute-start | bytes 442376 | tf_op jit(solution)/shard_map/ppermute | solution.py:108
  32.9 0.3 fusion.34
  33.2 0.6 collective-permute-start.12
  34.3 0.3 add_add_fusion.1
  35.1 0.3 fusion.32
  36.2 1.6 %collective-permute-start.20 = (bf16[192,1024]{1,0:T(8,128)(2,1)S(1)}, bf16[192,1024]{1,0:T(8,128)(2,1)S(1)}, u32[]{:S(2)}, u32[]{:S(2)}) collective-permute-start(bf16[192,1024]{1,0:T(8,128)(2,1)S(1)} %fusion.79), channel_id=1, source_target_pairs={{0,16},{8,24},{16,0},{24,8},{1,17},{9,25},{17,1},{25,9},{2,18},{10... | collective-permute-start | bytes 1179656 | tf_op jit(solution)/shard_map/ppermute | solution.py:108
  38.0 1.9 %collective-permute-start.15 = (bf16[144,512]{1,0:T(8,128)(2,1)S(1)}, bf16[144,512]{1,0:T(8,128)(2,1)S(1)}, u32[]{:S(2)}, u32[]{:S(2)}) collective-permute-start(bf16[144,512]{1,0:T(8,128)(2,1)S(1)} %pad_maximum_fusion.10), channel_id=1, source_target_pairs={{0,2},{2,0},{4,6},{6,4},{1,3},{3,1},{5,7},{7,5},{8,10},{10,8},{12,... | collective-permute-start | bytes 442376 | tf_op jit(solution)/shard_map/ppermute | solution.py:108
  40.0 4.6 %collective-permute-done.16 = bf16[144,512]{1,0:T(8,128)(2,1)S(1)} collective-permute-done((bf16[144,512]{1,0:T(8,128)(2,1)S(1)}, bf16[144,512]{1,0:T(8,128)(2,1)S(1)}, u32[]{:S(2)}, u32[]{:S(2)}) %collective-permute-start.16) | collective-permute-done | bytes 147488 | tf_op jit(solution)/shard_map/ppermute | solution.py:108
  44.6 2.6 %collective-permute-done.15 = bf16[144,512]{1,0:T(8,128)(2,1)S(1)} collective-permute-done((bf16[144,512]{1,0:T(8,128)(2,1)S(1)}, bf16[144,512]{1,0:T(8,128)(2,1)S(1)}, u32[]{:S(2)}, u32[]{:S(2)}) %collective-permute-start.15) | collective-permute-done | bytes 147488 | tf_op jit(solution)/shard_map/ppermute | solution.py:108
  47.4 0.4 collective-permute-done.20
  47.8 1.5 %collective-permute-start.22 = (bf16[96,1024]{1,0:T(8,128)(2,1)S(1)}, bf16[96,1024]{1,0:T(8,128)(2,1)S(1)}, u32[]{:S(2)}, u32[]{:S(2)}) collective-permute-start(bf16[96,1024]{1,0:T(8,128)(2,1)S(1)} %slice.231), channel_id=1, source_target_pairs={{0,8},{8,0},{16,24},{24,16},{1,9},{9,1},{17,25},{25,17},{2,10},{10... | collective-permute-start | bytes 589832 | tf_op jit(solution)/shard_map/ppermute | solution.py:108
  49.4 0.4 collective-permute-start.21
  49.9 0.3 fusion
  50.2 1.0 %fusion.119 = (bf16[768,1024]{1,0:T(8,128)(2,1)S(1)}, f32[768,1024]{1,0:T(8,128)S(1)}) fusion(bf16[768,512]{1,0:T(8,128)(2,1)S(1)} %pad_maximum_fusion.1, bf16[1024,512]{1,0:T(8,128)(2,1)S(1)} %fusion), kind=kOutput, calls=%fused_computation.192 | convolution fusion | flops 806092800 | bytes 6553600 | tf_op jit(solution)/shard_map/dot_general | solution.py:248
  51.3 1.8 %collective-permute-start.26 = (bf16[96,1024]{1,0:T(8,128)(2,1)S(1)}, bf16[96,1024]{1,0:T(8,128)(2,1)S(1)}, u32[]{:S(2)}, u32[]{:S(2)}) collective-permute-start(bf16[96,1024]{1,0:T(8,128)(2,1)S(1)} %get-tuple-element.117), channel_id=1, source_target_pairs={{0,8},{8,0},{16,24},{24,16},{1,9},{9,1},{17,25},{25,17},{2,10},{10... | collective-permute-start | bytes 589832 | tf_op jit(solution)/shard_map/ppermute | solution.py:108
  53.1 0.5 collective-permute-start.24
  53.7 1.9 %collective-permute-done.22 = bf16[96,1024]{1,0:T(8,128)(2,1)S(1)} collective-permute-done((bf16[96,1024]{1,0:T(8,128)(2,1)S(1)}, bf16[96,1024]{1,0:T(8,128)(2,1)S(1)}, u32[]{:S(2)}, u32[]{:S(2)}) %collective-permute-start.22) | collective-permute-done | bytes 196640 | tf_op jit(solution)/shard_map/ppermute | solution.py:108
  55.6 1.6 %collective-permute-done.21 = bf16[96,1024]{1,0:T(8,128)(2,1)S(1)} collective-permute-done((bf16[96,1024]{1,0:T(8,128)(2,1)S(1)}, bf16[96,1024]{1,0:T(8,128)(2,1)S(1)}, u32[]{:S(2)}, u32[]{:S(2)}) %collective-permute-start.21) | collective-permute-done | bytes 196640 | tf_op jit(solution)/shard_map/ppermute | solution.py:108
  57.3 0.6 fusion.3
  58.1 0.9 %collective-permute-done.26 = bf16[96,1024]{1,0:T(8,128)(2,1)S(1)} collective-permute-done((bf16[96,1024]{1,0:T(8,128)(2,1)S(1)}, bf16[96,1024]{1,0:T(8,128)(2,1)S(1)}, u32[]{:S(2)}, u32[]{:S(2)}) %collective-permute-start.26) | collective-permute-done | bytes 196640 | tf_op jit(solution)/shard_map/ppermute | solution.py:108
  59.0 1.4 %collective-permute-done.24 = bf16[96,1024]{1,0:T(8,128)(2,1)S(1)} collective-permute-done((bf16[96,1024]{1,0:T(8,128)(2,1)S(1)}, bf16[96,1024]{1,0:T(8,128)(2,1)S(1)}, u32[]{:S(2)}, u32[]{:S(2)}) %collective-permute-start.24) | collective-permute-done | bytes 196640 | tf_op jit(solution)/shard_map/ppermute | solution.py:108
  60.5 0.5 collective-permute-start.25
  61.0 1.7 %collective-permute-start.27 = (bf16[192,1024]{1,0:T(8,128)(2,1)S(1)}, bf16[192,1024]{1,0:T(8,128)(2,1)S(1)}, u32[]{:S(2)}, u32[]{:S(2)}) collective-permute-start(bf16[192,1024]{1,0:T(8,128)(2,1)S(1)} %pad_maximum_fusion.4), channel_id=1, source_target_pairs={{0,16},{8,24},{16,0},{24,8},{1,17},{9,25},{17,1},{25,9},{2,18},{10... | collective-permute-start | bytes 1179656 | tf_op jit(solution)/shard_map/ppermute | solution.py:108
  62.7 0.6 convert_add_fusion
  63.5 1.5 %collective-permute-start.28 = (bf16[128,512]{1,0:T(8,128)(2,1)S(1)}, bf16[128,512]{1,0:T(8,128)(2,1)S(1)}, u32[]{:S(2)}, u32[]{:S(2)}) collective-permute-start(bf16[128,512]{1,0:T(8,128)(2,1)S(1)} %get-tuple-element.128), channel_id=1, source_target_pairs={{0,4},{2,6},{4,0},{6,2},{1,5},{3,7},{5,1},{7,3},{8,12},{10,14},{12... | collective-permute-start | bytes 393224 | tf_op jit(solution)/shard_map/ppermute | solution.py:108
  65.0 1.8 %collective-permute-start.30 = (bf16[128,512]{1,0:T(8,128)(2,1)S(1)}, bf16[128,512]{1,0:T(8,128)(2,1)S(1)}, u32[]{:S(2)}, u32[]{:S(2)}) collective-permute-start(bf16[128,512]{1,0:T(8,128)(2,1)S(1)} %get-tuple-element.129), channel_id=1, source_target_pairs={{0,6},{2,4},{4,2},{6,0},{1,7},{3,5},{5,3},{7,1},{8,14},{10,12},{12... | collective-permute-start | bytes 393224 | tf_op jit(solution)/shard_map/ppermute | solution.py:108
  67.0 1.0 %convolution_convert_fusion = bf16[768,512]{1,0:T(8,128)(2,1)S(1)} fusion(bf16[768,1024]{1,0:T(8,128)(2,1)S(1)} %constant_dynamic-update-slice_fusion.9, bf16[1024,512]{1,0:T(8,128)(2,1)S(1)} %fusion), kind=kOutput, calls=%fused_computation.3 | convolution fusion | flops 805699584 | bytes 3407872 | tf_op jit(solution)/shard_map/dot_general | solution.py:271
  68.1 0.9 %maximum_bitcast_fusion = bf16[1,768,512]{2,1,0:T(8,128)(2,1)} fusion(bf16[192,512]{1,0:T(8,128)(2,1)S(1)} %get-tuple-element.121, bf16[192,512]{1,0:T(8,128)(2,1)S(1)} %get-tuple-element.122, bf16[192,512]{1,0:T(8,128)(2,1)S(1)} %get-tuple-element.123, bf16[192,512]{1,0:T(8,128)(2,1)S(1)} %get-tuple-element.120), kind=kLoop, calls=%fused_computation.27 | loop fusion | flops 3145728 | bytes 1572864 | tf_op jit(solution)/shard_map/broadcast_in_dim | solution.py:278
  69.0 1.7 %collective-permute-done.25.x_ref = bf16[192,1024]{1,0:T(8,128)(2,1)S(1)} collective-permute-done((bf16[192,1024]{1,0:T(8,128)(2,1)S(1)}, bf16[192,1024]{1,0:T(8,128)(2,1)S(1)}, u32[]{:S(2)}, u32[]{:S(2)}) %collective-permute-start.25) | collective-permute-done | bytes 393248 | tf_op jit(solution)/shard_map/ppermute | solution.py:108
  70.7 0.3 collective-permute-done.27.y_ref
  71.0 2.8 %shard_map.102 = (bf16[192,2048]{1,0:T(8,128)(2,1)}, bf16[192,2048]{1,0:T(8,128)(2,1)}) custom-call(s32[1]{0:T(128)} %bitcast.15.place_ref, f32[192,1024]{1,0:T(8,128)S(1)} %slice.229.share_ref, bf16[192,1024]{1,0:T(8,128)(2,1)S(1)} %collective-permute-done.25.x_ref, bf16[192,1024]{1,0:T(8,128)(2,1)S(1)} %collective-permute-done.27.y_ref, ...), custom_call_target="tpu_custom_call" | custom-call | tf_op jit(solution)/shard_map/pallas_call | solution.py:170
  73.9 0.8 %collective-permute-done.28 = bf16[128,512]{1,0:T(8,128)(2,1)S(1)} collective-permute-done((bf16[128,512]{1,0:T(8,128)(2,1)S(1)}, bf16[128,512]{1,0:T(8,128)(2,1)S(1)}, u32[]{:S(2)}, u32[]{:S(2)}) %collective-permute-start.28) | collective-permute-done | bytes 131104 | tf_op jit(solution)/shard_map/ppermute | solution.py:108
  74.6 0.7 collective-permute-done.29
  75.3 0.7 add_convert_fusion
  (107 shorter events, 8.2 us)
Async XLA Ops:
  0.6 14.8 %collective-permute-start.3 = (bf16[128,512]{1,0:T(8,128)(2,1)}, bf16[128,512]{1,0:T(8,128)(2,1)S(1)}, u32[]{:S(2)}, u32[]{:S(2)}) collective-permute-start(bf16[128,512]{1,0:T(8,128)(2,1)} %param.7), channel_id=1, source_target_pairs={{0,4},{2,6},{4,0},{6,2},{1,5},{3,7},{5,1},{7,3},{8,12},{10,14},{12... | collective-permute-start | bytes 393224 | tf_op jit(solution)/shard_map/ppermute | solution.py:108
  4.7 9.0 %collective-permute-start.2 = (bf16[128,512]{1,0:T(8,128)(2,1)}, bf16[128,512]{1,0:T(8,128)(2,1)S(1)}, u32[]{:S(2)}, u32[]{:S(2)}) collective-permute-start(bf16[128,512]{1,0:T(8,128)(2,1)} %param.7), channel_id=1, source_target_pairs={{0,24},{8,16},{16,8},{24,0},{1,25},{9,17},{17,9},{25,1},{2,26},{10... | collective-permute-start | bytes 393224 | tf_op jit(solution)/shard_map/ppermute | solution.py:108
  7.2 6.5 %collective-permute-start.1 = (bf16[128,512]{1,0:T(8,128)(2,1)}, bf16[128,512]{1,0:T(8,128)(2,1)S(1)}, u32[]{:S(2)}, u32[]{:S(2)}) collective-permute-start(bf16[128,512]{1,0:T(8,128)(2,1)} %param.7), channel_id=1, source_target_pairs={{0,16},{8,24},{16,0},{24,8},{1,17},{9,25},{17,1},{25,9},{2,18},{10... | collective-permute-start | bytes 393224 | tf_op jit(solution)/shard_map/ppermute | solution.py:108
  7.7 6.0 %collective-permute-start = (bf16[128,512]{1,0:T(8,128)(2,1)}, bf16[128,512]{1,0:T(8,128)(2,1)S(1)}, u32[]{:S(2)}, u32[]{:S(2)}) collective-permute-start(bf16[128,512]{1,0:T(8,128)(2,1)} %param.7), channel_id=1, source_target_pairs={{0,8},{8,0},{16,24},{24,16},{1,9},{9,1},{17,25},{25,17},{2,10},{10... | collective-permute-start | bytes 393224 | tf_op jit(solution)/shard_map/ppermute | solution.py:108
  8.2 7.2 %collective-permute-start.4 = (bf16[128,512]{1,0:T(8,128)(2,1)}, bf16[128,512]{1,0:T(8,128)(2,1)S(1)}, u32[]{:S(2)}, u32[]{:S(2)}) collective-permute-start(bf16[128,512]{1,0:T(8,128)(2,1)} %param.7), channel_id=1, source_target_pairs={{0,6},{2,4},{4,2},{6,0},{1,7},{3,5},{5,3},{7,1},{8,14},{10,12},{12... | collective-permute-start | bytes 393224 | tf_op jit(solution)/shard_map/ppermute | solution.py:108
  10.3 1.5 %copy-start.2 = (bf16[128,512]{1,0:T(8,128)(2,1)S(1)}, bf16[128,512]{1,0:T(8,128)(2,1)}, u32[]{:S(2)}) copy-start(bf16[128,512]{1,0:T(8,128)(2,1)} %param.8) | copy-start | bytes 393220
  10.3 1.6 %copy-start.3 = (bf16[128,512]{1,0:T(8,128)(2,1)S(1)}, bf16[128,512]{1,0:T(8,128)(2,1)}, u32[]{:S(2)}) copy-start(bf16[128,512]{1,0:T(8,128)(2,1)} %param.7) | copy-start | bytes 393220
  13.7 13.6 %collective-permute-start.8 = (bf16[512,512]{1,0:T(8,128)(2,1)S(1)}, bf16[512,512]{1,0:T(8,128)(2,1)S(1)}, u32[]{:S(2)}, u32[]{:S(2)}) collective-permute-start(bf16[512,512]{1,0:T(8,128)(2,1)S(1)} %constant_dynamic-update-slice_fusion.refs_4_), channel_id=1, source_target_pairs={{0,2},{2,0},{4,6},{6,4},{1,3},{3,1},{5,7},{7,5},{8,10},{10,8},{12,... | collective-permute-start | bytes 1572872 | tf_op jit(solution)/shard_map/ppermute | solution.py:108
  15.4 4.7 %collective-permute-start.11 = (bf16[256,512]{1,0:T(8,128)(2,1)S(1)}, bf16[256,512]{1,0:T(8,128)(2,1)S(1)}, u32[]{:S(2)}, u32[]{:S(2)}) collective-permute-start(bf16[256,512]{1,0:T(8,128)(2,1)S(1)} %pad_maximum_fusion.9.refs_6_), channel_id=1, source_target_pairs={{0,1},{1,0},{2,3},{3,2},{4,5},{5,4},{6,7},{7,6},{8,9},{9,8},{10,11... | collective-permute-start | bytes 786440 | tf_op jit(solution)/shard_map/ppermute | solution.py:108
  15.5 17.3 %collective-permute-start.7 = (bf16[256,512]{1,0:T(8,128)(2,1)S(1)}, bf16[256,512]{1,0:T(8,128)(2,1)S(1)}, u32[]{:S(2)}, u32[]{:S(2)}) collective-permute-start(bf16[256,512]{1,0:T(8,128)(2,1)S(1)} %pad_maximum_fusion.9.refs_6_), channel_id=1, source_target_pairs={{0,24},{8,16},{16,8},{24,0},{1,25},{9,17},{17,9},{25,1},{2,26},{10... | collective-permute-start | bytes 786440 | tf_op jit(solution)/shard_map/ppermute | solution.py:108
  18.6 14.2 %collective-permute-start.6 = (bf16[256,512]{1,0:T(8,128)(2,1)S(1)}, bf16[256,512]{1,0:T(8,128)(2,1)S(1)}, u32[]{:S(2)}, u32[]{:S(2)}) collective-permute-start(bf16[256,512]{1,0:T(8,128)(2,1)S(1)} %pad_maximum_fusion.9.refs_6_), channel_id=1, source_target_pairs={{0,16},{8,24},{16,0},{24,8},{1,17},{9,25},{17,1},{25,9},{2,18},{10... | collective-permute-start | bytes 786440 | tf_op jit(solution)/shard_map/ppermute | solution.py:108
  18.6 2.5 %collective-permute-start.9 = (bf16[512,512]{1,0:T(8,128)(2,1)S(1)}, bf16[512,512]{1,0:T(8,128)(2,1)S(1)}, u32[]{:S(2)}, u32[]{:S(2)}) collective-permute-start(bf16[512,512]{1,0:T(8,128)(2,1)S(1)} %constant_dynamic-update-slice_fusion.refs_4_), channel_id=1, source_target_pairs={{0,1},{1,0},{2,3},{3,2},{4,5},{5,4},{6,7},{7,6},{8,9},{9,8},{10,11... | collective-permute-start | bytes 1572872 | tf_op jit(solution)/shard_map/ppermute | solution.py:108
  20.1 12.7 %collective-permute-start.5 = (bf16[256,512]{1,0:T(8,128)(2,1)S(1)}, bf16[256,512]{1,0:T(8,128)(2,1)S(1)}, u32[]{:S(2)}, u32[]{:S(2)}) collective-permute-start(bf16[256,512]{1,0:T(8,128)(2,1)S(1)} %pad_maximum_fusion.9.refs_6_), channel_id=1, source_target_pairs={{0,8},{8,0},{16,24},{24,16},{1,9},{9,1},{17,25},{25,17},{2,10},{10... | collective-permute-start | bytes 786440 | tf_op jit(solution)/shard_map/ppermute | solution.py:108
  27.6 2.4 %collective-permute-start.10 = (bf16[512,512]{1,0:T(8,128)(2,1)S(1)}, bf16[512,512]{1,0:T(8,128)(2,1)S(1)}, u32[]{:S(2)}, u32[]{:S(2)}) collective-permute-start(bf16[512,512]{1,0:T(8,128)(2,1)S(1)} %collective-permute-done.8.refs_5_), channel_id=1, source_target_pairs={{0,1},{1,0},{2,3},{3,2},{4,5},{5,4},{6,7},{7,6},{8,9},{9,8},{10,11... | collective-permute-start | bytes 1572872 | tf_op jit(solution)/shard_map/ppermute | solution.py:108
  27.7 12.3 %collective-permute-start.17 = (bf16[144,512]{1,0:T(8,128)(2,1)S(1)}, bf16[144,512]{1,0:T(8,128)(2,1)S(1)}, u32[]{:S(2)}, u32[]{:S(2)}) collective-permute-start(bf16[144,512]{1,0:T(8,128)(2,1)S(1)} %pad_maximum_fusion.10), channel_id=1, source_target_pairs={{0,6},{2,4},{4,2},{6,0},{1,7},{3,5},{5,3},{7,1},{8,14},{10,12},{12... | collective-permute-start | bytes 442376 | tf_op jit(solution)/shard_map/ppermute | solution.py:108
  30.1 14.5 %collective-permute-start.16 = (bf16[144,512]{1,0:T(8,128)(2,1)S(1)}, bf16[144,512]{1,0:T(8,128)(2,1)S(1)}, u32[]{:S(2)}, u32[]{:S(2)}) collective-permute-start(bf16[144,512]{1,0:T(8,128)(2,1)S(1)} %pad_maximum_fusion.10), channel_id=1, source_target_pairs={{0,4},{2,6},{4,0},{6,2},{1,5},{3,7},{5,1},{7,3},{8,12},{10,14},{12... | collective-permute-start | bytes 442376 | tf_op jit(solution)/shard_map/ppermute | solution.py:108
  32.8 2.3 %collective-permute-start.13 = (bf16[256,512]{1,0:T(8,128)(2,1)S(1)}, bf16[256,512]{1,0:T(8,128)(2,1)S(1)}, u32[]{:S(2)}, u32[]{:S(2)}) collective-permute-start(bf16[256,512]{1,0:T(8,128)(2,1)S(1)} %collective-permute-done.6.refs_8_), channel_id=1, source_target_pairs={{0,1},{1,0},{2,3},{3,2},{4,5},{5,4},{6,7},{7,6},{8,9},{9,8},{10,11... | collective-permute-start | bytes 786440 | tf_op jit(solution)/shard_map/ppermute | solution.py:108
  33.2 2.2 %collective-permute-start.12 = (bf16[256,512]{1,0:T(8,128)(2,1)S(1)}, bf16[256,512]{1,0:T(8,128)(2,1)S(1)}, u32[]{:S(2)}, u32[]{:S(2)}) collective-permute-start(bf16[256,512]{1,0:T(8,128)(2,1)S(1)} %collective-permute-done.5.refs_7_), channel_id=1, source_target_pairs={{0,1},{1,0},{2,3},{3,2},{4,5},{5,4},{6,7},{7,6},{8,9},{9,8},{10,11... | collective-permute-start | bytes 786440 | tf_op jit(solution)/shard_map/ppermute | solution.py:108
  34.0 1.7 %collective-permute-start.14 = (bf16[256,512]{1,0:T(8,128)(2,1)S(1)}, bf16[256,512]{1,0:T(8,128)(2,1)S(1)}, u32[]{:S(2)}, u32[]{:S(2)}) collective-permute-start(bf16[256,512]{1,0:T(8,128)(2,1)S(1)} %collective-permute-done.7.refs_9_), channel_id=1, source_target_pairs={{0,1},{1,0},{2,3},{3,2},{4,5},{5,4},{6,7},{7,6},{8,9},{9,8},{10,11... | collective-permute-start | bytes 786440 | tf_op jit(solution)/shard_map/ppermute | solution.py:108
  35.7 2.2 %copy-start.1 = (bf16[1,768,512]{2,1,0:T(8,128)(2,1)S(1)}, bf16[1,768,512]{2,1,0:T(8,128)(2,1)}, u32[]{:S(2)}) copy-start(bf16[1,768,512]{2,1,0:T(8,128)(2,1)} %param.13) | copy-start | bytes 2359300
  36.2 11.6 %collective-permute-start.20 = (bf16[192,1024]{1,0:T(8,128)(2,1)S(1)}, bf16[192,1024]{1,0:T(8,128)(2,1)S(1)}, u32[]{:S(2)}, u32[]{:S(2)}) collective-permute-start(bf16[192,1024]{1,0:T(8,128)(2,1)S(1)} %fusion.79), channel_id=1, source_target_pairs={{0,16},{8,24},{16,0},{24,8},{1,17},{9,25},{17,1},{25,9},{2,18},{10... | collective-permute-start | bytes 1179656 | tf_op jit(solution)/shard_map/ppermute | solution.py:108
  37.8 11.6 %collective-permute-start.19 = (bf16[192,1024]{1,0:T(8,128)(2,1)S(1)}, bf16[192,1024]{1,0:T(8,128)(2,1)S(1)}, u32[]{:S(2)}, u32[]{:S(2)}) collective-permute-start(bf16[192,1024]{1,0:T(8,128)(2,1)S(1)} %fusion.79), channel_id=1, source_target_pairs={{0,8},{8,0},{16,24},{24,16},{1,9},{9,1},{17,25},{25,17},{2,10},{10... | collective-permute-start | bytes 1179656 | tf_op jit(solution)/shard_map/ppermute | solution.py:108
  38.0 9.1 %collective-permute-start.15 = (bf16[144,512]{1,0:T(8,128)(2,1)S(1)}, bf16[144,512]{1,0:T(8,128)(2,1)S(1)}, u32[]{:S(2)}, u32[]{:S(2)}) collective-permute-start(bf16[144,512]{1,0:T(8,128)(2,1)S(1)} %pad_maximum_fusion.10), channel_id=1, source_target_pairs={{0,2},{2,0},{4,6},{6,4},{1,3},{3,1},{5,7},{7,5},{8,10},{10,8},{12,... | collective-permute-start | bytes 442376 | tf_op jit(solution)/shard_map/ppermute | solution.py:108
  47.2 2.5 %collective-permute-start.18 = (bf16[4,144,512]{2,1,0:T(8,128)(2,1)S(1)}, bf16[4,144,512]{2,1,0:T(8,128)(2,1)S(1)}, u32[]{:S(2)}, u32[]{:S(2)}) collective-permute-start(bf16[4,144,512]{2,1,0:T(8,128)(2,1)S(1)} %pad_maximum_fusion.2), channel_id=1, source_target_pairs={{0,1},{1,0},{2,3},{3,2},{4,5},{5,4},{6,7},{7,6},{8,9},{9,8},{10,11... | collective-permute-start | bytes 1769480 | tf_op jit(solution)/shard_map/ppermute | solution.py:108
  47.8 7.8 %collective-permute-start.22 = (bf16[96,1024]{1,0:T(8,128)(2,1)S(1)}, bf16[96,1024]{1,0:T(8,128)(2,1)S(1)}, u32[]{:S(2)}, u32[]{:S(2)}) collective-permute-start(bf16[96,1024]{1,0:T(8,128)(2,1)S(1)} %slice.231), channel_id=1, source_target_pairs={{0,8},{8,0},{16,24},{24,16},{1,9},{9,1},{17,25},{25,17},{2,10},{10... | collective-permute-start | bytes 589832 | tf_op jit(solution)/shard_map/ppermute | solution.py:108
  49.4 7.8 %collective-permute-start.21 = (bf16[96,1024]{1,0:T(8,128)(2,1)S(1)}, bf16[96,1024]{1,0:T(8,128)(2,1)S(1)}, u32[]{:S(2)}, u32[]{:S(2)}) collective-permute-start(bf16[96,1024]{1,0:T(8,128)(2,1)S(1)} %slice.230), channel_id=1, source_target_pairs={{0,16},{8,24},{16,0},{24,8},{1,17},{9,25},{17,1},{25,9},{2,18},{10... | collective-permute-start | bytes 589832 | tf_op jit(solution)/shard_map/ppermute | solution.py:108
  51.3 7.7 %collective-permute-start.26 = (bf16[96,1024]{1,0:T(8,128)(2,1)S(1)}, bf16[96,1024]{1,0:T(8,128)(2,1)S(1)}, u32[]{:S(2)}, u32[]{:S(2)}) collective-permute-start(bf16[96,1024]{1,0:T(8,128)(2,1)S(1)} %get-tuple-element.117), channel_id=1, source_target_pairs={{0,8},{8,0},{16,24},{24,16},{1,9},{9,1},{17,25},{25,17},{2,10},{10... | collective-permute-start | bytes 589832 | tf_op jit(solution)/shard_map/ppermute | solution.py:108
  53.1 7.3 %collective-permute-start.24 = (bf16[96,1024]{1,0:T(8,128)(2,1)S(1)}, bf16[96,1024]{1,0:T(8,128)(2,1)S(1)}, u32[]{:S(2)}, u32[]{:S(2)}) collective-permute-start(bf16[96,1024]{1,0:T(8,128)(2,1)S(1)} %get-tuple-element.119), channel_id=1, source_target_pairs={{0,16},{8,24},{16,0},{24,8},{1,17},{9,25},{17,1},{25,9},{2,18},{10... | collective-permute-start | bytes 589832 | tf_op jit(solution)/shard_map/ppermute | solution.py:108
  58.0 4.7 %collective-permute-start.23 = (bf16[512,512]{1,0:T(8,128)(2,1)S(1)}, bf16[512,512]{1,0:T(8,128)(2,1)S(1)}, u32[]{:S(2)}, u32[]{:S(2)}) collective-permute-start(bf16[512,512]{1,0:T(8,128)(2,1)S(1)} %fusion.3), channel_id=1, source_target_pairs={{0,1},{1,0},{2,3},{3,2},{4,5},{5,4},{6,7},{7,6},{8,9},{9,8},{10,11... | collective-permute-start | bytes 1572872 | tf_op jit(solution)/shard_map/ppermute | solution.py:108
  60.5 10.2 %collective-permute-start.25 = (bf16[192,1024]{1,0:T(8,128)(2,1)S(1)}, bf16[192,1024]{1,0:T(8,128)(2,1)S(1)}, u32[]{:S(2)}, u32[]{:S(2)}) collective-permute-start(bf16[192,1024]{1,0:T(8,128)(2,1)S(1)} %pad_maximum_fusion.3), channel_id=1, source_target_pairs={{0,8},{8,0},{16,24},{24,16},{1,9},{9,1},{17,25},{25,17},{2,10},{10... | collective-permute-start | bytes 1179656 | tf_op jit(solution)/shard_map/ppermute | solution.py:108
  61.0 10.0 %collective-permute-start.27 = (bf16[192,1024]{1,0:T(8,128)(2,1)S(1)}, bf16[192,1024]{1,0:T(8,128)(2,1)S(1)}, u32[]{:S(2)}, u32[]{:S(2)}) collective-permute-start(bf16[192,1024]{1,0:T(8,128)(2,1)S(1)} %pad_maximum_fusion.4), channel_id=1, source_target_pairs={{0,16},{8,24},{16,0},{24,8},{1,17},{9,25},{17,1},{25,9},{2,18},{10... | collective-permute-start | bytes 1179656 | tf_op jit(solution)/shard_map/ppermute | solution.py:108
  63.3 4.7 %copy-start = (f32[512,512]{1,0:T(8,128)}, f32[512,512]{1,0:T(8,128)S(1)}, u32[]{:S(2)}) copy-start(f32[512,512]{1,0:T(8,128)S(1)} %convert_add_fusion) | copy-start | bytes 3145732
  63.5 11.2 %collective-permute-start.28 = (bf16[128,512]{1,0:T(8,128)(2,1)S(1)}, bf16[128,512]{1,0:T(8,128)(2,1)S(1)}, u32[]{:S(2)}, u32[]{:S(2)}) collective-permute-start(bf16[128,512]{1,0:T(8,128)(2,1)S(1)} %get-tuple-element.128), channel_id=1, source_target_pairs={{0,4},{2,6},{4,0},{6,2},{1,5},{3,7},{5,1},{7,3},{8,12},{10,14},{12... | collective-permute-start | bytes 393224 | tf_op jit(solution)/shard_map/ppermute | solution.py:108
  65.0 9.6 %collective-permute-start.30 = (bf16[128,512]{1,0:T(8,128)(2,1)S(1)}, bf16[128,512]{1,0:T(8,128)(2,1)S(1)}, u32[]{:S(2)}, u32[]{:S(2)}) collective-permute-start(bf16[128,512]{1,0:T(8,128)(2,1)S(1)} %get-tuple-element.129), channel_id=1, source_target_pairs={{0,6},{2,4},{4,2},{6,0},{1,7},{3,5},{5,3},{7,1},{8,14},{10,12},{12... | collective-permute-start | bytes 393224 | tf_op jit(solution)/shard_map/ppermute | solution.py:108
  66.8 8.5 %collective-permute-start.29 = (bf16[128,512]{1,0:T(8,128)(2,1)S(1)}, bf16[128,512]{1,0:T(8,128)(2,1)S(1)}, u32[]{:S(2)}, u32[]{:S(2)}) collective-permute-start(bf16[128,512]{1,0:T(8,128)(2,1)S(1)} %get-tuple-element.130), channel_id=1, source_target_pairs={{0,2},{2,0},{4,6},{6,4},{1,3},{3,1},{5,7},{7,5},{8,10},{10,8},{12,... | collective-permute-start | bytes 393224 | tf_op jit(solution)/shard_map/ppermute | solution.py:108
  71.0 4.3 %slice-start = ((f32[512,512]{1,0:T(8,128)}), f32[128,512]{1,0:T(8,128)S(1)}, s32[]{:S(2)}) async-start(f32[512,512]{1,0:T(8,128)} %copy-done), calls=%async_computation | async-start | bytes 524288 | tf_op jit(solution)/shard_map/slice | solution.py:269

commit v7 on v6

--- a/solution.py
+++ b/solution.py
@@ -213,9 +213,9 @@
 
     p2 = [far] + spread(far)
     late, own_there = phase(payload, own_there)
+    g2 = swap(late, "grp", 2)
+    late, p1, *pre_own = phase(payload, p1, *pre_own)
     g3 = swap(late, "grp", 3)
-    late, p1, *pre_own = phase(payload, p1, *pre_own)
-    g2 = swap(late, "grp", 2)
     p1_there = to_core(p1)
     pre_near = [block_part(in_weights, block) for block in (p1, p1_there)]
     values = phase(*p2, payload, p1, p1_there, far_there, *pre_far, *pre_own, *pre_near)
@@ -263,7 +263,9 @@
         * scale[k * 4 * rows : (k + 1) * 4 * rows]
         for k in range(2)
     ]
-    out, hidden, grads = phase(out[0] + to_core(out[1].astype(half_type)).astype(wide_type), hidden, grads)
+    theirs = to_core(out[1].astype(half_type))
+    out_own, own_share = phase(out[0], own_share)
+    out, hidden, grads = phase(out_own + theirs.astype(wide_type), hidden, grads)
     back = out[rows:].astype(half_type)
     back = [swap(back[k * rows : (k + 1) * rows], "grp", k + 1) for k in (1, 0, 2)]
     total, *sums = phase(out[:rows], *sums)

time: 76.2 us -> 75.2 us (0.987)
  starting transfers between devices: 32.2 us -> 30.7 us
    ppermute x31, starting transfers between devices: 32.2 us -> 30.7 us  [swap(): return lax.ppermute(value, axis, pairs)]
where the time goes in v7:
time: 75.2 us; the launch traced here: 75 us
  starting transfers between devices  30.7 us (41%)
  waiting for transfers between devices  24.1 us (32%)
  matrix products  9.71 us (13%)
  other arithmetic  5.6 us (7%)
  Pallas kernels  2.82 us (4%)
  between operations  1.38 us (2%)
    ppermute x31, starting transfers between devices, swap(): return lax.ppermute(value, axis, pairs)  30.7 us
    ppermute x31, waiting for transfers between devices, swap(): return lax.ppermute(value, axis, pairs)  24.1 us
    dot_general x24, matrix products, dot_part(): return lax.dot_general(weights, part, contract_last, **wide)  6.52 us
    pallas_call x1, Pallas kernels, in_gradients(): pl.pallas_call(kernel, out_shape=[jax.ShapeDtypeStruct((units, 4 * quarte...  2.82 us
    concatenate x6, other arithmetic, stack(): return jnp.concatenate(values, axis=0)  1.61 us
  transfers between devices with their start and end apart: 31, of which 13 were waited for; matrix products, arithmetic and copies ran while one was open for 20% of the time, Pallas kernels for 4%

profile of v7, /device:TPU:0, one launch (start us, length us, event | category | flops | bytes accessed | tf_op | source)
XLA Modules:
  0.0 75.0 jit_solution(18582514735183292)
XLA Ops:
  0.6 4.1 %collective-permute-start.3 = (bf16[128,512]{1,0:T(8,128)(2,1)}, bf16[128,512]{1,0:T(8,128)(2,1)S(1)}, u32[]{:S(2)}, u32[]{:S(2)}) collective-permute-start(bf16[128,512]{1,0:T(8,128)(2,1)} %param.7), channel_id=1, source_target_pairs={{0,4},{2,6},{4,0},{6,2},{1,5},{3,7},{5,1},{7,3},{8,12},{10,14},{12... | collective-permute-start | bytes 393224 | tf_op jit(solution)/shard_map/ppermute | solution.py:108
  4.7 2.4 %collective-permute-start.2 = (bf16[128,512]{1,0:T(8,128)(2,1)}, bf16[128,512]{1,0:T(8,128)(2,1)S(1)}, u32[]{:S(2)}, u32[]{:S(2)}) collective-permute-start(bf16[128,512]{1,0:T(8,128)(2,1)} %param.7), channel_id=1, source_target_pairs={{0,24},{8,16},{16,8},{24,0},{1,25},{9,17},{17,9},{25,1},{2,26},{10... | collective-permute-start | bytes 393224 | tf_op jit(solution)/shard_map/ppermute | solution.py:108
  7.2 0.5 collective-permute-start.1
  7.7 0.5 collective-permute-start
  8.2 1.3 %collective-permute-start.4 = (bf16[128,512]{1,0:T(8,128)(2,1)}, bf16[128,512]{1,0:T(8,128)(2,1)S(1)}, u32[]{:S(2)}, u32[]{:S(2)}) collective-permute-start(bf16[128,512]{1,0:T(8,128)(2,1)} %param.7), channel_id=1, source_target_pairs={{0,6},{2,4},{4,2},{6,0},{1,7},{3,5},{5,3},{7,1},{8,14},{10,12},{12... | collective-permute-start | bytes 393224 | tf_op jit(solution)/shard_map/ppermute | solution.py:108
  9.6 0.7 select_reduce_fusion
  10.3 1.5 %pad_maximum_fusion = bf16[384,2048]{1,0:T(8,128)(2,1)S(1)} fusion(bf16[192,2048]{1,0:T(8,128)(2,1)} %bitcast.49, bf16[192,2048]{1,0:T(8,128)(2,1)} %bitcast.50), kind=kLoop, calls=%fused_computation.2 | loop fusion | flops 3145728 | bytes 3145728 | tf_op jit(solution)/shard_map/concatenate | solution.py:120
  11.9 1.7 %collective-permute-done = bf16[128,512]{1,0:T(8,128)(2,1)S(1)} collective-permute-done((bf16[128,512]{1,0:T(8,128)(2,1)}, bf16[128,512]{1,0:T(8,128)(2,1)S(1)}, u32[]{:S(2)}, u32[]{:S(2)}) %collective-permute-start) | collective-permute-done | bytes 131104 | tf_op jit(solution)/shard_map/ppermute | solution.py:108
  13.7 1.6 %collective-permute-start.8 = (bf16[512,512]{1,0:T(8,128)(2,1)S(1)}, bf16[512,512]{1,0:T(8,128)(2,1)S(1)}, u32[]{:S(2)}, u32[]{:S(2)}) collective-permute-start(bf16[512,512]{1,0:T(8,128)(2,1)S(1)} %constant_dynamic-update-slice_fusion.refs_4_), channel_id=1, source_target_pairs={{0,2},{2,0},{4,6},{6,4},{1,3},{3,1},{5,7},{7,5},{8,10},{10,8},{12,... | collective-permute-start | bytes 1572872 | tf_op jit(solution)/shard_map/ppermute | solution.py:108
  15.5 3.1 %collective-permute-start.7 = (bf16[256,512]{1,0:T(8,128)(2,1)S(1)}, bf16[256,512]{1,0:T(8,128)(2,1)S(1)}, u32[]{:S(2)}, u32[]{:S(2)}) collective-permute-start(bf16[256,512]{1,0:T(8,128)(2,1)S(1)} %pad_maximum_fusion.9.refs_6_), channel_id=1, source_target_pairs={{0,24},{8,16},{16,8},{24,0},{1,25},{9,17},{17,9},{25,1},{2,26},{10... | collective-permute-start | bytes 786440 | tf_op jit(solution)/shard_map/ppermute | solution.py:108
  19.8 0.3 fusion.56
  20.1 0.6 collective-permute-start.5
  20.8 0.3 fusion.54
  22.1 5.2 %collective-permute-done.8.refs_5_ = bf16[512,512]{1,0:T(8,128)(2,1)S(1)} collective-permute-done((bf16[512,512]{1,0:T(8,128)(2,1)S(1)}, bf16[512,512]{1,0:T(8,128)(2,1)S(1)}, u32[]{:S(2)}, u32[]{:S(2)}) %collective-permute-start.8) | collective-permute-done | bytes 524320 | tf_op jit(solution)/shard_map/ppermute | solution.py:108
  27.7 0.5 collective-permute-start.16
  29.0 0.6 collective-permute-done.10.refs_11_
  29.6 3.0 %collective-permute-start.17 = (bf16[144,512]{1,0:T(8,128)(2,1)S(1)}, bf16[144,512]{1,0:T(8,128)(2,1)S(1)}, u32[]{:S(2)}, u32[]{:S(2)}) collective-permute-start(bf16[144,512]{1,0:T(8,128)(2,1)S(1)} %pad_maximum_fusion.10), channel_id=1, source_target_pairs={{0,6},{2,4},{4,2},{6,0},{1,7},{3,5},{5,3},{7,1},{8,14},{10,12},{12... | collective-permute-start | bytes 442376 | tf_op jit(solution)/shard_map/ppermute | solution.py:108
  34.1 0.6 collective-permute-start.12
  35.2 0.3 add_add_fusion.1
  36.0 0.3 fusion.30
  36.6 0.3 add_add_fusion
  37.1 1.6 %collective-permute-start.20 = (bf16[192,1024]{1,0:T(8,128)(2,1)S(1)}, bf16[192,1024]{1,0:T(8,128)(2,1)S(1)}, u32[]{:S(2)}, u32[]{:S(2)}) collective-permute-start(bf16[192,1024]{1,0:T(8,128)(2,1)S(1)} %fusion.77), channel_id=1, source_target_pairs={{0,16},{8,24},{16,0},{24,8},{1,17},{9,25},{17,1},{25,9},{2,18},{10... | collective-permute-start | bytes 1179656 | tf_op jit(solution)/shard_map/ppermute | solution.py:108
  39.2 2.5 %collective-permute-done.16 = bf16[144,512]{1,0:T(8,128)(2,1)S(1)} collective-permute-done((bf16[144,512]{1,0:T(8,128)(2,1)S(1)}, bf16[144,512]{1,0:T(8,128)(2,1)S(1)}, u32[]{:S(2)}, u32[]{:S(2)}) %collective-permute-start.16) | collective-permute-done | bytes 147488 | tf_op jit(solution)/shard_map/ppermute | solution.py:108
  41.7 3.3 %collective-permute-done.15 = bf16[144,512]{1,0:T(8,128)(2,1)S(1)} collective-permute-done((bf16[144,512]{1,0:T(8,128)(2,1)S(1)}, bf16[144,512]{1,0:T(8,128)(2,1)S(1)}, u32[]{:S(2)}, u32[]{:S(2)}) %collective-permute-start.15) | collective-permute-done | bytes 147488 | tf_op jit(solution)/shard_map/ppermute | solution.py:108
  45.1 3.6 %collective-permute-done.20 = bf16[192,1024]{1,0:T(8,128)(2,1)S(1)} collective-permute-done((bf16[192,1024]{1,0:T(8,128)(2,1)S(1)}, bf16[192,1024]{1,0:T(8,128)(2,1)S(1)}, u32[]{:S(2)}, u32[]{:S(2)}) %collective-permute-start.20) | collective-permute-done | bytes 393248 | tf_op jit(solution)/shard_map/ppermute | solution.py:108
  48.7 1.6 %collective-permute-start.22 = (bf16[96,1024]{1,0:T(8,128)(2,1)S(1)}, bf16[96,1024]{1,0:T(8,128)(2,1)S(1)}, u32[]{:S(2)}, u32[]{:S(2)}) collective-permute-start(bf16[96,1024]{1,0:T(8,128)(2,1)S(1)} %slice.231), channel_id=1, source_target_pairs={{0,8},{8,0},{16,24},{24,16},{1,9},{9,1},{17,25},{25,17},{2,10},{10... | collective-permute-start | bytes 589832 | tf_op jit(solution)/shard_map/ppermute | solution.py:108
  50.3 0.4 collective-permute-start.21
  50.8 0.3 fusion
  51.2 1.0 %fusion.117 = (bf16[768,1024]{1,0:T(8,128)(2,1)S(1)}, f32[768,1024]{1,0:T(8,128)S(1)}) fusion(bf16[768,512]{1,0:T(8,128)(2,1)S(1)} %pad_maximum_fusion.1, bf16[1024,512]{1,0:T(8,128)(2,1)S(1)} %fusion), kind=kOutput, calls=%fused_computation.192 | convolution fusion | flops 806092800 | bytes 6553600 | tf_op jit(solution)/shard_map/dot_general | solution.py:248
  52.2 1.8 %collective-permute-start.26 = (bf16[96,1024]{1,0:T(8,128)(2,1)S(1)}, bf16[96,1024]{1,0:T(8,128)(2,1)S(1)}, u32[]{:S(2)}, u32[]{:S(2)}) collective-permute-start(bf16[96,1024]{1,0:T(8,128)(2,1)S(1)} %get-tuple-element.121), channel_id=1, source_target_pairs={{0,8},{8,0},{16,24},{24,16},{1,9},{9,1},{17,25},{25,17},{2,10},{10... | collective-permute-start | bytes 589832 | tf_op jit(solution)/shard_map/ppermute | solution.py:108
  54.1 0.5 collective-permute-start.24
  54.6 1.6 %collective-permute-done.22 = bf16[96,1024]{1,0:T(8,128)(2,1)S(1)} collective-permute-done((bf16[96,1024]{1,0:T(8,128)(2,1)S(1)}, bf16[96,1024]{1,0:T(8,128)(2,1)S(1)}, u32[]{:S(2)}, u32[]{:S(2)}) %collective-permute-start.22) | collective-permute-done | bytes 196640 | tf_op jit(solution)/shard_map/ppermute | solution.py:108
  56.2 1.4 %collective-permute-done.21 = bf16[96,1024]{1,0:T(8,128)(2,1)S(1)} collective-permute-done((bf16[96,1024]{1,0:T(8,128)(2,1)S(1)}, bf16[96,1024]{1,0:T(8,128)(2,1)S(1)}, u32[]{:S(2)}, u32[]{:S(2)}) %collective-permute-start.21) | collective-permute-done | bytes 196640 | tf_op jit(solution)/shard_map/ppermute | solution.py:108
  57.8 0.6 fusion.3
  58.5 0.6 fusion.5
  59.1 0.4 collective-permute-done.26
  59.5 1.3 %collective-permute-done.24 = bf16[96,1024]{1,0:T(8,128)(2,1)S(1)} collective-permute-done((bf16[96,1024]{1,0:T(8,128)(2,1)S(1)}, bf16[96,1024]{1,0:T(8,128)(2,1)S(1)}, u32[]{:S(2)}, u32[]{:S(2)}) %collective-permute-start.24) | collective-permute-done | bytes 196640 | tf_op jit(solution)/shard_map/ppermute | solution.py:108
  60.9 0.6 collective-permute-start.25
  61.6 1.6 %collective-permute-start.27 = (bf16[192,1024]{1,0:T(8,128)(2,1)S(1)}, bf16[192,1024]{1,0:T(8,128)(2,1)S(1)}, u32[]{:S(2)}, u32[]{:S(2)}) collective-permute-start(bf16[192,1024]{1,0:T(8,128)(2,1)S(1)} %pad_maximum_fusion.4), channel_id=1, source_target_pairs={{0,16},{8,24},{16,0},{24,8},{1,17},{9,25},{17,1},{25,9},{2,18},{10... | collective-permute-start | bytes 1179656 | tf_op jit(solution)/shard_map/ppermute | solution.py:108
  63.4 1.1 %collective-permute-start.28 = (bf16[128,512]{1,0:T(8,128)(2,1)S(1)}, bf16[128,512]{1,0:T(8,128)(2,1)S(1)}, u32[]{:S(2)}, u32[]{:S(2)}) collective-permute-start(bf16[128,512]{1,0:T(8,128)(2,1)S(1)} %get-tuple-element.132), channel_id=1, source_target_pairs={{0,4},{2,6},{4,0},{6,2},{1,5},{3,7},{5,1},{7,3},{8,12},{10,14},{12... | collective-permute-start | bytes 393224 | tf_op jit(solution)/shard_map/ppermute | solution.py:108
  64.6 0.9 %collective-permute-start.30 = (bf16[128,512]{1,0:T(8,128)(2,1)S(1)}, bf16[128,512]{1,0:T(8,128)(2,1)S(1)}, u32[]{:S(2)}, u32[]{:S(2)}) collective-permute-start(bf16[128,512]{1,0:T(8,128)(2,1)S(1)} %get-tuple-element.133), channel_id=1, source_target_pairs={{0,6},{2,4},{4,2},{6,0},{1,7},{3,5},{5,3},{7,1},{8,14},{10,12},{12... | collective-permute-start | bytes 393224 | tf_op jit(solution)/shard_map/ppermute | solution.py:108
  65.4 1.6 %collective-permute-start.29 = (bf16[128,512]{1,0:T(8,128)(2,1)S(1)}, bf16[128,512]{1,0:T(8,128)(2,1)S(1)}, u32[]{:S(2)}, u32[]{:S(2)}) collective-permute-start(bf16[128,512]{1,0:T(8,128)(2,1)S(1)} %get-tuple-element.134), channel_id=1, source_target_pairs={{0,2},{2,0},{4,6},{6,4},{1,3},{3,1},{5,7},{7,5},{8,10},{10,8},{12,... | collective-permute-start | bytes 393224 | tf_op jit(solution)/shard_map/ppermute | solution.py:108
  67.0 1.0 %convolution_convert_fusion = bf16[768,512]{1,0:T(8,128)(2,1)S(1)} fusion(bf16[768,1024]{1,0:T(8,128)(2,1)S(1)} %constant_dynamic-update-slice_fusion.9, bf16[1024,512]{1,0:T(8,128)(2,1)S(1)} %fusion), kind=kOutput, calls=%fused_computation.3 | convolution fusion | flops 805699584 | bytes 3407872 | tf_op jit(solution)/shard_map/dot_general | solution.py:273
  68.1 0.9 %maximum_bitcast_fusion = bf16[1,768,512]{2,1,0:T(8,128)(2,1)} fusion(bf16[192,512]{1,0:T(8,128)(2,1)S(1)} %get-tuple-element.125, bf16[192,512]{1,0:T(8,128)(2,1)S(1)} %get-tuple-element.126, bf16[192,512]{1,0:T(8,128)(2,1)S(1)} %get-tuple-element.127, bf16[192,512]{1,0:T(8,128)(2,1)S(1)} %get-tuple-element.124), kind=kLoop, calls=%fused_computation.27 | loop fusion | flops 3145728 | bytes 1572864 | tf_op jit(solution)/shard_map/broadcast_in_dim | solution.py:280
  69.0 2.1 %collective-permute-done.25.x_ref = bf16[192,1024]{1,0:T(8,128)(2,1)S(1)} collective-permute-done((bf16[192,1024]{1,0:T(8,128)(2,1)S(1)}, bf16[192,1024]{1,0:T(8,128)(2,1)S(1)}, u32[]{:S(2)}, u32[]{:S(2)}) %collective-permute-start.25) | collective-permute-done | bytes 393248 | tf_op jit(solution)/shard_map/ppermute | solution.py:108
  71.1 0.3 collective-permute-done.27.y_ref
  71.4 2.8 %shard_map.102 = (bf16[192,2048]{1,0:T(8,128)(2,1)}, bf16[192,2048]{1,0:T(8,128)(2,1)}) custom-call(s32[1]{0:T(128)} %bitcast.15.place_ref, f32[192,1024]{1,0:T(8,128)S(1)} %slice.229.share_ref, bf16[192,1024]{1,0:T(8,128)(2,1)S(1)} %collective-permute-done.25.x_ref, bf16[192,1024]{1,0:T(8,128)(2,1)S(1)} %collective-permute-done.27.y_ref, ...), custom_call_target="tpu_custom_call" | custom-call | tf_op jit(solution)/shard_map/pallas_call | solution.py:170
  74.3 0.7 add_convert_fusion
  (108 shorter events, 8.0 us)
Async XLA Ops:
  0.6 14.8 %collective-permute-start.3 = (bf16[128,512]{1,0:T(8,128)(2,1)}, bf16[128,512]{1,0:T(8,128)(2,1)S(1)}, u32[]{:S(2)}, u32[]{:S(2)}) collective-permute-start(bf16[128,512]{1,0:T(8,128)(2,1)} %param.7), channel_id=1, source_target_pairs={{0,4},{2,6},{4,0},{6,2},{1,5},{3,7},{5,1},{7,3},{8,12},{10,14},{12... | collective-permute-start | bytes 393224 | tf_op jit(solution)/shard_map/ppermute | solution.py:108
  4.7 9.0 %collective-permute-start.2 = (bf16[128,512]{1,0:T(8,128)(2,1)}, bf16[128,512]{1,0:T(8,128)(2,1)S(1)}, u32[]{:S(2)}, u32[]{:S(2)}) collective-permute-start(bf16[128,512]{1,0:T(8,128)(2,1)} %param.7), channel_id=1, source_target_pairs={{0,24},{8,16},{16,8},{24,0},{1,25},{9,17},{17,9},{25,1},{2,26},{10... | collective-permute-start | bytes 393224 | tf_op jit(solution)/shard_map/ppermute | solution.py:108
  7.2 6.5 %collective-permute-start.1 = (bf16[128,512]{1,0:T(8,128)(2,1)}, bf16[128,512]{1,0:T(8,128)(2,1)S(1)}, u32[]{:S(2)}, u32[]{:S(2)}) collective-permute-start(bf16[128,512]{1,0:T(8,128)(2,1)} %param.7), channel_id=1, source_target_pairs={{0,16},{8,24},{16,0},{24,8},{1,17},{9,25},{17,1},{25,9},{2,18},{10... | collective-permute-start | bytes 393224 | tf_op jit(solution)/shard_map/ppermute | solution.py:108
  7.7 6.0 %collective-permute-start = (bf16[128,512]{1,0:T(8,128)(2,1)}, bf16[128,512]{1,0:T(8,128)(2,1)S(1)}, u32[]{:S(2)}, u32[]{:S(2)}) collective-permute-start(bf16[128,512]{1,0:T(8,128)(2,1)} %param.7), channel_id=1, source_target_pairs={{0,8},{8,0},{16,24},{24,16},{1,9},{9,1},{17,25},{25,17},{2,10},{10... | collective-permute-start | bytes 393224 | tf_op jit(solution)/shard_map/ppermute | solution.py:108
  8.2 7.2 %collective-permute-start.4 = (bf16[128,512]{1,0:T(8,128)(2,1)}, bf16[128,512]{1,0:T(8,128)(2,1)S(1)}, u32[]{:S(2)}, u32[]{:S(2)}) collective-permute-start(bf16[128,512]{1,0:T(8,128)(2,1)} %param.7), channel_id=1, source_target_pairs={{0,6},{2,4},{4,2},{6,0},{1,7},{3,5},{5,3},{7,1},{8,14},{10,12},{12... | collective-permute-start | bytes 393224 | tf_op jit(solution)/shard_map/ppermute | solution.py:108
  10.3 1.5 %copy-start.2 = (bf16[128,512]{1,0:T(8,128)(2,1)S(1)}, bf16[128,512]{1,0:T(8,128)(2,1)}, u32[]{:S(2)}) copy-start(bf16[128,512]{1,0:T(8,128)(2,1)} %param.8) | copy-start | bytes 393220
  10.3 1.6 %copy-start.3 = (bf16[128,512]{1,0:T(8,128)(2,1)S(1)}, bf16[128,512]{1,0:T(8,128)(2,1)}, u32[]{:S(2)}) copy-start(bf16[128,512]{1,0:T(8,128)(2,1)} %param.7) | copy-start | bytes 393220
  13.7 13.6 %collective-permute-start.8 = (bf16[512,512]{1,0:T(8,128)(2,1)S(1)}, bf16[512,512]{1,0:T(8,128)(2,1)S(1)}, u32[]{:S(2)}, u32[]{:S(2)}) collective-permute-start(bf16[512,512]{1,0:T(8,128)(2,1)S(1)} %constant_dynamic-update-slice_fusion.refs_4_), channel_id=1, source_target_pairs={{0,2},{2,0},{4,6},{6,4},{1,3},{3,1},{5,7},{7,5},{8,10},{10,8},{12,... | collective-permute-start | bytes 1572872 | tf_op jit(solution)/shard_map/ppermute | solution.py:108
  15.4 4.7 %collective-permute-start.11 = (bf16[256,512]{1,0:T(8,128)(2,1)S(1)}, bf16[256,512]{1,0:T(8,128)(2,1)S(1)}, u32[]{:S(2)}, u32[]{:S(2)}) collective-permute-start(bf16[256,512]{1,0:T(8,128)(2,1)S(1)} %pad_maximum_fusion.9.refs_6_), channel_id=1, source_target_pairs={{0,1},{1,0},{2,3},{3,2},{4,5},{5,4},{6,7},{7,6},{8,9},{9,8},{10,11... | collective-permute-start | bytes 786440 | tf_op jit(solution)/shard_map/ppermute | solution.py:108
  15.5 18.2 %collective-permute-start.7 = (bf16[256,512]{1,0:T(8,128)(2,1)S(1)}, bf16[256,512]{1,0:T(8,128)(2,1)S(1)}, u32[]{:S(2)}, u32[]{:S(2)}) collective-permute-start(bf16[256,512]{1,0:T(8,128)(2,1)S(1)} %pad_maximum_fusion.9.refs_6_), channel_id=1, source_target_pairs={{0,24},{8,16},{16,8},{24,0},{1,25},{9,17},{17,9},{25,1},{2,26},{10... | collective-permute-start | bytes 786440 | tf_op jit(solution)/shard_map/ppermute | solution.py:108
  18.6 15.1 %collective-permute-start.6 = (bf16[256,512]{1,0:T(8,128)(2,1)S(1)}, bf16[256,512]{1,0:T(8,128)(2,1)S(1)}, u32[]{:S(2)}, u32[]{:S(2)}) collective-permute-start(bf16[256,512]{1,0:T(8,128)(2,1)S(1)} %pad_maximum_fusion.9.refs_6_), channel_id=1, source_target_pairs={{0,16},{8,24},{16,0},{24,8},{1,17},{9,25},{17,1},{25,9},{2,18},{10... | collective-permute-start | bytes 786440 | tf_op jit(solution)/shard_map/ppermute | solution.py:108
  18.6 2.5 %collective-permute-start.9 = (bf16[512,512]{1,0:T(8,128)(2,1)S(1)}, bf16[512,512]{1,0:T(8,128)(2,1)S(1)}, u32[]{:S(2)}, u32[]{:S(2)}) collective-permute-start(bf16[512,512]{1,0:T(8,128)(2,1)S(1)} %constant_dynamic-update-slice_fusion.refs_4_), channel_id=1, source_target_pairs={{0,1},{1,0},{2,3},{3,2},{4,5},{5,4},{6,7},{7,6},{8,9},{9,8},{10,11... | collective-permute-start | bytes 1572872 | tf_op jit(solution)/shard_map/ppermute | solution.py:108
  20.1 13.6 %collective-permute-start.5 = (bf16[256,512]{1,0:T(8,128)(2,1)S(1)}, bf16[256,512]{1,0:T(8,128)(2,1)S(1)}, u32[]{:S(2)}, u32[]{:S(2)}) collective-permute-start(bf16[256,512]{1,0:T(8,128)(2,1)S(1)} %pad_maximum_fusion.9.refs_6_), channel_id=1, source_target_pairs={{0,8},{8,0},{16,24},{24,16},{1,9},{9,1},{17,25},{25,17},{2,10},{10... | collective-permute-start | bytes 786440 | tf_op jit(solution)/shard_map/ppermute | solution.py:108
  27.6 2.0 %collective-permute-start.10 = (bf16[512,512]{1,0:T(8,128)(2,1)S(1)}, bf16[512,512]{1,0:T(8,128)(2,1)S(1)}, u32[]{:S(2)}, u32[]{:S(2)}) collective-permute-start(bf16[512,512]{1,0:T(8,128)(2,1)S(1)} %collective-permute-done.8.refs_5_), channel_id=1, source_target_pairs={{0,1},{1,0},{2,3},{3,2},{4,5},{5,4},{6,7},{7,6},{8,9},{9,8},{10,11... | collective-permute-start | bytes 1572872 | tf_op jit(solution)/shard_map/ppermute | solution.py:108
  27.7 13.9 %collective-permute-start.16 = (bf16[144,512]{1,0:T(8,128)(2,1)S(1)}, bf16[144,512]{1,0:T(8,128)(2,1)S(1)}, u32[]{:S(2)}, u32[]{:S(2)}) collective-permute-start(bf16[144,512]{1,0:T(8,128)(2,1)S(1)} %pad_maximum_fusion.10), channel_id=1, source_target_pairs={{0,4},{2,6},{4,0},{6,2},{1,5},{3,7},{5,1},{7,3},{8,12},{10,14},{12... | collective-permute-start | bytes 442376 | tf_op jit(solution)/shard_map/ppermute | solution.py:108
  29.6 12.0 %collective-permute-start.17 = (bf16[144,512]{1,0:T(8,128)(2,1)S(1)}, bf16[144,512]{1,0:T(8,128)(2,1)S(1)}, u32[]{:S(2)}, u32[]{:S(2)}) collective-permute-start(bf16[144,512]{1,0:T(8,128)(2,1)S(1)} %pad_maximum_fusion.10), channel_id=1, source_target_pairs={{0,6},{2,4},{4,2},{6,0},{1,7},{3,5},{5,3},{7,1},{8,14},{10,12},{12... | collective-permute-start | bytes 442376 | tf_op jit(solution)/shard_map/ppermute | solution.py:108
  33.7 2.3 %collective-permute-start.13 = (bf16[256,512]{1,0:T(8,128)(2,1)S(1)}, bf16[256,512]{1,0:T(8,128)(2,1)S(1)}, u32[]{:S(2)}, u32[]{:S(2)}) collective-permute-start(bf16[256,512]{1,0:T(8,128)(2,1)S(1)} %collective-permute-done.6.refs_8_), channel_id=1, source_target_pairs={{0,1},{1,0},{2,3},{3,2},{4,5},{5,4},{6,7},{7,6},{8,9},{9,8},{10,11... | collective-permute-start | bytes 786440 | tf_op jit(solution)/shard_map/ppermute | solution.py:108
  34.1 2.2 %collective-permute-start.12 = (bf16[256,512]{1,0:T(8,128)(2,1)S(1)}, bf16[256,512]{1,0:T(8,128)(2,1)S(1)}, u32[]{:S(2)}, u32[]{:S(2)}) collective-permute-start(bf16[256,512]{1,0:T(8,128)(2,1)S(1)} %collective-permute-done.5.refs_7_), channel_id=1, source_target_pairs={{0,1},{1,0},{2,3},{3,2},{4,5},{5,4},{6,7},{7,6},{8,9},{9,8},{10,11... | collective-permute-start | bytes 786440 | tf_op jit(solution)/shard_map/ppermute | solution.py:108
  35.0 1.7 %collective-permute-start.14 = (bf16[256,512]{1,0:T(8,128)(2,1)S(1)}, bf16[256,512]{1,0:T(8,128)(2,1)S(1)}, u32[]{:S(2)}, u32[]{:S(2)}) collective-permute-start(bf16[256,512]{1,0:T(8,128)(2,1)S(1)} %collective-permute-done.7.refs_9_), channel_id=1, source_target_pairs={{0,1},{1,0},{2,3},{3,2},{4,5},{5,4},{6,7},{7,6},{8,9},{9,8},{10,11... | collective-permute-start | bytes 786440 | tf_op jit(solution)/shard_map/ppermute | solution.py:108
  36.6 2.1 %copy-start.1 = (bf16[1,768,512]{2,1,0:T(8,128)(2,1)S(1)}, bf16[1,768,512]{2,1,0:T(8,128)(2,1)}, u32[]{:S(2)}) copy-start(bf16[1,768,512]{2,1,0:T(8,128)(2,1)} %param.13) | copy-start | bytes 2359300
  37.1 11.6 %collective-permute-start.20 = (bf16[192,1024]{1,0:T(8,128)(2,1)S(1)}, bf16[192,1024]{1,0:T(8,128)(2,1)S(1)}, u32[]{:S(2)}, u32[]{:S(2)}) collective-permute-start(bf16[192,1024]{1,0:T(8,128)(2,1)S(1)} %fusion.77), channel_id=1, source_target_pairs={{0,16},{8,24},{16,0},{24,8},{1,17},{9,25},{17,1},{25,9},{2,18},{10... | collective-permute-start | bytes 1179656 | tf_op jit(solution)/shard_map/ppermute | solution.py:108
  38.7 11.6 %collective-permute-start.19 = (bf16[192,1024]{1,0:T(8,128)(2,1)S(1)}, bf16[192,1024]{1,0:T(8,128)(2,1)S(1)}, u32[]{:S(2)}, u32[]{:S(2)}) collective-permute-start(bf16[192,1024]{1,0:T(8,128)(2,1)S(1)} %fusion.77), channel_id=1, source_target_pairs={{0,8},{8,0},{16,24},{24,16},{1,9},{9,1},{17,25},{25,17},{2,10},{10... | collective-permute-start | bytes 1179656 | tf_op jit(solution)/shard_map/ppermute | solution.py:108
  38.9 6.0 %collective-permute-start.15 = (bf16[144,512]{1,0:T(8,128)(2,1)S(1)}, bf16[144,512]{1,0:T(8,128)(2,1)S(1)}, u32[]{:S(2)}, u32[]{:S(2)}) collective-permute-start(bf16[144,512]{1,0:T(8,128)(2,1)S(1)} %pad_maximum_fusion.10), channel_id=1, source_target_pairs={{0,2},{2,0},{4,6},{6,4},{1,3},{3,1},{5,7},{7,5},{8,10},{10,8},{12,... | collective-permute-start | bytes 442376 | tf_op jit(solution)/shard_map/ppermute | solution.py:108
  45.0 5.7 %collective-permute-start.18 = (bf16[4,144,512]{2,1,0:T(8,128)(2,1)S(1)}, bf16[4,144,512]{2,1,0:T(8,128)(2,1)S(1)}, u32[]{:S(2)}, u32[]{:S(2)}) collective-permute-start(bf16[4,144,512]{2,1,0:T(8,128)(2,1)S(1)} %pad_maximum_fusion.2), channel_id=1, source_target_pairs={{0,1},{1,0},{2,3},{3,2},{4,5},{5,4},{6,7},{7,6},{8,9},{9,8},{10,11... | collective-permute-start | bytes 1769480 | tf_op jit(solution)/shard_map/ppermute | solution.py:108
  48.7 7.5 %collective-permute-start.22 = (bf16[96,1024]{1,0:T(8,128)(2,1)S(1)}, bf16[96,1024]{1,0:T(8,128)(2,1)S(1)}, u32[]{:S(2)}, u32[]{:S(2)}) collective-permute-start(bf16[96,1024]{1,0:T(8,128)(2,1)S(1)} %slice.231), channel_id=1, source_target_pairs={{0,8},{8,0},{16,24},{24,16},{1,9},{9,1},{17,25},{25,17},{2,10},{10... | collective-permute-start | bytes 589832 | tf_op jit(solution)/shard_map/ppermute | solution.py:108
  50.3 7.3 %collective-permute-start.21 = (bf16[96,1024]{1,0:T(8,128)(2,1)S(1)}, bf16[96,1024]{1,0:T(8,128)(2,1)S(1)}, u32[]{:S(2)}, u32[]{:S(2)}) collective-permute-start(bf16[96,1024]{1,0:T(8,128)(2,1)S(1)} %slice.230), channel_id=1, source_target_pairs={{0,16},{8,24},{16,0},{24,8},{1,17},{9,25},{17,1},{25,9},{2,18},{10... | collective-permute-start | bytes 589832 | tf_op jit(solution)/shard_map/ppermute | solution.py:108
  52.2 7.3 %collective-permute-start.26 = (bf16[96,1024]{1,0:T(8,128)(2,1)S(1)}, bf16[96,1024]{1,0:T(8,128)(2,1)S(1)}, u32[]{:S(2)}, u32[]{:S(2)}) collective-permute-start(bf16[96,1024]{1,0:T(8,128)(2,1)S(1)} %get-tuple-element.121), channel_id=1, source_target_pairs={{0,8},{8,0},{16,24},{24,16},{1,9},{9,1},{17,25},{25,17},{2,10},{10... | collective-permute-start | bytes 589832 | tf_op jit(solution)/shard_map/ppermute | solution.py:108
  54.1 6.8 %collective-permute-start.24 = (bf16[96,1024]{1,0:T(8,128)(2,1)S(1)}, bf16[96,1024]{1,0:T(8,128)(2,1)S(1)}, u32[]{:S(2)}, u32[]{:S(2)}) collective-permute-start(bf16[96,1024]{1,0:T(8,128)(2,1)S(1)} %get-tuple-element.123), channel_id=1, source_target_pairs={{0,16},{8,24},{16,0},{24,8},{1,17},{9,25},{17,1},{25,9},{2,18},{10... | collective-permute-start | bytes 589832 | tf_op jit(solution)/shard_map/ppermute | solution.py:108
  58.4 4.8 %collective-permute-start.23 = (bf16[512,512]{1,0:T(8,128)(2,1)S(1)}, bf16[512,512]{1,0:T(8,128)(2,1)S(1)}, u32[]{:S(2)}, u32[]{:S(2)}) collective-permute-start(bf16[512,512]{1,0:T(8,128)(2,1)S(1)} %fusion.3), channel_id=1, source_target_pairs={{0,1},{1,0},{2,3},{3,2},{4,5},{5,4},{6,7},{7,6},{8,9},{9,8},{10,11... | collective-permute-start | bytes 1572872 | tf_op jit(solution)/shard_map/ppermute | solution.py:108
  60.9 10.2 %collective-permute-start.25 = (bf16[192,1024]{1,0:T(8,128)(2,1)S(1)}, bf16[192,1024]{1,0:T(8,128)(2,1)S(1)}, u32[]{:S(2)}, u32[]{:S(2)}) collective-permute-start(bf16[192,1024]{1,0:T(8,128)(2,1)S(1)} %pad_maximum_fusion.3), channel_id=1, source_target_pairs={{0,8},{8,0},{16,24},{24,16},{1,9},{9,1},{17,25},{25,17},{2,10},{10... | collective-permute-start | bytes 1179656 | tf_op jit(solution)/shard_map/ppermute | solution.py:108
  61.6 9.9 %collective-permute-start.27 = (bf16[192,1024]{1,0:T(8,128)(2,1)S(1)}, bf16[192,1024]{1,0:T(8,128)(2,1)S(1)}, u32[]{:S(2)}, u32[]{:S(2)}) collective-permute-start(bf16[192,1024]{1,0:T(8,128)(2,1)S(1)} %pad_maximum_fusion.4), channel_id=1, source_target_pairs={{0,16},{8,24},{16,0},{24,8},{1,17},{9,25},{17,1},{25,9},{2,18},{10... | collective-permute-start | bytes 1179656 | tf_op jit(solution)/shard_map/ppermute | solution.py:108
  63.3 4.7 %copy-start = (f32[512,512]{1,0:T(8,128)}, f32[512,512]{1,0:T(8,128)S(1)}, u32[]{:S(2)}) copy-start(f32[512,512]{1,0:T(8,128)S(1)} %convert_add_fusion) | copy-start | bytes 3145732
  63.4 10.8 %collective-permute-start.28 = (bf16[128,512]{1,0:T(8,128)(2,1)S(1)}, bf16[128,512]{1,0:T(8,128)(2,1)S(1)}, u32[]{:S(2)}, u32[]{:S(2)}) collective-permute-start(bf16[128,512]{1,0:T(8,128)(2,1)S(1)} %get-tuple-element.132), channel_id=1, source_target_pairs={{0,4},{2,6},{4,0},{6,2},{1,5},{3,7},{5,1},{7,3},{8,12},{10,14},{12... | collective-permute-start | bytes 393224 | tf_op jit(solution)/shard_map/ppermute | solution.py:108
  64.6 9.7 %collective-permute-start.30 = (bf16[128,512]{1,0:T(8,128)(2,1)S(1)}, bf16[128,512]{1,0:T(8,128)(2,1)S(1)}, u32[]{:S(2)}, u32[]{:S(2)}) collective-permute-start(bf16[128,512]{1,0:T(8,128)(2,1)S(1)} %get-tuple-element.133), channel_id=1, source_target_pairs={{0,6},{2,4},{4,2},{6,0},{1,7},{3,5},{5,3},{7,1},{8,14},{10,12},{12... | collective-permute-start | bytes 393224 | tf_op jit(solution)/shard_map/ppermute | solution.py:108
  65.4 8.9 %collective-permute-start.29 = (bf16[128,512]{1,0:T(8,128)(2,1)S(1)}, bf16[128,512]{1,0:T(8,128)(2,1)S(1)}, u32[]{:S(2)}, u32[]{:S(2)}) collective-permute-start(bf16[128,512]{1,0:T(8,128)(2,1)S(1)} %get-tuple-element.134), channel_id=1, source_target_pairs={{0,2},{2,0},{4,6},{6,4},{1,3},{3,1},{5,7},{7,5},{8,10},{10,8},{12,... | collective-permute-start | bytes 393224 | tf_op jit(solution)/shard_map/ppermute | solution.py:108
  71.4 2.9 %slice-start = ((f32[512,512]{1,0:T(8,128)}), f32[128,512]{1,0:T(8,128)S(1)}, s32[]{:S(2)}) async-start(f32[512,512]{1,0:T(8,128)} %copy-done), calls=%async_computation | async-start | bytes 524288 | tf_op jit(solution)/shard_map/slice | solution.py:271

commit v8 on v7

--- a/solution.py
+++ b/solution.py
@@ -214,7 +214,7 @@
     p2 = [far] + spread(far)
     late, own_there = phase(payload, own_there)
     g2 = swap(late, "grp", 2)
-    late, p1, *pre_own = phase(payload, p1, *pre_own)
+    late, p1, *pre_own, pre_far[0], pre_far[1] = phase(payload, p1, *pre_own, *pre_far)
     g3 = swap(late, "grp", 3)
     p1_there = to_core(p1)
     pre_near = [block_part(in_weights, block) for block in (p1, p1_there)]

time: 75.2 us -> 75.2 us (level)
  no operation moved by 1% of the time
where the time goes in v8:
time: 75.2 us; the launch traced here: 75 us
  starting transfers between devices  30.7 us (41%)
  waiting for transfers between devices  24.1 us (32%)
  matrix products  9.71 us (13%)
  other arithmetic  5.6 us (7%)
  Pallas kernels  2.82 us (4%)
  between operations  1.38 us (2%)
    ppermute x31, starting transfers between devices, swap(): return lax.ppermute(value, axis, pairs)  30.7 us
    ppermute x31, waiting for transfers between devices, swap(): return lax.ppermute(value, axis, pairs)  24.1 us
    dot_general x24, matrix products, dot_part(): return lax.dot_general(weights, part, contract_last, **wide)  6.52 us
    pallas_call x1, Pallas kernels, in_gradients(): pl.pallas_call(kernel, out_shape=[jax.ShapeDtypeStruct((units, 4 * quarte...  2.82 us
    concatenate x6, other arithmetic, stack(): return jnp.concatenate(values, axis=0)  1.61 us
  transfers between devices with their start and end apart: 31, of which 13 were waited for; matrix products, arithmetic and copies ran while one was open for 20% of the time, Pallas kernels for 4%

profile of v8, /device:TPU:0, one launch (start us, length us, event | category | flops | bytes accessed | tf_op | source)
XLA Modules:
  0.0 75.0 jit_solution(18582514735183292)
XLA Ops:
  0.6 4.1 %collective-permute-start.3 = (bf16[128,512]{1,0:T(8,128)(2,1)}, bf16[128,512]{1,0:T(8,128)(2,1)S(1)}, u32[]{:S(2)}, u32[]{:S(2)}) collective-permute-start(bf16[128,512]{1,0:T(8,128)(2,1)} %param.7), channel_id=1, source_target_pairs={{0,4},{2,6},{4,0},{6,2},{1,5},{3,7},{5,1},{7,3},{8,12},{10,14},{12... | collective-permute-start | bytes 393224 | tf_op jit(solution)/shard_map/ppermute | solution.py:108
  4.7 2.4 %collective-permute-start.2 = (bf16[128,512]{1,0:T(8,128)(2,1)}, bf16[128,512]{1,0:T(8,128)(2,1)S(1)}, u32[]{:S(2)}, u32[]{:S(2)}) collective-permute-start(bf16[128,512]{1,0:T(8,128)(2,1)} %param.7), channel_id=1, source_target_pairs={{0,24},{8,16},{16,8},{24,0},{1,25},{9,17},{17,9},{25,1},{2,26},{10... | collective-permute-start | bytes 393224 | tf_op jit(solution)/shard_map/ppermute | solution.py:108
  7.2 0.5 collective-permute-start.1
  7.7 0.5 collective-permute-start
  8.2 1.3 %collective-permute-start.4 = (bf16[128,512]{1,0:T(8,128)(2,1)}, bf16[128,512]{1,0:T(8,128)(2,1)S(1)}, u32[]{:S(2)}, u32[]{:S(2)}) collective-permute-start(bf16[128,512]{1,0:T(8,128)(2,1)} %param.7), channel_id=1, source_target_pairs={{0,6},{2,4},{4,2},{6,0},{1,7},{3,5},{5,3},{7,1},{8,14},{10,12},{12... | collective-permute-start | bytes 393224 | tf_op jit(solution)/shard_map/ppermute | solution.py:108
  9.6 0.7 select_reduce_fusion
  10.3 1.5 %pad_maximum_fusion = bf16[384,2048]{1,0:T(8,128)(2,1)S(1)} fusion(bf16[192,2048]{1,0:T(8,128)(2,1)} %bitcast.49, bf16[192,2048]{1,0:T(8,128)(2,1)} %bitcast.50), kind=kLoop, calls=%fused_computation.2 | loop fusion | flops 3145728 | bytes 3145728 | tf_op jit(solution)/shard_map/concatenate | solution.py:120
  11.9 1.7 %collective-permute-done = bf16[128,512]{1,0:T(8,128)(2,1)S(1)} collective-permute-done((bf16[128,512]{1,0:T(8,128)(2,1)}, bf16[128,512]{1,0:T(8,128)(2,1)S(1)}, u32[]{:S(2)}, u32[]{:S(2)}) %collective-permute-start) | collective-permute-done | bytes 131104 | tf_op jit(solution)/shard_map/ppermute | solution.py:108
  13.7 1.6 %collective-permute-start.8 = (bf16[512,512]{1,0:T(8,128)(2,1)S(1)}, bf16[512,512]{1,0:T(8,128)(2,1)S(1)}, u32[]{:S(2)}, u32[]{:S(2)}) collective-permute-start(bf16[512,512]{1,0:T(8,128)(2,1)S(1)} %constant_dynamic-update-slice_fusion.refs_4_), channel_id=1, source_target_pairs={{0,2},{2,0},{4,6},{6,4},{1,3},{3,1},{5,7},{7,5},{8,10},{10,8},{12,... | collective-permute-start | bytes 1572872 | tf_op jit(solution)/shard_map/ppermute | solution.py:108
  15.5 3.1 %collective-permute-start.7 = (bf16[256,512]{1,0:T(8,128)(2,1)S(1)}, bf16[256,512]{1,0:T(8,128)(2,1)S(1)}, u32[]{:S(2)}, u32[]{:S(2)}) collective-permute-start(bf16[256,512]{1,0:T(8,128)(2,1)S(1)} %pad_maximum_fusion.9.refs_6_), channel_id=1, source_target_pairs={{0,24},{8,16},{16,8},{24,0},{1,25},{9,17},{17,9},{25,1},{2,26},{10... | collective-permute-start | bytes 786440 | tf_op jit(solution)/shard_map/ppermute | solution.py:108
  19.8 0.3 fusion.56
  20.1 0.6 collective-permute-start.5
  20.8 0.3 fusion.54
  22.1 5.2 %collective-permute-done.8.refs_5_ = bf16[512,512]{1,0:T(8,128)(2,1)S(1)} collective-permute-done((bf16[512,512]{1,0:T(8,128)(2,1)S(1)}, bf16[512,512]{1,0:T(8,128)(2,1)S(1)}, u32[]{:S(2)}, u32[]{:S(2)}) %collective-permute-start.8) | collective-permute-done | bytes 524320 | tf_op jit(solution)/shard_map/ppermute | solution.py:108
  27.7 0.5 collective-permute-start.16
  29.0 0.6 collective-permute-done.11.refs_11_
  29.6 3.0 %collective-permute-start.17 = (bf16[144,512]{1,0:T(8,128)(2,1)S(1)}, bf16[144,512]{1,0:T(8,128)(2,1)S(1)}, u32[]{:S(2)}, u32[]{:S(2)}) collective-permute-start(bf16[144,512]{1,0:T(8,128)(2,1)S(1)} %pad_maximum_fusion.10), channel_id=1, source_target_pairs={{0,6},{2,4},{4,2},{6,0},{1,7},{3,5},{5,3},{7,1},{8,14},{10,12},{12... | collective-permute-start | bytes 442376 | tf_op jit(solution)/shard_map/ppermute | solution.py:108
  34.1 0.6 collective-permute-start.12
  35.2 0.3 add_add_fusion.1
  36.0 0.3 fusion.30
  36.6 0.3 add_add_fusion
  37.1 1.6 %collective-permute-start.20 = (bf16[192,1024]{1,0:T(8,128)(2,1)S(1)}, bf16[192,1024]{1,0:T(8,128)(2,1)S(1)}, u32[]{:S(2)}, u32[]{:S(2)}) collective-permute-start(bf16[192,1024]{1,0:T(8,128)(2,1)S(1)} %fusion.77), channel_id=1, source_target_pairs={{0,16},{8,24},{16,0},{24,8},{1,17},{9,25},{17,1},{25,9},{2,18},{10... | collective-permute-start | bytes 1179656 | tf_op jit(solution)/shard_map/ppermute | solution.py:108
  39.2 2.5 %collective-permute-done.16 = bf16[144,512]{1,0:T(8,128)(2,1)S(1)} collective-permute-done((bf16[144,512]{1,0:T(8,128)(2,1)S(1)}, bf16[144,512]{1,0:T(8,128)(2,1)S(1)}, u32[]{:S(2)}, u32[]{:S(2)}) %collective-permute-start.16) | collective-permute-done | bytes 147488 | tf_op jit(solution)/shard_map/ppermute | solution.py:108
  41.7 3.3 %collective-permute-done.15 = bf16[144,512]{1,0:T(8,128)(2,1)S(1)} collective-permute-done((bf16[144,512]{1,0:T(8,128)(2,1)S(1)}, bf16[144,512]{1,0:T(8,128)(2,1)S(1)}, u32[]{:S(2)}, u32[]{:S(2)}) %collective-permute-start.15) | collective-permute-done | bytes 147488 | tf_op jit(solution)/shard_map/ppermute | solution.py:108
  45.1 3.6 %collective-permute-done.20 = bf16[192,1024]{1,0:T(8,128)(2,1)S(1)} collective-permute-done((bf16[192,1024]{1,0:T(8,128)(2,1)S(1)}, bf16[192,1024]{1,0:T(8,128)(2,1)S(1)}, u32[]{:S(2)}, u32[]{:S(2)}) %collective-permute-start.20) | collective-permute-done | bytes 393248 | tf_op jit(solution)/shard_map/ppermute | solution.py:108
  48.7 1.6 %collective-permute-start.22 = (bf16[96,1024]{1,0:T(8,128)(2,1)S(1)}, bf16[96,1024]{1,0:T(8,128)(2,1)S(1)}, u32[]{:S(2)}, u32[]{:S(2)}) collective-permute-start(bf16[96,1024]{1,0:T(8,128)(2,1)S(1)} %slice.231), channel_id=1, source_target_pairs={{0,8},{8,0},{16,24},{24,16},{1,9},{9,1},{17,25},{25,17},{2,10},{10... | collective-permute-start | bytes 589832 | tf_op jit(solution)/shard_map/ppermute | solution.py:108
  50.3 0.4 collective-permute-start.21
  50.8 0.3 fusion
  51.2 1.0 %fusion.117 = (bf16[768,1024]{1,0:T(8,128)(2,1)S(1)}, f32[768,1024]{1,0:T(8,128)S(1)}) fusion(bf16[768,512]{1,0:T(8,128)(2,1)S(1)} %pad_maximum_fusion.1, bf16[1024,512]{1,0:T(8,128)(2,1)S(1)} %fusion), kind=kOutput, calls=%fused_computation.192 | convolution fusion | flops 806092800 | bytes 6553600 | tf_op jit(solution)/shard_map/dot_general | solution.py:248
  52.2 1.8 %collective-permute-start.26 = (bf16[96,1024]{1,0:T(8,128)(2,1)S(1)}, bf16[96,1024]{1,0:T(8,128)(2,1)S(1)}, u32[]{:S(2)}, u32[]{:S(2)}) collective-permute-start(bf16[96,1024]{1,0:T(8,128)(2,1)S(1)} %get-tuple-element.125), channel_id=1, source_target_pairs={{0,8},{8,0},{16,24},{24,16},{1,9},{9,1},{17,25},{25,17},{2,10},{10... | collective-permute-start | bytes 589832 | tf_op jit(solution)/shard_map/ppermute | solution.py:108
  54.1 0.5 collective-permute-start.24
  54.6 1.6 %collective-permute-done.22 = bf16[96,1024]{1,0:T(8,128)(2,1)S(1)} collective-permute-done((bf16[96,1024]{1,0:T(8,128)(2,1)S(1)}, bf16[96,1024]{1,0:T(8,128)(2,1)S(1)}, u32[]{:S(2)}, u32[]{:S(2)}) %collective-permute-start.22) | collective-permute-done | bytes 196640 | tf_op jit(solution)/shard_map/ppermute | solution.py:108
  56.2 1.4 %collective-permute-done.21 = bf16[96,1024]{1,0:T(8,128)(2,1)S(1)} collective-permute-done((bf16[96,1024]{1,0:T(8,128)(2,1)S(1)}, bf16[96,1024]{1,0:T(8,128)(2,1)S(1)}, u32[]{:S(2)}, u32[]{:S(2)}) %collective-permute-start.21) | collective-permute-done | bytes 196640 | tf_op jit(solution)/shard_map/ppermute | solution.py:108
  57.8 0.6 fusion.3
  58.5 0.6 fusion.5
  59.1 0.4 collective-permute-done.26
  59.5 1.3 %collective-permute-done.24 = bf16[96,1024]{1,0:T(8,128)(2,1)S(1)} collective-permute-done((bf16[96,1024]{1,0:T(8,128)(2,1)S(1)}, bf16[96,1024]{1,0:T(8,128)(2,1)S(1)}, u32[]{:S(2)}, u32[]{:S(2)}) %collective-permute-start.24) | collective-permute-done | bytes 196640 | tf_op jit(solution)/shard_map/ppermute | solution.py:108
  60.9 0.6 collective-permute-start.25
  61.6 1.6 %collective-permute-start.27 = (bf16[192,1024]{1,0:T(8,128)(2,1)S(1)}, bf16[192,1024]{1,0:T(8,128)(2,1)S(1)}, u32[]{:S(2)}, u32[]{:S(2)}) collective-permute-start(bf16[192,1024]{1,0:T(8,128)(2,1)S(1)} %pad_maximum_fusion.4), channel_id=1, source_target_pairs={{0,16},{8,24},{16,0},{24,8},{1,17},{9,25},{17,1},{25,9},{2,18},{10... | collective-permute-start | bytes 1179656 | tf_op jit(solution)/shard_map/ppermute | solution.py:108
  63.4 1.1 %collective-permute-start.28 = (bf16[128,512]{1,0:T(8,128)(2,1)S(1)}, bf16[128,512]{1,0:T(8,128)(2,1)S(1)}, u32[]{:S(2)}, u32[]{:S(2)}) collective-permute-start(bf16[128,512]{1,0:T(8,128)(2,1)S(1)} %get-tuple-element.136), channel_id=1, source_target_pairs={{0,4},{2,6},{4,0},{6,2},{1,5},{3,7},{5,1},{7,3},{8,12},{10,14},{12... | collective-permute-start | bytes 393224 | tf_op jit(solution)/shard_map/ppermute | solution.py:108
  64.6 0.9 %collective-permute-start.30 = (bf16[128,512]{1,0:T(8,128)(2,1)S(1)}, bf16[128,512]{1,0:T(8,128)(2,1)S(1)}, u32[]{:S(2)}, u32[]{:S(2)}) collective-permute-start(bf16[128,512]{1,0:T(8,128)(2,1)S(1)} %get-tuple-element.137), channel_id=1, source_target_pairs={{0,6},{2,4},{4,2},{6,0},{1,7},{3,5},{5,3},{7,1},{8,14},{10,12},{12... | collective-permute-start | bytes 393224 | tf_op jit(solution)/shard_map/ppermute | solution.py:108
  65.4 1.6 %collective-permute-start.29 = (bf16[128,512]{1,0:T(8,128)(2,1)S(1)}, bf16[128,512]{1,0:T(8,128)(2,1)S(1)}, u32[]{:S(2)}, u32[]{:S(2)}) collective-permute-start(bf16[128,512]{1,0:T(8,128)(2,1)S(1)} %get-tuple-element.138), channel_id=1, source_target_pairs={{0,2},{2,0},{4,6},{6,4},{1,3},{3,1},{5,7},{7,5},{8,10},{10,8},{12,... | collective-permute-start | bytes 393224 | tf_op jit(solution)/shard_map/ppermute | solution.py:108
  67.0 1.0 %convolution_convert_fusion = bf16[768,512]{1,0:T(8,128)(2,1)S(1)} fusion(bf16[768,1024]{1,0:T(8,128)(2,1)S(1)} %constant_dynamic-update-slice_fusion.9, bf16[1024,512]{1,0:T(8,128)(2,1)S(1)} %fusion), kind=kOutput, calls=%fused_computation.3 | convolution fusion | flops 805699584 | bytes 3407872 | tf_op jit(solution)/shard_map/dot_general | solution.py:273
  68.1 0.9 %maximum_bitcast_fusion = bf16[1,768,512]{2,1,0:T(8,128)(2,1)} fusion(bf16[192,512]{1,0:T(8,128)(2,1)S(1)} %get-tuple-element.129, bf16[192,512]{1,0:T(8,128)(2,1)S(1)} %get-tuple-element.130, bf16[192,512]{1,0:T(8,128)(2,1)S(1)} %get-tuple-element.131, bf16[192,512]{1,0:T(8,128)(2,1)S(1)} %get-tuple-element.128), kind=kLoop, calls=%fused_computation.27 | loop fusion | flops 3145728 | bytes 1572864 | tf_op jit(solution)/shard_map/broadcast_in_dim | solution.py:280
  69.0 2.1 %collective-permute-done.25.x_ref = bf16[192,1024]{1,0:T(8,128)(2,1)S(1)} collective-permute-done((bf16[192,1024]{1,0:T(8,128)(2,1)S(1)}, bf16[192,1024]{1,0:T(8,128)(2,1)S(1)}, u32[]{:S(2)}, u32[]{:S(2)}) %collective-permute-start.25) | collective-permute-done | bytes 393248 | tf_op jit(solution)/shard_map/ppermute | solution.py:108
  71.1 0.3 collective-permute-done.27.y_ref
  71.4 2.8 %shard_map.102 = (bf16[192,2048]{1,0:T(8,128)(2,1)}, bf16[192,2048]{1,0:T(8,128)(2,1)}) custom-call(s32[1]{0:T(128)} %bitcast.15.place_ref, f32[192,1024]{1,0:T(8,128)S(1)} %slice.229.share_ref, bf16[192,1024]{1,0:T(8,128)(2,1)S(1)} %collective-permute-done.25.x_ref, bf16[192,1024]{1,0:T(8,128)(2,1)S(1)} %collective-permute-done.27.y_ref, ...), custom_call_target="tpu_custom_call" | custom-call | tf_op jit(solution)/shard_map/pallas_call | solution.py:170
  74.3 0.7 add_convert_fusion
  (108 shorter events, 8.0 us)
Async XLA Ops:
  0.6 14.8 %collective-permute-start.3 = (bf16[128,512]{1,0:T(8,128)(2,1)}, bf16[128,512]{1,0:T(8,128)(2,1)S(1)}, u32[]{:S(2)}, u32[]{:S(2)}) collective-permute-start(bf16[128,512]{1,0:T(8,128)(2,1)} %param.7), channel_id=1, source_target_pairs={{0,4},{2,6},{4,0},{6,2},{1,5},{3,7},{5,1},{7,3},{8,12},{10,14},{12... | collective-permute-start | bytes 393224 | tf_op jit(solution)/shard_map/ppermute | solution.py:108
  4.7 9.0 %collective-permute-start.2 = (bf16[128,512]{1,0:T(8,128)(2,1)}, bf16[128,512]{1,0:T(8,128)(2,1)S(1)}, u32[]{:S(2)}, u32[]{:S(2)}) collective-permute-start(bf16[128,512]{1,0:T(8,128)(2,1)} %param.7), channel_id=1, source_target_pairs={{0,24},{8,16},{16,8},{24,0},{1,25},{9,17},{17,9},{25,1},{2,26},{10... | collective-permute-start | bytes 393224 | tf_op jit(solution)/shard_map/ppermute | solution.py:108
  7.2 6.5 %collective-permute-start.1 = (bf16[128,512]{1,0:T(8,128)(2,1)}, bf16[128,512]{1,0:T(8,128)(2,1)S(1)}, u32[]{:S(2)}, u32[]{:S(2)}) collective-permute-start(bf16[128,512]{1,0:T(8,128)(2,1)} %param.7), channel_id=1, source_target_pairs={{0,16},{8,24},{16,0},{24,8},{1,17},{9,25},{17,1},{25,9},{2,18},{10... | collective-permute-start | bytes 393224 | tf_op jit(solution)/shard_map/ppermute | solution.py:108
  7.7 6.0 %collective-permute-start = (bf16[128,512]{1,0:T(8,128)(2,1)}, bf16[128,512]{1,0:T(8,128)(2,1)S(1)}, u32[]{:S(2)}, u32[]{:S(2)}) collective-permute-start(bf16[128,512]{1,0:T(8,128)(2,1)} %param.7), channel_id=1, source_target_pairs={{0,8},{8,0},{16,24},{24,16},{1,9},{9,1},{17,25},{25,17},{2,10},{10... | collective-permute-start | bytes 393224 | tf_op jit(solution)/shard_map/ppermute | solution.py:108
  8.2 7.2 %collective-permute-start.4 = (bf16[128,512]{1,0:T(8,128)(2,1)}, bf16[128,512]{1,0:T(8,128)(2,1)S(1)}, u32[]{:S(2)}, u32[]{:S(2)}) collective-permute-start(bf16[128,512]{1,0:T(8,128)(2,1)} %param.7), channel_id=1, source_target_pairs={{0,6},{2,4},{4,2},{6,0},{1,7},{3,5},{5,3},{7,1},{8,14},{10,12},{12... | collective-permute-start | bytes 393224 | tf_op jit(solution)/shard_map/ppermute | solution.py:108
  10.3 1.5 %copy-start.2 = (bf16[128,512]{1,0:T(8,128)(2,1)S(1)}, bf16[128,512]{1,0:T(8,128)(2,1)}, u32[]{:S(2)}) copy-start(bf16[128,512]{1,0:T(8,128)(2,1)} %param.8) | copy-start | bytes 393220
  10.3 1.6 %copy-start.3 = (bf16[128,512]{1,0:T(8,128)(2,1)S(1)}, bf16[128,512]{1,0:T(8,128)(2,1)}, u32[]{:S(2)}) copy-start(bf16[128,512]{1,0:T(8,128)(2,1)} %param.7) | copy-start | bytes 393220
  13.7 13.6 %collective-permute-start.8 = (bf16[512,512]{1,0:T(8,128)(2,1)S(1)}, bf16[512,512]{1,0:T(8,128)(2,1)S(1)}, u32[]{:S(2)}, u32[]{:S(2)}) collective-permute-start(bf16[512,512]{1,0:T(8,128)(2,1)S(1)} %constant_dynamic-update-slice_fusion.refs_4_), channel_id=1, source_target_pairs={{0,2},{2,0},{4,6},{6,4},{1,3},{3,1},{5,7},{7,5},{8,10},{10,8},{12,... | collective-permute-start | bytes 1572872 | tf_op jit(solution)/shard_map/ppermute | solution.py:108
  15.4 4.7 %collective-permute-start.10 = (bf16[256,512]{1,0:T(8,128)(2,1)S(1)}, bf16[256,512]{1,0:T(8,128)(2,1)S(1)}, u32[]{:S(2)}, u32[]{:S(2)}) collective-permute-start(bf16[256,512]{1,0:T(8,128)(2,1)S(1)} %pad_maximum_fusion.9.refs_6_), channel_id=1, source_target_pairs={{0,1},{1,0},{2,3},{3,2},{4,5},{5,4},{6,7},{7,6},{8,9},{9,8},{10,11... | collective-permute-start | bytes 786440 | tf_op jit(solution)/shard_map/ppermute | solution.py:108
  15.5 18.2 %collective-permute-start.7 = (bf16[256,512]{1,0:T(8,128)(2,1)S(1)}, bf16[256,512]{1,0:T(8,128)(2,1)S(1)}, u32[]{:S(2)}, u32[]{:S(2)}) collective-permute-start(bf16[256,512]{1,0:T(8,128)(2,1)S(1)} %pad_maximum_fusion.9.refs_6_), channel_id=1, source_target_pairs={{0,24},{8,16},{16,8},{24,0},{1,25},{9,17},{17,9},{25,1},{2,26},{10... | collective-permute-start | bytes 786440 | tf_op jit(solution)/shard_map/ppermute | solution.py:108
  18.6 15.1 %collective-permute-start.6 = (bf16[256,512]{1,0:T(8,128)(2,1)S(1)}, bf16[256,512]{1,0:T(8,128)(2,1)S(1)}, u32[]{:S(2)}, u32[]{:S(2)}) collective-permute-start(bf16[256,512]{1,0:T(8,128)(2,1)S(1)} %pad_maximum_fusion.9.refs_6_), channel_id=1, source_target_pairs={{0,16},{8,24},{16,0},{24,8},{1,17},{9,25},{17,1},{25,9},{2,18},{10... | collective-permute-start | bytes 786440 | tf_op jit(solution)/shard_map/ppermute | solution.py:108
  18.6 2.5 %collective-permute-start.9 = (bf16[512,512]{1,0:T(8,128)(2,1)S(1)}, bf16[512,512]{1,0:T(8,128)(2,1)S(1)}, u32[]{:S(2)}, u32[]{:S(2)}) collective-permute-start(bf16[512,512]{1,0:T(8,128)(2,1)S(1)} %constant_dynamic-update-slice_fusion.refs_4_), channel_id=1, source_target_pairs={{0,1},{1,0},{2,3},{3,2},{4,5},{5,4},{6,7},{7,6},{8,9},{9,8},{10,11... | collective-permute-start | bytes 1572872 | tf_op jit(solution)/shard_map/ppermute | solution.py:108
  20.1 13.6 %collective-permute-start.5 = (bf16[256,512]{1,0:T(8,128)(2,1)S(1)}, bf16[256,512]{1,0:T(8,128)(2,1)S(1)}, u32[]{:S(2)}, u32[]{:S(2)}) collective-permute-start(bf16[256,512]{1,0:T(8,128)(2,1)S(1)} %pad_maximum_fusion.9.refs_6_), channel_id=1, source_target_pairs={{0,8},{8,0},{16,24},{24,16},{1,9},{9,1},{17,25},{25,17},{2,10},{10... | collective-permute-start | bytes 786440 | tf_op jit(solution)/shard_map/ppermute | solution.py:108
  27.6 2.0 %collective-permute-start.11 = (bf16[512,512]{1,0:T(8,128)(2,1)S(1)}, bf16[512,512]{1,0:T(8,128)(2,1)S(1)}, u32[]{:S(2)}, u32[]{:S(2)}) collective-permute-start(bf16[512,512]{1,0:T(8,128)(2,1)S(1)} %collective-permute-done.8.refs_5_), channel_id=1, source_target_pairs={{0,1},{1,0},{2,3},{3,2},{4,5},{5,4},{6,7},{7,6},{8,9},{9,8},{10,11... | collective-permute-start | bytes 1572872 | tf_op jit(solution)/shard_map/ppermute | solution.py:108
  27.7 13.9 %collective-permute-start.16 = (bf16[144,512]{1,0:T(8,128)(2,1)S(1)}, bf16[144,512]{1,0:T(8,128)(2,1)S(1)}, u32[]{:S(2)}, u32[]{:S(2)}) collective-permute-start(bf16[144,512]{1,0:T(8,128)(2,1)S(1)} %pad_maximum_fusion.10), channel_id=1, source_target_pairs={{0,4},{2,6},{4,0},{6,2},{1,5},{3,7},{5,1},{7,3},{8,12},{10,14},{12... | collective-permute-start | bytes 442376 | tf_op jit(solution)/shard_map/ppermute | solution.py:108
  29.6 12.0 %collective-permute-start.17 = (bf16[144,512]{1,0:T(8,128)(2,1)S(1)}, bf16[144,512]{1,0:T(8,128)(2,1)S(1)}, u32[]{:S(2)}, u32[]{:S(2)}) collective-permute-start(bf16[144,512]{1,0:T(8,128)(2,1)S(1)} %pad_maximum_fusion.10), channel_id=1, source_target_pairs={{0,6},{2,4},{4,2},{6,0},{1,7},{3,5},{5,3},{7,1},{8,14},{10,12},{12... | collective-permute-start | bytes 442376 | tf_op jit(solution)/shard_map/ppermute | solution.py:108
  33.7 2.3 %collective-permute-start.13 = (bf16[256,512]{1,0:T(8,128)(2,1)S(1)}, bf16[256,512]{1,0:T(8,128)(2,1)S(1)}, u32[]{:S(2)}, u32[]{:S(2)}) collective-permute-start(bf16[256,512]{1,0:T(8,128)(2,1)S(1)} %collective-permute-done.6.refs_8_), channel_id=1, source_target_pairs={{0,1},{1,0},{2,3},{3,2},{4,5},{5,4},{6,7},{7,6},{8,9},{9,8},{10,11... | collective-permute-start | bytes 786440 | tf_op jit(solution)/shard_map/ppermute | solution.py:108
  34.1 2.2 %collective-permute-start.12 = (bf16[256,512]{1,0:T(8,128)(2,1)S(1)}, bf16[256,512]{1,0:T(8,128)(2,1)S(1)}, u32[]{:S(2)}, u32[]{:S(2)}) collective-permute-start(bf16[256,512]{1,0:T(8,128)(2,1)S(1)} %collective-permute-done.5.refs_7_), channel_id=1, source_target_pairs={{0,1},{1,0},{2,3},{3,2},{4,5},{5,4},{6,7},{7,6},{8,9},{9,8},{10,11... | collective-permute-start | bytes 786440 | tf_op jit(solution)/shard_map/ppermute | solution.py:108
  35.0 1.7 %collective-permute-start.14 = (bf16[256,512]{1,0:T(8,128)(2,1)S(1)}, bf16[256,512]{1,0:T(8,128)(2,1)S(1)}, u32[]{:S(2)}, u32[]{:S(2)}) collective-permute-start(bf16[256,512]{1,0:T(8,128)(2,1)S(1)} %collective-permute-done.7.refs_9_), channel_id=1, source_target_pairs={{0,1},{1,0},{2,3},{3,2},{4,5},{5,4},{6,7},{7,6},{8,9},{9,8},{10,11... | collective-permute-start | bytes 786440 | tf_op jit(solution)/shard_map/ppermute | solution.py:108
  36.6 2.1 %copy-start.1 = (bf16[1,768,512]{2,1,0:T(8,128)(2,1)S(1)}, bf16[1,768,512]{2,1,0:T(8,128)(2,1)}, u32[]{:S(2)}) copy-start(bf16[1,768,512]{2,1,0:T(8,128)(2,1)} %param.13) | copy-start | bytes 2359300
  37.1 11.6 %collective-permute-start.20 = (bf16[192,1024]{1,0:T(8,128)(2,1)S(1)}, bf16[192,1024]{1,0:T(8,128)(2,1)S(1)}, u32[]{:S(2)}, u32[]{:S(2)}) collective-permute-start(bf16[192,1024]{1,0:T(8,128)(2,1)S(1)} %fusion.77), channel_id=1, source_target_pairs={{0,16},{8,24},{16,0},{24,8},{1,17},{9,25},{17,1},{25,9},{2,18},{10... | collective-permute-start | bytes 1179656 | tf_op jit(solution)/shard_map/ppermute | solution.py:108
  38.7 11.6 %collective-permute-start.19 = (bf16[192,1024]{1,0:T(8,128)(2,1)S(1)}, bf16[192,1024]{1,0:T(8,128)(2,1)S(1)}, u32[]{:S(2)}, u32[]{:S(2)}) collective-permute-start(bf16[192,1024]{1,0:T(8,128)(2,1)S(1)} %fusion.77), channel_id=1, source_target_pairs={{0,8},{8,0},{16,24},{24,16},{1,9},{9,1},{17,25},{25,17},{2,10},{10... | collective-permute-start | bytes 1179656 | tf_op jit(solution)/shard_map/ppermute | solution.py:108
  38.9 6.0 %collective-permute-start.15 = (bf16[144,512]{1,0:T(8,128)(2,1)S(1)}, bf16[144,512]{1,0:T(8,128)(2,1)S(1)}, u32[]{:S(2)}, u32[]{:S(2)}) collective-permute-start(bf16[144,512]{1,0:T(8,128)(2,1)S(1)} %pad_maximum_fusion.10), channel_id=1, source_target_pairs={{0,2},{2,0},{4,6},{6,4},{1,3},{3,1},{5,7},{7,5},{8,10},{10,8},{12,... | collective-permute-start | bytes 442376 | tf_op jit(solution)/shard_map/ppermute | solution.py:108
  45.0 5.7 %collective-permute-start.18 = (bf16[4,144,512]{2,1,0:T(8,128)(2,1)S(1)}, bf16[4,144,512]{2,1,0:T(8,128)(2,1)S(1)}, u32[]{:S(2)}, u32[]{:S(2)}) collective-permute-start(bf16[4,144,512]{2,1,0:T(8,128)(2,1)S(1)} %pad_maximum_fusion.2), channel_id=1, source_target_pairs={{0,1},{1,0},{2,3},{3,2},{4,5},{5,4},{6,7},{7,6},{8,9},{9,8},{10,11... | collective-permute-start | bytes 1769480 | tf_op jit(solution)/shard_map/ppermute | solution.py:108
  48.7 7.5 %collective-permute-start.22 = (bf16[96,1024]{1,0:T(8,128)(2,1)S(1)}, bf16[96,1024]{1,0:T(8,128)(2,1)S(1)}, u32[]{:S(2)}, u32[]{:S(2)}) collective-permute-start(bf16[96,1024]{1,0:T(8,128)(2,1)S(1)} %slice.231), channel_id=1, source_target_pairs={{0,8},{8,0},{16,24},{24,16},{1,9},{9,1},{17,25},{25,17},{2,10},{10... | collective-permute-start | bytes 589832 | tf_op jit(solution)/shard_map/ppermute | solution.py:108
  50.3 7.3 %collective-permute-start.21 = (bf16[96,1024]{1,0:T(8,128)(2,1)S(1)}, bf16[96,1024]{1,0:T(8,128)(2,1)S(1)}, u32[]{:S(2)}, u32[]{:S(2)}) collective-permute-start(bf16[96,1024]{1,0:T(8,128)(2,1)S(1)} %slice.230), channel_id=1, source_target_pairs={{0,16},{8,24},{16,0},{24,8},{1,17},{9,25},{17,1},{25,9},{2,18},{10... | collective-permute-start | bytes 589832 | tf_op jit(solution)/shard_map/ppermute | solution.py:108
  52.2 7.3 %collective-permute-start.26 = (bf16[96,1024]{1,0:T(8,128)(2,1)S(1)}, bf16[96,1024]{1,0:T(8,128)(2,1)S(1)}, u32[]{:S(2)}, u32[]{:S(2)}) collective-permute-start(bf16[96,1024]{1,0:T(8,128)(2,1)S(1)} %get-tuple-element.125), channel_id=1, source_target_pairs={{0,8},{8,0},{16,24},{24,16},{1,9},{9,1},{17,25},{25,17},{2,10},{10... | collective-permute-start | bytes 589832 | tf_op jit(solution)/shard_map/ppermute | solution.py:108
  54.1 6.8 %collective-permute-start.24 = (bf16[96,1024]{1,0:T(8,128)(2,1)S(1)}, bf16[96,1024]{1,0:T(8,128)(2,1)S(1)}, u32[]{:S(2)}, u32[]{:S(2)}) collective-permute-start(bf16[96,1024]{1,0:T(8,128)(2,1)S(1)} %get-tuple-element.127), channel_id=1, source_target_pairs={{0,16},{8,24},{16,0},{24,8},{1,17},{9,25},{17,1},{25,9},{2,18},{10... | collective-permute-start | bytes 589832 | tf_op jit(solution)/shard_map/ppermute | solution.py:108
  58.4 4.8 %collective-permute-start.23 = (bf16[512,512]{1,0:T(8,128)(2,1)S(1)}, bf16[512,512]{1,0:T(8,128)(2,1)S(1)}, u32[]{:S(2)}, u32[]{:S(2)}) collective-permute-start(bf16[512,512]{1,0:T(8,128)(2,1)S(1)} %fusion.3), channel_id=1, source_target_pairs={{0,1},{1,0},{2,3},{3,2},{4,5},{5,4},{6,7},{7,6},{8,9},{9,8},{10,11... | collective-permute-start | bytes 1572872 | tf_op jit(solution)/shard_map/ppermute | solution.py:108
  60.9 10.2 %collective-permute-start.25 = (bf16[192,1024]{1,0:T(8,128)(2,1)S(1)}, bf16[192,1024]{1,0:T(8,128)(2,1)S(1)}, u32[]{:S(2)}, u32[]{:S(2)}) collective-permute-start(bf16[192,1024]{1,0:T(8,128)(2,1)S(1)} %pad_maximum_fusion.3), channel_id=1, source_target_pairs={{0,8},{8,0},{16,24},{24,16},{1,9},{9,1},{17,25},{25,17},{2,10},{10... | collective-permute-start | bytes 1179656 | tf_op jit(solution)/shard_map/ppermute | solution.py:108
  61.6 9.9 %collective-permute-start.27 = (bf16[192,1024]{1,0:T(8,128)(2,1)S(1)}, bf16[192,1024]{1,0:T(8,128)(2,1)S(1)}, u32[]{:S(2)}, u32[]{:S(2)}) collective-permute-start(bf16[192,1024]{1,0:T(8,128)(2,1)S(1)} %pad_maximum_fusion.4), channel_id=1, source_target_pairs={{0,16},{8,24},{16,0},{24,8},{1,17},{9,25},{17,1},{25,9},{2,18},{10... | collective-permute-start | bytes 1179656 | tf_op jit(solution)/shard_map/ppermute | solution.py:108
  63.3 4.7 %copy-start = (f32[512,512]{1,0:T(8,128)}, f32[512,512]{1,0:T(8,128)S(1)}, u32[]{:S(2)}) copy-start(f32[512,512]{1,0:T(8,128)S(1)} %convert_add_fusion) | copy-start | bytes 3145732
  63.4 10.8 %collective-permute-start.28 = (bf16[128,512]{1,0:T(8,128)(2,1)S(1)}, bf16[128,512]{1,0:T(8,128)(2,1)S(1)}, u32[]{:S(2)}, u32[]{:S(2)}) collective-permute-start(bf16[128,512]{1,0:T(8,128)(2,1)S(1)} %get-tuple-element.136), channel_id=1, source_target_pairs={{0,4},{2,6},{4,0},{6,2},{1,5},{3,7},{5,1},{7,3},{8,12},{10,14},{12... | collective-permute-start | bytes 393224 | tf_op jit(solution)/shard_map/ppermute | solution.py:108
  64.6 9.7 %collective-permute-start.30 = (bf16[128,512]{1,0:T(8,128)(2,1)S(1)}, bf16[128,512]{1,0:T(8,128)(2,1)S(1)}, u32[]{:S(2)}, u32[]{:S(2)}) collective-permute-start(bf16[128,512]{1,0:T(8,128)(2,1)S(1)} %get-tuple-element.137), channel_id=1, source_target_pairs={{0,6},{2,4},{4,2},{6,0},{1,7},{3,5},{5,3},{7,1},{8,14},{10,12},{12... | collective-permute-start | bytes 393224 | tf_op jit(solution)/shard_map/ppermute | solution.py:108
  65.4 8.9 %collective-permute-start.29 = (bf16[128,512]{1,0:T(8,128)(2,1)S(1)}, bf16[128,512]{1,0:T(8,128)(2,1)S(1)}, u32[]{:S(2)}, u32[]{:S(2)}) collective-permute-start(bf16[128,512]{1,0:T(8,128)(2,1)S(1)} %get-tuple-element.138), channel_id=1, source_target_pairs={{0,2},{2,0},{4,6},{6,4},{1,3},{3,1},{5,7},{7,5},{8,10},{10,8},{12,... | collective-permute-start | bytes 393224 | tf_op jit(solution)/shard_map/ppermute | solution.py:108
  71.4 2.9 %slice-start = ((f32[512,512]{1,0:T(8,128)}), f32[128,512]{1,0:T(8,128)S(1)}, s32[]{:S(2)}) async-start(f32[512,512]{1,0:T(8,128)} %copy-done), calls=%async_computation | async-start | bytes 524288 | tf_op jit(solution)/shard_map/slice | solution.py:271
